TPU v7x, 32 devices: a whole 2x2x4 slice. The times are simulated.
32 devices in a mesh: ckpt: 2 (over x), dp: 16 (over z, y, core).
Axes of the slice: x: 2, y: 2, z: 4, core: 2. Of those that a mesh axis runs over, the one named last changes fastest.
Arguments:
- img_feats: bfloat16 [4096, 1664], P(('ckpt', 'dp')), parts along dimension 0, may hold values from -6 to 6
- txt_feats: bfloat16 [4096, 1280], P(('ckpt', 'dp')), parts along dimension 0, may hold values from -6 to 6
- w_img: bfloat16 [3328, 1280], P('ckpt'), parts along dimension 0, may hold values from -1 to 1
- w_txt: bfloat16 [2560, 1280], P('ckpt'), parts along dimension 0, may hold values from -1 to 1
- a_img: bfloat16 [1664, 32], replicated, may hold values from -6 to 6
- b_img: bfloat16 [1280, 128], replicated, may hold values from -6 to 6
- a_txt: bfloat16 [1280, 32], replicated, may hold values from -6 to 6
- b_txt: bfloat16 [1280, 128], replicated, may hold values from -6 to 6
Outputs:
- img_sketch: bfloat16 [4096, 4096], P(('ckpt', 'dp')), parts along dimension 0
- txt_sketch: bfloat16 [4096, 4096], P(('ckpt', 'dp')), parts along dimension 0
There are 2 independent parts, one for each index of `ckpt`. A program takes and returns all parts, laid end to end along the dimension named above; an argument that names none is the same for every part. Nothing has to cross between parts.
All inputs are finite; a program needn't handle non-finite values.
Results may differ from a plain program's by a relative error of at most 0.012.
The roundings to bfloat16 on the way count: a program that leaves them out, or rounds other values in their place, can miss the bound.
Values may be sent and summed in bfloat16 or wider, within the bound.
No kernel may reach another device: no remote copies, remote signals or barrier semaphores. Data moves between devices by JAX's collectives and lax.ppermute only.
A program may use at most 128 MiB of HBM per device.

v0:
```python
import jax
import jax.numpy as jnp
from jax import lax
from jax.sharding import PartitionSpec as P

LOGIT_SCALE = 100.0
EPSILON = 1e-06


def embed(feats, weight):
    raw = jnp.dot(feats, weight, preferred_element_type=jnp.float32)
    inverse = lax.rsqrt(jnp.sum(raw * raw, axis=1) + EPSILON)
    return ((raw * inverse[:, None]).astype(jnp.bfloat16), inverse)


def against(left, right):
    return lax.dot_general(
        left, right, (((1,), (1,)), ((), ())), preferred_element_type=jnp.float32
    )


def body(img_feats, txt_feats, w_img, w_txt, a_img, b_img, a_txt, b_txt):
    rows_here = img_feats.shape[0]
    img_emb, img_inv = embed(img_feats, w_img)
    txt_emb, txt_inv = embed(txt_feats, w_txt)
    img_low = jnp.dot(img_emb, b_img, preferred_element_type=jnp.float32)
    own_low = jnp.dot(txt_emb, b_img, preferred_element_type=jnp.float32).astype(jnp.bfloat16)
    img_side = jnp.dot(img_emb, b_txt, preferred_element_type=jnp.float32).astype(jnp.bfloat16)
    txt_side = jnp.dot(txt_emb, b_txt, preferred_element_type=jnp.float32)
    img_keys = jnp.dot(img_feats, a_img, preferred_element_type=jnp.float32)
    txt_keys = jnp.dot(txt_feats, a_txt, preferred_element_type=jnp.float32)
    diagonal = jnp.sum(img_emb.astype(jnp.float32) * txt_emb.astype(jnp.float32), axis=1)
    all_texts = lax.all_gather(txt_emb, "dp", axis=0, tiled=True)
    raw = against(img_emb, all_texts)
    txt_low = jnp.dot(all_texts, b_img, preferred_element_type=jnp.float32).astype(jnp.bfloat16)
    scores = LOGIT_SCALE * raw
    row_top = jnp.max(scores, axis=1)
    row_lse = row_top + jnp.log(jnp.sum(jnp.exp(scores - row_top[:, None]), axis=1))
    col_top = jnp.max(scores, axis=0)
    glob_top = lax.pmax(col_top.astype(jnp.bfloat16), "dp").astype(col_top.dtype)
    glob_total = lax.psum(jnp.sum(jnp.exp(scores - glob_top[None, :]), axis=0), "dp")
    col_lse = glob_top + jnp.log(glob_total)
    weights = jnp.exp(scores - row_lse[:, None]) + jnp.exp(scores - col_lse[None, :])
    weights_bf = weights.astype(jnp.bfloat16)
    weighted = weights * raw
    carried = jnp.dot(weights_bf, txt_low, preferred_element_type=jnp.float32)
    inner = jnp.sum(weighted, axis=1) - 2.0 * diagonal
    img_grad = (carried - 2.0 * own_low.astype(jnp.float32) - inner[:, None] * img_low) * img_inv[
        :, None
    ]
    img_sketch = (
        (img_keys[:, :, None] * img_grad[:, None, :]).reshape(rows_here, -1).astype(jnp.bfloat16)
    )
    partial_value = lax.dot_general(
        weights_bf, img_side, (((0,), (0,)), ((), ())), preferred_element_type=jnp.float32
    )
    colsum = jnp.sum(weighted, axis=0)
    mine, mine_sum = (
        lax.psum_scatter(partial_value, "dp", scatter_dimension=0, tiled=True),
        lax.psum_scatter(colsum, "dp", scatter_dimension=0, tiled=True),
    )
    inner_txt = mine_sum - 2.0 * diagonal
    txt_grad = (
        mine - 2.0 * img_side.astype(jnp.float32) - inner_txt[:, None] * txt_side
    ) * txt_inv[:, None]
    txt_sketch = (
        (txt_keys[:, :, None] * txt_grad[:, None, :]).reshape(rows_here, -1).astype(jnp.bfloat16)
    )
    return (img_sketch, txt_sketch)


def solution(mesh):
    placed = (
        P(("ckpt", "dp"), None),
        P(("ckpt", "dp"), None),
        P("ckpt", None),
        P("ckpt", None),
        P(),
        P(),
        P(),
        P(),
    )
    return jax.shard_map(
        body,
        mesh=mesh,
        in_specs=placed,
        out_specs=(P(("ckpt", "dp"), None), P(("ckpt", "dp"), None)),
        check_vma=False,
    )
```

profile of v0, /device:TPU:0, one launch (start us, length us, event | category | flops | bytes accessed | tf_op | source)
XLA Modules:
  0.0 207.9 jit_solution(16558000445811726961)
XLA Ops:
  7.2 0.0 copy-start
  7.2 0.0 all-gather.2.cloned.1.call-start
  7.2 0.0 copy-start.2
  7.2 3.3 %multiply_reduce_fusion.4 = (f32[128]{0:T(128)S(1)}, f32[128,1280]{1,0:T(8,128)S(1)}) fusion(bf16[128,1664]{1,0:T(8,128)(2,1)} %param.8, bf16[1664,1280]{1,0:T(8,128)(2,1)} %param.10), kind=kOutput, calls=%fused_computation.28 | convolution fusion | flops 545587072 | bytes 5341696 | tf_op jit(solution)/shard_map/dot_general | solution.py:11
  10.6 0.0 copy-done
  10.6 0.0 copy-done.2
  10.6 0.0 copy-start.5
  10.6 0.0 copy-start.3
  10.6 0.7 multiply_reduce_fusion.3
  11.4 1.1 multiply_reduce_fusion.2
  12.4 0.0 all-gather.2.cloned.1.call-update
  12.4 0.0 reduce-scatter.2.cloned.1.call-start
  12.5 0.0 copy-done.5
  12.5 0.6 dynamic-slice
  13.7 0.0 copy-done.3
  13.8 1.2 fusion.15
  15.0 1.3 convolution_convert_fusion.1
  16.3 1.9 fusion.7
  18.2 53.0 %all-gather.2.cloned.1.call-done = bf16[2048,1280]{1,0:T(8,128)(2,1)} async-done(((bf16[128,1280]{1,0:T(8,128)(2,1)}), bf16[2048,1280]{1,0:T(8,128)(2,1)}) %all-gather.2.cloned.1.call-update) | async-done | bytes 5242896 | tf_op jit(solution)/shard_map/all_gather | solution.py:33
  71.3 4.5 %multiply_reduce_fusion.1 = (f32[128]{0:T(128)S(1)}, f32[128,2048]{1,0:T(8,128)S(1)}) fusion(bf16[128,1280]{1,0:T(8,128)(2,1)} %get-tuple-element.7, bf16[2048,1280]{1,0:T(8,128)(2,1)} %all-gather.2.cloned.1.call-done), kind=kOutput, calls=%fused_computation.21 | convolution fusion | flops 671612800 | bytes 6619648 | tf_op jit(solution)/shard_map/dot_general | solution.py:17
  75.8 0.0 copy-start.1
  75.8 0.0 copy-start.4
  75.8 1.0 copy-done.1
  76.8 0.3 exponential_reduce_fusion.1
  77.1 31.3 %pmax.7 = bf16[2048]{0:T(1024)(128)(2,1)S(1)} all-reduce(bf16[2048]{0:T(1024)(128)(2,1)S(1)} %get-tuple-element.5), channel_id=1, replica_groups=mesh['ckpt'=2,'dp'=16] {'dp'}, use_global_device_ids=true, to_apply=%region_5.0 | all-reduce | flops 2048 | bytes 8192 | tf_op jit(solution)/shard_map/pmax | solution.py:40
  108.4 1.4 exponential_reduce_fusion
  109.8 30.0 %psum.7 = f32[2048]{0:T(1024)S(1)} all-reduce(f32[2048]{0:T(1024)S(1)} %exponential_reduce_fusion), channel_id=1, replica_groups=mesh['ckpt'=2,'dp'=16] {'dp'}, use_global_device_ids=true, to_apply=%region_7.0 | all-reduce | flops 2048 | bytes 16384 | tf_op jit(solution)/shard_map/psum | solution.py:41
  139.9 2.8 %fusion.12 = f32[2048,128]{1,0:T(8,128)} fusion(bf16[128,128]{1,0:T(8,128)(2,1)S(1)} %convolution_convert_fusion.1, f32[128,2048]{1,0:T(8,128)} %copy-done.1, f32[2048]{0:T(1024)S(1)} %log_add_fusion, f32[128]{0:T(128)S(1)} %log_add_fusion.1), kind=kOutput, calls=%fused_computation.37 | convolution fusion | flops 68419584 | bytes 2138624 | tf_op jit(solution)/shard_map/dot_general | solution.py:54
  142.7 0.0 reduce-scatter.2.cloned.1.call-update
  142.7 0.0 copy-done.4
  142.7 1.2 fusion.16
  143.9 1.7 fusion.10
  145.6 30.1 %all-reduce = f32[2048]{0:T(1024)S(1)} all-reduce(f32[2048]{0:T(1024)S(1)} %get-tuple-element.2), channel_id=3, replica_groups=mesh['ckpt'=2,'dp'=16] {'dp'}, use_global_device_ids=true, to_apply=%region_12.0.clone | all-reduce | flops 2048 | bytes 16384
  175.7 0.1 dynamic-slice_subtract_fusion
  175.8 4.7 %fusion.5 = f32[128,128]{1,0:T(8,128)S(1)} fusion(f32[128,128]{1,0:T(8,128)} %fusion.7, bf16[2048,1280]{1,0:T(8,128)(2,1)} %all-gather.2.cloned.1.call-done, bf16[1280,128]{1,0:T(8,128)(2,1)} %param.13, f32[128,2048]{1,0:T(8,128)} %copy-done.1, f32[2048]{0:T(1024)S(1)} %log_add_fusion, f32[128]{0:T(128)S(1)} %log_add_fusion.1), kind=kOutput, calls=%fused_computation.10 | convolution fusion | flops 739786752 | bytes 6758912 | tf_op jit(solution)/shard_map/dot_general | solution.py:46
  180.5 1.3 fusion.4
  181.8 0.8 multiply_convert_fusion.1
  182.6 1.4 copy.21
  184.0 13.6 %reduce-scatter.2.cloned.1.call-done = f32[128,128]{1,0:T(8,128)} async-done(((f32[2048,128]{1,0:T(8,128)}), f32[128,128]{1,0:T(8,128)}) %reduce-scatter.2.cloned.1.call-update) | async-done | bytes 65552 | tf_op jit(solution)/shard_map/reduce_scatter | solution.py:59
  197.6 1.3 fusion.2
  198.9 0.8 multiply_convert_fusion
  199.7 1.4 copy.20
  (4 shorter events, 0.0 us)
Async XLA Ops:
  7.2 3.4 %copy-start = (bf16[1280,1280]{1,0:T(8,128)(2,1)S(1)}, bf16[1280,1280]{1,0:T(8,128)(2,1)}, u32[]{:S(2)}) copy-start(bf16[1280,1280]{1,0:T(8,128)(2,1)} %param.11) | copy-start | bytes 9830404
  7.2 64.1 %all-gather.2.cloned.1.call-start = ((), (), s32[]{:S(2)}) async-start(), calls=%async_computation.1 | async-start | bytes 5570560 | tf_op jit(solution)/shard_map/all_gather | solution.py:33
  7.2 3.4 %copy-start.2 = (bf16[128,1280]{1,0:T(8,128)(2,1)S(1)}, bf16[128,1280]{1,0:T(8,128)(2,1)}, u32[]{:S(2)}) copy-start(bf16[128,1280]{1,0:T(8,128)(2,1)} %param.9) | copy-start | bytes 983044
  10.6 1.9 copy-start.5
  10.6 3.1 %copy-start.3 = (bf16[1664,32]{0,1:T(8,128)(2,1)S(1)}, bf16[1664,32]{0,1:T(8,128)(2,1)}, u32[]{:S(2)}) copy-start(bf16[1664,32]{0,1:T(8,128)(2,1)} %param.12) | copy-start | bytes 319492
  12.4 185.2 %reduce-scatter.2.cloned.1.call-start = ((), (), s32[]{:S(2)}) async-start(), calls=%async_computation.2 | async-start | bytes 1114112 | tf_op jit(solution)/shard_map/reduce_scatter | solution.py:59
  75.8 1.0 copy-start.1
  75.8 66.9 %copy-start.4 = (bf16[1280,32]{0,1:T(8,128)(2,1)S(1)}, bf16[1280,32]{0,1:T(8,128)(2,1)}, u32[]{:S(2)}) copy-start(bf16[1280,32]{0,1:T(8,128)(2,1)} %param.14) | copy-start | bytes 245764
Sparse Core Ops, SparseCore 0:
  12.6 58.6 all-gather.1
  142.8 54.7 reduce-scatter.1
where the time goes:
time: 208 us
  blocking collectives  91.4 us (44%)
  waiting for transfers between devices  66.7 us (32%)
  matrix products  24.3 us (12%)
  between operations  14.9 us (7%)
  other arithmetic  6.16 us (3%)
  local copies, waits for them, and re-layouts  4.4 us (2%)
    all_gather x1, waiting for transfers between devices, body(): all_texts = lax.all_gather(txt_emb, 'dp', axis=0, tiled=True)  53 us
    pmax x1, blocking collectives, body(): lax.pmax(col_top.astype(jnp.bfloat16), 'dp').astype(col_top.dtype)  31.3 us
    unnamed x1, blocking collectives  30.1 us
    psum x1, blocking collectives, body(): lax.psum(jnp.sum(jnp.exp(scores - glob_top[None, :]), axis=0), 'dp')  30 us
    reduce_scatter x1, waiting for transfers between devices, body(): lax.psum_scatter(partial_value, 'dp', scatter_dimension=0, tiled=True)  13.6 us
    dot_general x1, matrix products, body(): carried = jnp.dot(weights_bf, txt_low, preferred_element_type=jnp.float32)  4.7 us
    dot_general x1, matrix products, against(): lax.dot_general(left, right, (((1,), (1,)), ((), ())), preferred_element_...  4.49 us
    unnamed x15, local copies, waits for them, and re-layouts  4.4 us
  transfers between devices with their start and end apart: 2, of which 2 were waited for; matrix products, arithmetic and copies ran while one was open for 8% of the time, Pallas kernels for 0%

commit v1 on v0

v1 whole, which is shorter than its diff:
```python
import jax
import jax.numpy as jnp
from jax import lax
from jax.sharding import PartitionSpec as P

LOGIT_SCALE = 100.0
EPSILON = 1e-06


def embed(feats, weight):
    raw = jnp.dot(feats, weight, preferred_element_type=jnp.float32)
    inverse = lax.rsqrt(jnp.sum(raw * raw, axis=1) + EPSILON)
    return ((raw * inverse[:, None]).astype(jnp.bfloat16), inverse)


def against(left, right):
    return lax.dot_general(
        left, right, (((1,), (1,)), ((), ())), preferred_element_type=jnp.float32
    )


def split_bits(n):
    bits = [1 << b for b in range(n.bit_length() - 1)]
    assert 1 << len(bits) == n
    half = len(bits) // 2
    return bits[: half : -1] + bits[:1], bits[half : 0 : -1]


def swap(x, bit, n):
    return lax.ppermute(x, "dp", [(i, i ^ bit) for i in range(n)])


def gather(block, bits, n):
    blocks = [block]
    for bit in bits:
        blocks = blocks + [swap(b, bit, n) for b in blocks]
    return jnp.concatenate(blocks, axis=0)


def merge_lse(lse, bits, n):
    for j, bit in enumerate(bits):
        other = swap(lse, bit, n)
        cut = other.reshape(-1, 2, 1 << j, lse.shape[1])
        lse = jnp.logaddexp(lse, cut[:, ::-1].reshape(lse.shape))
    return lse


def halve(part, bits, n):
    for bit in reversed(bits):
        half = part.shape[0] // 2
        part = part[:half] + swap(part[half:], bit, n)
    return part


def lse_of(scores, axis):
    top = jnp.max(scores, axis=axis)
    return top + jnp.log(jnp.sum(jnp.exp(scores - jnp.expand_dims(top, axis)), axis=axis))


def body(n, img_feats, txt_feats, w_img, w_txt, a_img, b_img, a_txt, b_txt):
    rows_here = img_feats.shape[0]
    img_bits, txt_bits = split_bits(n)
    txt_emb, txt_inv = embed(txt_feats, w_txt)
    img_emb, img_inv = embed(img_feats, w_img)
    texts = gather(txt_emb, txt_bits, n)
    images = gather(img_emb, img_bits, n)
    diagonal = jnp.sum(img_emb.astype(jnp.float32) * txt_emb.astype(jnp.float32), axis=1)
    img_keys = jnp.dot(img_feats, a_img, preferred_element_type=jnp.float32)
    txt_keys = jnp.dot(txt_feats, a_txt, preferred_element_type=jnp.float32)
    img_low = jnp.dot(images, b_img, preferred_element_type=jnp.float32)
    txt_low = jnp.dot(texts, b_img, preferred_element_type=jnp.float32).astype(jnp.bfloat16)
    img_side = jnp.dot(images, b_txt, preferred_element_type=jnp.float32).astype(jnp.bfloat16)
    txt_side = jnp.dot(texts, b_txt, preferred_element_type=jnp.float32)
    raw = against(images, texts)
    scores = LOGIT_SCALE * raw
    row_lse = merge_lse(lse_of(scores, 1).reshape(-1, rows_here), img_bits, n).reshape(-1)
    col_lse = merge_lse(lse_of(scores, 0).reshape(-1, rows_here), txt_bits, n).reshape(-1)
    weights = jnp.exp(scores - row_lse[:, None]) + jnp.exp(scores - col_lse[None, :])
    weights_bf = weights.astype(jnp.bfloat16)
    weighted = weights * raw
    img_part = (
        jnp.dot(weights_bf, txt_low, preferred_element_type=jnp.float32)
        - jnp.sum(weighted, axis=1)[:, None] * img_low
    )
    txt_part = (
        lax.dot_general(
            weights_bf, img_side, (((0,), (0,)), ((), ())), preferred_element_type=jnp.float32
        )
        - jnp.sum(weighted, axis=0)[:, None] * txt_side
    )
    img_sum = halve(img_part, img_bits, n)
    txt_sum = halve(txt_part, txt_bits, n)
    twice = 2.0 * diagonal[:, None]
    own = slice(0, rows_here)
    img_grad = (img_sum - 2.0 * txt_low[own].astype(jnp.float32) + twice * img_low[own]) * img_inv[:, None]
    txt_grad = (txt_sum - 2.0 * img_side[own].astype(jnp.float32) + twice * txt_side[own]) * txt_inv[:, None]
    return tuple(
        (keys[:, :, None] * grad[:, None, :]).reshape(rows_here, -1).astype(jnp.bfloat16)
        for keys, grad in ((img_keys, img_grad), (txt_keys, txt_grad))
    )


def solution(mesh):
    n = mesh.shape["dp"]
    rows = P(("ckpt", "dp"), None)
    part = P("ckpt", None)
    return jax.shard_map(
        lambda *args: body(n, *args),
        mesh=mesh,
        in_specs=(rows, rows, part, part, P(), P(), P(), P()),
        out_specs=(rows, rows),
        check_vma=False,
    )
```

time: 208 us -> 73.5 us (0.35)
  blocking collectives: 91.4 us -> 0 us
  waiting for transfers between devices: 66.7 us -> 25.2 us
  starting transfers between devices: 0.08 us -> 14.3 us
  between operations: 14.9 us -> 0.98 us
  matrix products: 24.3 us -> 13.8 us
  local copies, waits for them, and re-layouts: 4.4 us -> 8.58 us
  other arithmetic: 6.16 us -> 10.2 us
    all_gather x1 -> x0, waiting for transfers between devices: 53 us -> none  [body(): all_texts = lax.all_gather(txt_emb, 'dp', axis=0, tiled=True)]
    pmax x1 -> x0, blocking collectives: 31.3 us -> none  [body(): lax.pmax(col_top.astype(jnp.bfloat16), 'dp').astype(col_top.dtype)]
    unnamed x1 -> x0, blocking collectives: 30.1 us -> none
    psum x1 -> x0, blocking collectives: 30 us -> none  [body(): lax.psum(jnp.sum(jnp.exp(scores - glob_top[None, :]), axis=0), 'dp')]
    ppermute x0 -> x14, waiting for transfers between devices: none -> 25.2 us  [swap(): return lax.ppermute(x, 'dp', [(i, i ^ bit) for i in range(n)])]
    ppermute x0 -> x14, starting transfers between devices: none -> 14.3 us  [swap(): return lax.ppermute(x, 'dp', [(i, i ^ bit) for i in range(n)])]
    reduce_scatter x1 -> x0, waiting for transfers between devices: 13.6 us -> none  [body(): lax.psum_scatter(partial_value, 'dp', scatter_dimension=0, tiled=True)]
    rev x0 -> x4, local copies, waits for them, and re-layouts: none -> 5.04 us  [merge_lse(): lse = jnp.logaddexp(lse, cut[:, ::-1].reshape(lse.shape))]
  transfers between devices with their start and end apart: 2 -> 14, of which waited for: 2 -> 7; matrix products, arithmetic and copies ran while one was open for 8% -> 19% of each run, Pallas kernels for 0% -> 0%
where the time goes in v1:
time: 73.5 us; the launch traced here: 73.1 us
  waiting for transfers between devices  25.2 us (34%)
  starting transfers between devices  14.3 us (19%)
  matrix products  13.8 us (19%)
  other arithmetic  10.2 us (14%)
  local copies, waits for them, and re-layouts  8.58 us (12%)
  between operations  0.98 us (1%)
    ppermute x14, waiting for transfers between devices, swap(): return lax.ppermute(x, 'dp', [(i, i ^ bit) for i in range(n)])  25.2 us
    ppermute x14, starting transfers between devices, swap(): return lax.ppermute(x, 'dp', [(i, i ^ bit) for i in range(n)])  14.3 us
    rev x4, local copies, waits for them, and re-layouts, merge_lse(): lse = jnp.logaddexp(lse, cut[:, ::-1].reshape(lse.shape))  5.04 us
    dot_general x2, matrix products, embed(): raw = jnp.dot(feats, weight, preferred_element_type=jnp.float32)  4.05 us
    select_n x4, other arithmetic, merge_lse(): lse = jnp.logaddexp(lse, cut[:, ::-1].reshape(lse.shape))  4.02 us
    unnamed x44, local copies, waits for them, and re-layouts  3.5 us
    dot_general x1, matrix products, body(): img_low = jnp.dot(images, b_img, preferred_element_type=jnp.float32)  2.59 us
    reduce_sum x1, other arithmetic, body(): jnp.sum(weighted, axis=0)[:, None] * txt_side  1.77 us
  transfers between devices with their start and end apart: 14, of which 7 were waited for; matrix products, arithmetic and copies ran while one was open for 19% of the time, Pallas kernels for 0%

profile of v1, /device:TPU:0, one launch (start us, length us, event | category | flops | bytes accessed | tf_op | source)
XLA Modules:
  0.0 73.1 jit_solution(9422962553782375359)
XLA Ops:
  0.6 0.0 copy-start
  0.7 3.3 %multiply_reduce_fusion.4 = (f32[128]{0:T(128)S(1)}, f32[128,1280]{1,0:T(8,128)S(1)}) fusion(bf16[128,1664]{1,0:T(8,128)(2,1)} %param.8, bf16[1664,1280]{1,0:T(8,128)(2,1)} %param.10), kind=kOutput, calls=%fused_computation.19 | convolution fusion | flops 545587072 | bytes 5341696 | tf_op jit(solution)/shard_map/dot_general | solution.py:11
  4.0 0.0 copy-done
  4.0 0.0 copy-start.9
  4.0 0.0 copy-start.2
  4.0 0.0 copy-start.8
  4.1 0.7 multiply_reduce_fusion.3
  4.8 0.8 %multiply_reduce_fusion.2 = (f32[128]{0:T(128)}, bf16[128,1280]{1,0:T(8,128)(2,1)S(1)}, bf16[128,1280]{1,0:T(8,128)(2,1)S(1)}) fusion(f32[128,1280]{1,0:T(8,128)S(1)} %get-tuple-element.13, f32[128]{0:T(128)S(1)} %get-tuple-element.18, f32[128,1280]{1,0:T(8,128)S(1)} %get-tuple-element.15, f32[128]{0:T(128)S(1)} %get-tuple-element.19), kind=kLoop, calls=%fused_computation.15 | loop fusion | flops 1310592 | bytes 1967616 | tf_op jit(solution)/shard_map/reduce_sum | solution.py:67
  5.6 3.0 %collective-permute-start.3 = (bf16[128,1280]{1,0:T(8,128)(2,1)S(1)}, bf16[128,1280]{1,0:T(8,128)(2,1)S(1)}, u32[]{:S(2)}, u32[]{:S(2)}) collective-permute-start(bf16[128,1280]{1,0:T(8,128)(2,1)S(1)} %get-tuple-element.7), channel_id=1, source_target_pairs={{0,4},{1,5},{2,6},{3,7},{4,0},{5,1},{6,2},{7,3},{8,12},{9,13},{10,... | collective-permute-start | bytes 983048 | tf_op jit(solution)/shard_map/ppermute | solution.py:30
  8.6 2.6 %collective-permute-start = (bf16[128,1280]{1,0:T(8,128)(2,1)S(1)}, bf16[128,1280]{1,0:T(8,128)(2,1)S(1)}, u32[]{:S(2)}, u32[]{:S(2)}) collective-permute-start(bf16[128,1280]{1,0:T(8,128)(2,1)S(1)} %get-tuple-element.8), channel_id=1, source_target_pairs={{0,8},{1,9},{2,10},{3,11},{4,12},{5,13},{6,14},{7,15},{8,0},{9,1},... | collective-permute-start | bytes 983048 | tf_op jit(solution)/shard_map/ppermute | solution.py:30
  11.2 1.5 %collective-permute-start.4 = (bf16[128,1280]{1,0:T(8,128)(2,1)S(1)}, bf16[128,1280]{1,0:T(8,128)(2,1)S(1)}, u32[]{:S(2)}, u32[]{:S(2)}) collective-permute-start(bf16[128,1280]{1,0:T(8,128)(2,1)S(1)} %get-tuple-element.7), channel_id=1, source_target_pairs={{0,2},{1,3},{2,0},{3,1},{4,6},{5,7},{6,4},{7,5},{8,10},{9,11},{10,... | collective-permute-start | bytes 983048 | tf_op jit(solution)/shard_map/ppermute | solution.py:30
  12.7 0.0 collective-permute-start.1
  12.7 10.5 %collective-permute-done.3 = bf16[128,1280]{1,0:T(8,128)(2,1)S(1)} collective-permute-done((bf16[128,1280]{1,0:T(8,128)(2,1)S(1)}, bf16[128,1280]{1,0:T(8,128)(2,1)S(1)}, u32[]{:S(2)}, u32[]{:S(2)}) %collective-permute-start.3) | collective-permute-done | bytes 327712 | tf_op jit(solution)/shard_map/ppermute | solution.py:30
  23.2 1.7 %collective-permute-start.5 = (bf16[128,1280]{1,0:T(8,128)(2,1)S(1)}, bf16[128,1280]{1,0:T(8,128)(2,1)S(1)}, u32[]{:S(2)}, u32[]{:S(2)}) collective-permute-start(bf16[128,1280]{1,0:T(8,128)(2,1)S(1)} %collective-permute-done.3), channel_id=1, source_target_pairs={{0,2},{1,3},{2,0},{3,1},{4,6},{5,7},{6,4},{7,5},{8,10},{9,11},{10,... | collective-permute-start | bytes 983048 | tf_op jit(solution)/shard_map/ppermute | solution.py:30
  24.9 0.8 %collective-permute-done = bf16[128,1280]{1,0:T(8,128)(2,1)S(1)} collective-permute-done((bf16[128,1280]{1,0:T(8,128)(2,1)S(1)}, bf16[128,1280]{1,0:T(8,128)(2,1)S(1)}, u32[]{:S(2)}, u32[]{:S(2)}) %collective-permute-start) | collective-permute-done | bytes 327712 | tf_op jit(solution)/shard_map/ppermute | solution.py:30
  25.7 0.0 collective-permute-start.2
  25.8 0.8 %fusion.16 = f32[128,32]{1,0:T(8,128)} fusion(bf16[128,1280]{1,0:T(8,128)(2,1)S(1)} %copy-done.3, bf16[1280,32]{0,1:T(8,128)(2,1)S(1)} %copy-done.9), kind=kOutput, calls=%fused_computation.53 | convolution fusion | flops 10485760 | bytes 425984 | tf_op jit(solution)/shard_map/dot_general | solution.py:69
  26.6 0.9 %fusion.15 = f32[128,32]{1,0:T(8,128)} fusion(bf16[128,1664]{1,0:T(8,128)(2,1)S(1)} %copy-done.2, bf16[1664,32]{0,1:T(8,128)(2,1)S(1)} %copy-done.8), kind=kOutput, calls=%fused_computation.52 | convolution fusion | flops 13631488 | bytes 548864 | tf_op jit(solution)/shard_map/dot_general | solution.py:68
  27.5 0.0 collective-permute-done.4
  27.5 0.0 collective-permute-done.1
  27.5 4.6 %collective-permute-done.5 = bf16[128,1280]{1,0:T(8,128)(2,1)S(1)} collective-permute-done((bf16[128,1280]{1,0:T(8,128)(2,1)S(1)}, bf16[128,1280]{1,0:T(8,128)(2,1)S(1)}, u32[]{:S(2)}, u32[]{:S(2)}) %collective-permute-start.5) | collective-permute-done | bytes 327712 | tf_op jit(solution)/shard_map/ppermute | solution.py:30
  32.1 0.0 collective-permute-done.2
  32.1 0.0 copy-start.20
  32.1 1.0 %multiply_reduce_fusion.1 = (f32[512]{0:T(512)S(1)}, f32[512,512]{1,0:T(8,128)S(1)}) fusion(bf16[128,1280]{1,0:T(8,128)(2,1)S(1)} %collective-permute-done.5, bf16[128,1280]{1,0:T(8,128)(2,1)S(1)} %collective-permute-done.4, bf16[128,1280]{1,0:T(8,128)(2,1)S(1)} %collective-permute-done.3, bf16[128,1280]{1,0:T(8,128)(2,1)S(1)} %get-tuple-element.7, ...), kind=kOutput, calls=%fused_computation.12 | convolution fusion | flops 682098176 | bytes 3672064 | tf_op jit(solution)/shard_map/dot_general | solution.py:17
  33.1 0.4 exponential_reduce_fusion.1
  33.5 0.2 exponential_reduce_fusion
  33.7 0.6 fusion.11
  34.3 0.4 collective-permute-start.6
  34.7 2.5 %collective-permute-start.8 = (f32[4,128]{1,0:T(4,128)}, f32[4,128]{1,0:T(4,128)}, u32[]{:S(2)}, u32[]{:S(2)}) collective-permute-start(f32[4,128]{1,0:T(4,128)} %fusion.11), channel_id=1, source_target_pairs={{0,4},{1,5},{2,6},{3,7},{4,0},{5,1},{6,2},{7,3},{8,12},{9,13},{10,... | collective-permute-start | bytes 6152 | tf_op jit(solution)/shard_map/ppermute | solution.py:30
  37.2 1.2 %convolution_convert_fusion.1 = bf16[512,128]{1,0:T(8,128)(2,1)} fusion(bf16[1280,128]{1,0:T(8,128)(2,1)S(1)} %copy-done.17, bf16[128,1280]{1,0:T(8,128)(2,1)S(1)} %collective-permute-done.5, bf16[128,1280]{1,0:T(8,128)(2,1)S(1)} %collective-permute-done.4, bf16[128,1280]{1,0:T(8,128)(2,1)S(1)} %collective-permute-done.3, ...), kind=kOutput, calls=%fused_computation.5 | convolution fusion | flops 173080576 | bytes 1769472 | tf_op jit(solution)/shard_map/dot_general | solution.py:71
  38.4 1.2 %convolution_convert_fusion = bf16[512,128]{1,0:T(8,128)(2,1)} fusion(bf16[1280,128]{1,0:T(8,128)(2,1)S(1)} %copy-done.16, bf16[128,1280]{1,0:T(8,128)(2,1)S(1)} %collective-permute-done.2, bf16[128,1280]{1,0:T(8,128)(2,1)S(1)} %collective-permute-done.1, bf16[128,1280]{1,0:T(8,128)(2,1)S(1)} %collective-permute-done, bf16[128,1280]{1,0:T(8,128)(2,1)S(1)} %get-tuple-element.8), kind=kOutput, calls=%fused_computation.4 | convolution fusion | flops 173080576 | bytes 1769472 | tf_op jit(solution)/shard_map/dot_general | solution.py:72
  39.5 0.5 fusion.12
  40.1 0.0 collective-permute-done.6
  40.1 0.6 copy-done.14
  40.7 1.3 %rev.12 = f32[2,2,1,128]{3,1,0,2:T(2,128)} reverse(f32[2,2,1,128]{3,1,0,2:T(2,128)} %bitcast.52), dimensions={1} | reverse | bytes 4096 | tf_op jit(solution)/shard_map/rev | solution.py:44
  41.9 1.3 %add_select_fusion.4 = f32[4,128]{1,0:T(4,128)} fusion(f32[4,128]{1,0:T(4,128)} %bitcast.46, f32[512]{0:T(512)S(1)} %get-tuple-element.16, f32[512]{0:T(512)S(1)} %get-tuple-element.4), kind=kLoop, calls=%fused_computation.41 | loop fusion | flops 4608 | bytes 8192 | tf_op jit(solution)/shard_map/select_n | solution.py:44
  43.2 0.0 collective-permute-start.7
  43.2 0.0 collective-permute-done.8
  43.2 1.3 %rev.14 = f32[2,2,1,128]{3,1,0,2:T(2,128)} reverse(f32[2,2,1,128]{3,1,0,2:T(2,128)} %bitcast.7), dimensions={1} | reverse | bytes 4096 | tf_op jit(solution)/shard_map/rev | solution.py:44
  44.5 1.3 %add_select_fusion.1 = f32[4,128]{1,0:T(4,128)} fusion(f32[4,128]{1,0:T(4,128)} %bitcast.48, f32[512]{0:T(512)S(1)} %get-tuple-element.5, f32[512]{0:T(512)S(1)} %exponential_reduce_fusion), kind=kLoop, calls=%fused_computation.37 | loop fusion | flops 4608 | bytes 8192 | tf_op jit(solution)/shard_map/select_n | solution.py:44
  45.8 1.5 %collective-permute-start.9 = (f32[4,128]{1,0:T(4,128)}, f32[4,128]{1,0:T(4,128)}, u32[]{:S(2)}, u32[]{:S(2)}) collective-permute-start(f32[4,128]{1,0:T(4,128)} %add_select_fusion.1), channel_id=1, source_target_pairs={{0,2},{1,3},{2,0},{3,1},{4,6},{5,7},{6,4},{7,5},{8,10},{9,11},{10,... | collective-permute-start | bytes 6152 | tf_op jit(solution)/shard_map/ppermute | solution.py:30
  47.3 2.6 %fusion.14 = f32[512,128]{1,0:T(8,128)} fusion(bf16[1280,128]{1,0:T(8,128)(2,1)} %param.13, bf16[128,1280]{1,0:T(8,128)(2,1)} %copy-done.20, bf16[128,1280]{1,0:T(8,128)(2,1)} %copy-done.19, bf16[128,1280]{1,0:T(8,128)(2,1)} %copy-done.18, bf16[128,1280]{1,0:T(8,128)(2,1)} %copy-done.4), kind=kOutput, calls=%fused_computation.51 | convolution fusion | flops 173015040 | bytes 1900544 | tf_op jit(solution)/shard_map/dot_general | solution.py:70
  49.9 0.0 collective-permute-done.7
  49.9 1.3 %rev.13 = f32[1,2,2,128]{3,2,1,0:T(2,128)} reverse(f32[1,2,2,128]{3,2,1,0:T(2,128)} %bitcast.4), dimensions={1} | reverse | bytes 4096 | tf_op jit(solution)/shard_map/rev | solution.py:44
  51.1 0.0 collective-permute-done.9
  51.1 1.2 %rev.15 = f32[1,2,2,128]{3,2,1,0:T(2,128)} reverse(f32[1,2,2,128]{3,2,1,0:T(2,128)} %bitcast.10), dimensions={1} | reverse | bytes 4096 | tf_op jit(solution)/shard_map/rev | solution.py:44
  52.4 0.7 %add_select_fusion.3 = f32[512]{0:T(512)S(1)} fusion(f32[512]{0:T(512)} %bitcast.50, f32[512]{0:T(512)} %bitcast.47, f32[512]{0:T(512)S(1)} %get-tuple-element.16, f32[512]{0:T(512)S(1)} %get-tuple-element.4), kind=kLoop, calls=%fused_computation.40 | loop fusion | flops 8704 | bytes 10240 | tf_op jit(solution)/shard_map/select_n | solution.py:44
  53.1 0.7 add_select_fusion
  53.9 1.8 %fusion.2 = (f32[512]{0:T(512)S(1)}, f32[512]{0:T(512)S(1)}, bf16[512,512]{1,0:T(8,128)(2,1)S(1)}) fusion(f32[512,512]{1,0:T(8,128)} %copy-done.1, f32[512]{0:T(512)S(1)} %add_select_fusion, f32[512]{0:T(512)S(1)} %add_select_fusion.3), kind=kLoop, calls=%fused_computation.20 | loop fusion | flops 2096128 | bytes 1581056 | tf_op jit(solution)/shard_map/reduce_sum | solution.py:89
  55.7 1.3 %multiply_subtract_fusion.1 = f32[512,128]{1,0:T(8,128)S(1)} fusion(f32[512,128]{1,0:T(8,128)} %fusion.14, f32[512]{0:T(512)S(1)} %get-tuple-element.3, bf16[512,512]{1,0:T(8,128)(2,1)S(1)} %get-tuple-element.9, bf16[512,128]{1,0:T(8,128)(2,1)} %convolution_convert_fusion.1), kind=kOutput, calls=%fused_computation.23 | convolution fusion | flops 67239936 | bytes 1181696 | tf_op jit(solution)/shard_map/dot_general | solution.py:82
  57.0 0.3 collective-permute-start.10
  57.3 0.3 multiply_subtract_fusion
  57.7 0.6 collective-permute-start.12
  58.3 0.2 collective-permute-done.10
  58.5 0.1 collective-permute-start.11
  58.6 4.8 %collective-permute-done.12 = f32[256,128]{1,0:T(8,128)S(1)} collective-permute-done((f32[256,128]{1,0:T(8,128)S(1)}, f32[256,128]{1,0:T(8,128)S(1)}, u32[]{:S(2)}, u32[]{:S(2)}) %collective-permute-start.12) | collective-permute-done | bytes 131104 | tf_op jit(solution)/shard_map/ppermute | solution.py:30
  63.5 0.1 collective-permute-start.13
  63.6 0.9 %collective-permute-done.11 = f32[128,128]{1,0:T(8,128)S(1)} collective-permute-done((f32[128,128]{1,0:T(8,128)S(1)}, f32[128,128]{1,0:T(8,128)S(1)}, u32[]{:S(2)}, u32[]{:S(2)}) %collective-permute-start.11) | collective-permute-done | bytes 65568 | tf_op jit(solution)/shard_map/ppermute | solution.py:30
  64.5 3.3 %collective-permute-done.13 = f32[128,128]{1,0:T(8,128)S(1)} collective-permute-done((f32[128,128]{1,0:T(8,128)S(1)}, f32[128,128]{1,0:T(8,128)S(1)}, u32[]{:S(2)}, u32[]{:S(2)}) %collective-permute-start.13) | collective-permute-done | bytes 65568 | tf_op jit(solution)/shard_map/ppermute | solution.py:30
  67.8 1.0 %fusion.5 = (f32[128,128]{1,0:T(8,128)S(1)}, f32[128,128]{1,0:T(8,128)S(1)}) fusion(f32[512,128]{1,0:T(8,128)S(1)} %fusion.12, f32[128,128]{1,0:T(8,128)S(1)} %collective-permute-done.13, f32[256,128]{1,0:T(8,128)S(1)} %slice_add_fusion, bf16[512,128]{1,0:T(8,128)(2,1)S(1)} %copy-done.7, f32[128]{0:T(128)S(1)} %copy-done.11, ...), kind=kLoop, calls=%fused_computation.28 | loop fusion | flops 229376 | bytes 591360 | tf_op jit(solution)/shard_map/mul | solution.py:96
  68.8 0.8 %multiply_convert_fusion = bf16[128,32,128]{2,1,0:T(8,128)(2,1)S(1)} fusion(f32[128,128]{1,0:T(8,128)S(1)} %get-tuple-element.10, f32[128,32]{1,0:T(8,128)S(1)} %copy-done.6), kind=kLoop, calls=%fused_computation | loop fusion | flops 1048576 | bytes 1130496 | tf_op jit(solution)/shard_map/convert_element_type | solution.py:98
  69.6 1.4 %copy.18 = bf16[16,8,32,128]{3,1,2,0:T(8,128)(2,1)} copy(bf16[16,8,32,128]{3,2,1,0:T(8,128)(2,1)S(1)} %bitcast.42) | data formatting | bytes 2097152
  71.0 0.7 %multiply_convert_fusion.1 = bf16[128,32,128]{2,1,0:T(8,128)(2,1)S(1)} fusion(f32[128,128]{1,0:T(8,128)S(1)} %get-tuple-element.11, f32[128,32]{1,0:T(8,128)S(1)} %copy-done.5), kind=kLoop, calls=%fused_computation.1 | loop fusion | flops 1048576 | bytes 1130496 | tf_op jit(solution)/shard_map/convert_element_type | solution.py:98
  71.7 1.4 %copy.19 = bf16[16,8,32,128]{3,1,2,0:T(8,128)(2,1)} copy(bf16[16,8,32,128]{3,2,1,0:T(8,128)(2,1)S(1)} %bitcast.43) | data formatting | bytes 2097152
  (44 shorter events, 0.1 us)
Async XLA Ops:
  0.6 3.4 %copy-start = (bf16[1280,1280]{1,0:T(8,128)(2,1)S(1)}, bf16[1280,1280]{1,0:T(8,128)(2,1)}, u32[]{:S(2)}) copy-start(bf16[1280,1280]{1,0:T(8,128)(2,1)} %param.11) | copy-start | bytes 9830404
  0.6 3.4 %copy-start.3 = (bf16[128,1280]{1,0:T(8,128)(2,1)S(1)}, bf16[128,1280]{1,0:T(8,128)(2,1)}, u32[]{:S(2)}) copy-start(bf16[128,1280]{1,0:T(8,128)(2,1)} %param.9) | copy-start | bytes 983044
  4.0 21.7 %copy-start.9 = (bf16[1280,32]{0,1:T(8,128)(2,1)S(1)}, bf16[1280,32]{0,1:T(8,128)(2,1)}, u32[]{:S(2)}) copy-start(bf16[1280,32]{0,1:T(8,128)(2,1)} %param.14) | copy-start | bytes 245764
  4.0 22.6 %copy-start.2 = (bf16[128,1664]{1,0:T(8,128)(2,1)S(1)}, bf16[128,1664]{1,0:T(8,128)(2,1)}, u32[]{:S(2)}) copy-start(bf16[128,1664]{1,0:T(8,128)(2,1)} %param.8) | copy-start | bytes 1277956
  4.0 22.6 %copy-start.8 = (bf16[1664,32]{0,1:T(8,128)(2,1)S(1)}, bf16[1664,32]{0,1:T(8,128)(2,1)}, u32[]{:S(2)}) copy-start(bf16[1664,32]{0,1:T(8,128)(2,1)} %param.12) | copy-start | bytes 319492
  4.8 27.3 %copy-start.10 = (f32[128]{0:T(128)}, f32[128]{0:T(128)S(1)}, u32[]{:S(2)}) copy-start(f32[128]{0:T(128)S(1)} %get-tuple-element.18) | copy-start | bytes 1540
  4.8 27.3 %copy-start.12 = (f32[128]{0:T(128)}, f32[128]{0:T(128)S(1)}, u32[]{:S(2)}) copy-start(f32[128]{0:T(128)S(1)} %get-tuple-element.19) | copy-start | bytes 1540
  5.6 32.8 %copy-start.4 = (bf16[128,1280]{1,0:T(8,128)(2,1)}, bf16[128,1280]{1,0:T(8,128)(2,1)S(1)}, u32[]{:S(2)}) copy-start(bf16[128,1280]{1,0:T(8,128)(2,1)S(1)} %get-tuple-element.8) | copy-start | bytes 983044
  5.6 17.6 %collective-permute-start.3 = (bf16[128,1280]{1,0:T(8,128)(2,1)S(1)}, bf16[128,1280]{1,0:T(8,128)(2,1)S(1)}, u32[]{:S(2)}, u32[]{:S(2)}) collective-permute-start(bf16[128,1280]{1,0:T(8,128)(2,1)S(1)} %get-tuple-element.7), channel_id=1, source_target_pairs={{0,4},{1,5},{2,6},{3,7},{4,0},{5,1},{6,2},{7,3},{8,12},{9,13},{10,... | collective-permute-start | bytes 983048 | tf_op jit(solution)/shard_map/ppermute | solution.py:30
  8.6 17.1 %collective-permute-start = (bf16[128,1280]{1,0:T(8,128)(2,1)S(1)}, bf16[128,1280]{1,0:T(8,128)(2,1)S(1)}, u32[]{:S(2)}, u32[]{:S(2)}) collective-permute-start(bf16[128,1280]{1,0:T(8,128)(2,1)S(1)} %get-tuple-element.8), channel_id=1, source_target_pairs={{0,8},{1,9},{2,10},{3,11},{4,12},{5,13},{6,14},{7,15},{8,0},{9,1},... | collective-permute-start | bytes 983048 | tf_op jit(solution)/shard_map/ppermute | solution.py:30
  11.2 16.3 %collective-permute-start.4 = (bf16[128,1280]{1,0:T(8,128)(2,1)S(1)}, bf16[128,1280]{1,0:T(8,128)(2,1)S(1)}, u32[]{:S(2)}, u32[]{:S(2)}) collective-permute-start(bf16[128,1280]{1,0:T(8,128)(2,1)S(1)} %get-tuple-element.7), channel_id=1, source_target_pairs={{0,2},{1,3},{2,0},{3,1},{4,6},{5,7},{6,4},{7,5},{8,10},{9,11},{10,... | collective-permute-start | bytes 983048 | tf_op jit(solution)/shard_map/ppermute | solution.py:30
  12.7 14.8 %collective-permute-start.1 = (bf16[128,1280]{1,0:T(8,128)(2,1)S(1)}, bf16[128,1280]{1,0:T(8,128)(2,1)S(1)}, u32[]{:S(2)}, u32[]{:S(2)}) collective-permute-start(bf16[128,1280]{1,0:T(8,128)(2,1)S(1)} %get-tuple-element.8), channel_id=1, source_target_pairs={{0,1},{1,0},{2,3},{3,2},{4,5},{5,4},{6,7},{7,6},{8,9},{9,8},{10,11... | collective-permute-start | bytes 983048 | tf_op jit(solution)/shard_map/ppermute | solution.py:30
  23.2 8.9 %collective-permute-start.5 = (bf16[128,1280]{1,0:T(8,128)(2,1)S(1)}, bf16[128,1280]{1,0:T(8,128)(2,1)S(1)}, u32[]{:S(2)}, u32[]{:S(2)}) collective-permute-start(bf16[128,1280]{1,0:T(8,128)(2,1)S(1)} %collective-permute-done.3), channel_id=1, source_target_pairs={{0,2},{1,3},{2,0},{3,1},{4,6},{5,7},{6,4},{7,5},{8,10},{9,11},{10,... | collective-permute-start | bytes 983048 | tf_op jit(solution)/shard_map/ppermute | solution.py:30
  25.7 12.6 %copy-start.18 = (bf16[128,1280]{1,0:T(8,128)(2,1)}, bf16[128,1280]{1,0:T(8,128)(2,1)S(1)}, u32[]{:S(2)}) copy-start(bf16[128,1280]{1,0:T(8,128)(2,1)S(1)} %collective-permute-done) | copy-start | bytes 983044
  25.7 6.4 %collective-permute-start.2 = (bf16[128,1280]{1,0:T(8,128)(2,1)S(1)}, bf16[128,1280]{1,0:T(8,128)(2,1)S(1)}, u32[]{:S(2)}, u32[]{:S(2)}) collective-permute-start(bf16[128,1280]{1,0:T(8,128)(2,1)S(1)} %collective-permute-done), channel_id=1, source_target_pairs={{0,1},{1,0},{2,3},{3,2},{4,5},{5,4},{6,7},{7,6},{8,9},{9,8},{10,11... | collective-permute-start | bytes 983048 | tf_op jit(solution)/shard_map/ppermute | solution.py:30
  27.5 9.7 %copy-start.17 = (bf16[1280,128]{1,0:T(8,128)(2,1)S(1)}, bf16[1280,128]{1,0:T(8,128)(2,1)}, u32[]{:S(2)}) copy-start(bf16[1280,128]{1,0:T(8,128)(2,1)} %param.13) | copy-start | bytes 983044
  27.5 10.9 %copy-start.19 = (bf16[128,1280]{1,0:T(8,128)(2,1)}, bf16[128,1280]{1,0:T(8,128)(2,1)S(1)}, u32[]{:S(2)}) copy-start(bf16[128,1280]{1,0:T(8,128)(2,1)S(1)} %collective-permute-done.1) | copy-start | bytes 983044
  32.1 6.2 %copy-start.20 = (bf16[128,1280]{1,0:T(8,128)(2,1)}, bf16[128,1280]{1,0:T(8,128)(2,1)S(1)}, u32[]{:S(2)}) copy-start(bf16[128,1280]{1,0:T(8,128)(2,1)S(1)} %collective-permute-done.2) | copy-start | bytes 983044
  33.1 5.3 %copy-start.1 = (f32[512,512]{1,0:T(8,128)}, f32[512,512]{1,0:T(8,128)S(1)}, u32[]{:S(2)}) copy-start(f32[512,512]{1,0:T(8,128)S(1)} %get-tuple-element.17) | copy-start | bytes 3145732
  34.3 4.1 %copy-start.16 = (bf16[1280,128]{1,0:T(8,128)(2,1)S(1)}, bf16[1280,128]{1,0:T(8,128)(2,1)}, u32[]{:S(2)}) copy-start(bf16[1280,128]{1,0:T(8,128)(2,1)} %param.15) | copy-start | bytes 983044
  34.3 5.8 %collective-permute-start.6 = (f32[4,128]{1,0:T(4,128)S(1)}, f32[4,128]{1,0:T(4,128)S(1)}, u32[]{:S(2)}, u32[]{:S(2)}) collective-permute-start(f32[4,128]{1,0:T(4,128)S(1)} %fusion.10), channel_id=1, source_target_pairs={{0,8},{1,9},{2,10},{3,11},{4,12},{5,13},{6,14},{7,15},{8,0},{9,1},... | collective-permute-start | bytes 6152 | tf_op jit(solution)/shard_map/ppermute | solution.py:30
  34.7 8.5 %collective-permute-start.8 = (f32[4,128]{1,0:T(4,128)}, f32[4,128]{1,0:T(4,128)}, u32[]{:S(2)}, u32[]{:S(2)}) collective-permute-start(f32[4,128]{1,0:T(4,128)} %fusion.11), channel_id=1, source_target_pairs={{0,4},{1,5},{2,6},{3,7},{4,0},{5,1},{6,2},{7,3},{8,12},{9,13},{10,... | collective-permute-start | bytes 6152 | tf_op jit(solution)/shard_map/ppermute | solution.py:30
  40.1 0.6 copy-start.14
  43.2 6.7 %collective-permute-start.7 = (f32[4,128]{1,0:T(4,128)}, f32[4,128]{1,0:T(4,128)}, u32[]{:S(2)}, u32[]{:S(2)}) collective-permute-start(f32[4,128]{1,0:T(4,128)} %add_select_fusion.4), channel_id=1, source_target_pairs={{0,1},{1,0},{2,3},{3,2},{4,5},{5,4},{6,7},{7,6},{8,9},{9,8},{10,11... | collective-permute-start | bytes 6152 | tf_op jit(solution)/shard_map/ppermute | solution.py:30
  45.8 5.4 %collective-permute-start.9 = (f32[4,128]{1,0:T(4,128)}, f32[4,128]{1,0:T(4,128)}, u32[]{:S(2)}, u32[]{:S(2)}) collective-permute-start(f32[4,128]{1,0:T(4,128)} %add_select_fusion.1), channel_id=1, source_target_pairs={{0,2},{1,3},{2,0},{3,1},{4,6},{5,7},{6,4},{7,5},{8,10},{9,11},{10,... | collective-permute-start | bytes 6152 | tf_op jit(solution)/shard_map/ppermute | solution.py:30
  52.4 5.0 %copy-start.7 = (bf16[512,128]{1,0:T(8,128)(2,1)S(1)}, bf16[512,128]{1,0:T(8,128)(2,1)}, u32[]{:S(2)}) copy-start(bf16[512,128]{1,0:T(8,128)(2,1)} %convolution_convert_fusion) | copy-start | bytes 393220
  53.9 9.7 %copy-start.15 = (f32[128]{0:T(128)S(1)}, f32[128]{0:T(128)}, u32[]{:S(2)}) copy-start(f32[128]{0:T(128)} %get-tuple-element.6) | copy-start | bytes 1540
  53.9 13.9 %copy-start.11 = (f32[128]{0:T(128)S(1)}, f32[128]{0:T(128)}, u32[]{:S(2)}) copy-start(f32[128]{0:T(128)} %copy-done.10) | copy-start | bytes 1540
  53.9 13.9 %copy-start.13 = (f32[128]{0:T(128)S(1)}, f32[128]{0:T(128)}, u32[]{:S(2)}) copy-start(f32[128]{0:T(128)} %copy-done.12) | copy-start | bytes 1540
  55.7 13.1 %copy-start.6 = (f32[128,32]{1,0:T(8,128)S(1)}, f32[128,32]{1,0:T(8,128)}, u32[]{:S(2)}) copy-start(f32[128,32]{1,0:T(8,128)} %fusion.16) | copy-start | bytes 49156
  57.0 1.4 %collective-permute-start.10 = (f32[256,128]{1,0:T(8,128)S(1)}, f32[256,128]{1,0:T(8,128)S(1)}, u32[]{:S(2)}, u32[]{:S(2)}) collective-permute-start(f32[256,128]{1,0:T(8,128)S(1)} %slice.49), channel_id=1, source_target_pairs={{0,1},{1,0},{2,3},{3,2},{4,5},{5,4},{6,7},{7,6},{8,9},{9,8},{10,11... | collective-permute-start | bytes 393224 | tf_op jit(solution)/shard_map/ppermute | solution.py:30
  57.7 13.3 %copy-start.5 = (f32[128,32]{1,0:T(8,128)S(1)}, f32[128,32]{1,0:T(8,128)}, u32[]{:S(2)}) copy-start(f32[128,32]{1,0:T(8,128)} %fusion.15) | copy-start | bytes 49156
  57.7 5.7 %collective-permute-start.12 = (f32[256,128]{1,0:T(8,128)S(1)}, f32[256,128]{1,0:T(8,128)S(1)}, u32[]{:S(2)}, u32[]{:S(2)}) collective-permute-start(f32[256,128]{1,0:T(8,128)S(1)} %slice.55), channel_id=1, source_target_pairs={{0,2},{1,3},{2,0},{3,1},{4,6},{5,7},{6,4},{7,5},{8,10},{9,11},{10,... | collective-permute-start | bytes 393224 | tf_op jit(solution)/shard_map/ppermute | solution.py:30
  58.5 6.0 %collective-permute-start.11 = (f32[128,128]{1,0:T(8,128)S(1)}, f32[128,128]{1,0:T(8,128)S(1)}, u32[]{:S(2)}, u32[]{:S(2)}) collective-permute-start(f32[128,128]{1,0:T(8,128)S(1)} %slice.51), channel_id=1, source_target_pairs={{0,8},{1,9},{2,10},{3,11},{4,12},{5,13},{6,14},{7,15},{8,0},{9,1},... | collective-permute-start | bytes 196616 | tf_op jit(solution)/shard_map/ppermute | solution.py:30
  63.5 4.3 %collective-permute-start.13 = (f32[128,128]{1,0:T(8,128)S(1)}, f32[128,128]{1,0:T(8,128)S(1)}, u32[]{:S(2)}, u32[]{:S(2)}) collective-permute-start(f32[128,128]{1,0:T(8,128)S(1)} %slice.57), channel_id=1, source_target_pairs={{0,4},{1,5},{2,6},{3,7},{4,0},{5,1},{6,2},{7,3},{8,12},{9,13},{10,... | collective-permute-start | bytes 196616 | tf_op jit(solution)/shard_map/ppermute | solution.py:30

commit v2 on v1

v2 whole, which is shorter than its diff:
```python
import functools
import jax
import jax.numpy as jnp
from jax import lax
from jax.experimental import pallas as pl
from jax.experimental.pallas import tpu as pltpu
from jax.sharding import PartitionSpec as P

LOGIT_SCALE = 100.0
EPSILON = 1e-06
F32 = jnp.float32
BF16 = jnp.bfloat16
LANES = 128


def dot(left, right, left_dim=1, right_dim=0):
    return lax.dot_general(
        left, right, (((left_dim,), (right_dim,)), ((), ())), preferred_element_type=F32
    )


def call(kernel, outs, args, scratch=(), flops=0, limit=32):
    args = [pltpu.with_memory_space_constraint(a, pltpu.VMEM) for a in args]
    size = sum(a.size * a.dtype.itemsize for a in args)
    return pl.pallas_call(
        kernel,
        out_shape=[jax.ShapeDtypeStruct(s, d) for s, d in outs],
        in_specs=[pl.BlockSpec(memory_space=pltpu.VMEM)] * len(args),
        out_specs=[pl.BlockSpec(memory_space=pltpu.VMEM)] * len(outs),
        scratch_shapes=list(scratch),
        compiler_params=pltpu.CompilerParams(vmem_limit_bytes=limit << 20),
        cost_estimate=pl.CostEstimate(flops=flops, bytes_accessed=size, transcendentals=0),
    )(*args)


def span(bits):
    offsets = [0]
    for bit in bits:
        offsets = offsets + [o ^ bit for o in offsets]
    return offsets


def split_bits(n):
    bits = [1 << b for b in range(n.bit_length() - 1)]
    assert 1 << len(bits) == n
    half = len(bits) // 2
    return bits[:half:-1] + bits[:1], bits[half:0:-1]


def swap(x, offset, n):
    return lax.ppermute(x, "dp", [(i, i ^ offset) for i in range(n)])


def gather(block, bits, n):
    blocks = [block]
    for bit in bits:
        blocks = blocks + [swap(b, bit, n) for b in blocks]
    return blocks


def embed_kernel(feats, weight, *rest):
    raw = dot(feats[...], weight[...])
    inverse = lax.rsqrt(jnp.sum(raw * raw, axis=1, keepdims=True) + EPSILON)
    if len(rest) == 3:
        factor, emb, keys = rest
        keys[...] = dot(feats[...], factor[...]) * inverse
    else:
        (emb,) = rest
    emb[...] = (raw * inverse).astype(BF16)


def embed(feats, weight, factor=None):
    rows, emb = feats.shape[0], weight.shape[1]
    outs = [((rows, emb), BF16)]
    args = [feats, weight]
    if factor is not None:
        outs.append(((rows, factor.shape[1]), F32))
        args.append(factor)
    return call(embed_kernel, outs, args, flops=2 * rows * weight.size)


def column_of(row):
    return jnp.broadcast_to(row, (LANES, LANES)).T


def scores_kernel(ni, nt, *refs):
    images, texts = refs[:ni], refs[ni : ni + nt]
    raw, row_lse, col_lse, all_images, all_texts = refs[ni + nt :]
    rows = images[0].shape[0]
    for a in range(ni):
        all_images[a * rows : (a + 1) * rows] = images[a][...]
    for t in range(nt):
        all_texts[t * rows : (t + 1) * rows] = texts[t][...]
    raw[...] = dot(all_images[...], all_texts[...], 1, 1)
    for a in range(ni):
        scores = LOGIT_SCALE * raw[a * rows : (a + 1) * rows]
        top = jnp.max(scores, axis=1, keepdims=True)
        lse = top + jnp.log(jnp.sum(jnp.exp(scores - top), axis=1, keepdims=True))
        row_lse[a : a + 1] = jnp.broadcast_to(lse, (rows, LANES)).T[:1]
    for t in range(nt):
        scores = LOGIT_SCALE * raw[:, t * rows : (t + 1) * rows]
        top = jnp.max(scores, axis=0, keepdims=True)
        col_lse[t : t + 1] = top + jnp.log(jnp.sum(jnp.exp(scores - top), axis=0, keepdims=True))


def factors_kernel(ni, nt, *refs):
    images, texts, (b_img, b_txt) = refs[:ni], refs[ni : ni + nt], refs[ni + nt : ni + nt + 2]
    img_low, img_side_t, txt_low, txt_side_t, img_base, txt_base = refs[ni + nt + 2 :]
    rows = images[0].shape[0]
    for a in range(ni):
        here = slice(a * rows, (a + 1) * rows)
        low = dot(images[a][...], b_img[...])
        side = dot(images[a][...], b_txt[...])
        img_low[here] = low
        img_side_t[:, here] = side.T.astype(BF16)
        if a == 0:
            own_img_low, own_img_side = low, side.astype(BF16).astype(F32)
    for t in range(nt):
        here = slice(t * rows, (t + 1) * rows)
        low = dot(texts[t][...], b_img[...]).astype(BF16)
        side = dot(texts[t][...], b_txt[...])
        txt_low[here] = low
        txt_side_t[:, here] = side.T
        if t == 0:
            own_txt_low, own_txt_side = low.astype(F32), side
    diagonal = jnp.sum(
        images[0][...].astype(F32) * texts[0][...].astype(F32), axis=1, keepdims=True
    )
    img_base[...] = 2.0 * (diagonal * own_img_low - own_txt_low)
    txt_base[...] = 2.0 * (diagonal * own_txt_side - own_img_side)


def merge(parts):
    slots = parts[0].shape[0]
    lined = [parts[0][...]]
    for k in range(1, len(parts)):
        lined.append(
            jnp.concatenate([parts[k][s ^ k : (s ^ k) + 1] for s in range(slots)], axis=0)
        )
    top = functools.reduce(jnp.maximum, lined)
    return top + jnp.log(sum(jnp.exp(p - top) for p in lined))


def weights_kernel(ni, nt, *refs):
    row_parts, col_parts = refs[:ni], refs[ni : ni + nt]
    raw, img_low, img_side_t, txt_low, txt_side_t = refs[ni + nt : ni + nt + 5]
    img_parts = refs[ni + nt + 5 : 2 * ni + nt + 5]
    txt_parts = refs[2 * ni + nt + 5 : 2 * ni + 2 * nt + 5]
    weights_bf = refs[-1]
    rows = LANES
    row_lse = merge(row_parts)
    col_lse = merge(col_parts)
    inner_col = [jnp.zeros((1, rows), F32) for _ in range(nt)]
    for a in range(ni):
        row = column_of(row_lse[a : a + 1])
        inner_row = jnp.zeros((rows, rows), F32)
        for t in range(nt):
            here = raw[a * rows : (a + 1) * rows, t * rows : (t + 1) * rows]
            scores = LOGIT_SCALE * here
            weights = jnp.exp(scores - row) + jnp.exp(scores - col_lse[t : t + 1])
            weights_bf[a * rows : (a + 1) * rows, t * rows : (t + 1) * rows] = weights.astype(BF16)
            weighted = weights * here
            inner_row = inner_row + weighted
            inner_col[t] = inner_col[t] + jnp.sum(weighted, axis=0, keepdims=True)
        inner = jnp.sum(inner_row, axis=1, keepdims=True)
        img_parts[a][...] = (
            dot(weights_bf[a * rows : (a + 1) * rows], txt_low[...])
            - inner * img_low[a * rows : (a + 1) * rows]
        )
    for t in range(nt):
        here = slice(t * rows, (t + 1) * rows)
        txt_parts[t][...] = dot(img_side_t[...], weights_bf[:, here]) - inner_col[t] * txt_side_t[:, here]


def sketch_kernel(ni, nt, *refs):
    img_parts, txt_parts = refs[:ni], refs[ni : ni + nt]
    img_base, txt_base, img_keys, txt_keys, img_out, txt_out = refs[ni + nt :]
    img_grad = sum((p[...] for p in img_parts), img_base[...])
    txt_grad = sum((p[...] for p in txt_parts[1:]), txt_parts[0][...]).T + txt_base[...]
    for keys, grad, out in ((img_keys, img_grad, img_out), (txt_keys, txt_grad, txt_out)):
        width = grad.shape[1]
        for a in range(keys.shape[1]):
            out[:, a * width : (a + 1) * width] = (keys[:, a : a + 1] * grad).astype(BF16)


def body(n, img_feats, txt_feats, w_img, w_txt, a_img, b_img, a_txt, b_txt):
    rows, wide = img_feats.shape[0], w_img.shape[1]
    low = b_img.shape[1]
    assert rows == LANES and low == LANES
    img_bits, txt_bits = split_bits(n)
    img_span, txt_span = span(img_bits), span(txt_bits)
    ni, nt = len(img_span), len(txt_span)
    feats = gather(txt_feats, txt_bits, n)
    img_emb, img_keys = embed(img_feats, w_img, a_img)
    images = gather(img_emb, img_bits, n)
    txt_emb, txt_keys = embed(txt_feats, w_txt, a_txt)
    texts = [txt_emb] + [embed(f, w_txt)[0] for f in feats[1:]]
    raw, row_lse, col_lse = call(
        functools.partial(scores_kernel, ni, nt),
        [((ni * rows, nt * rows), F32), ((ni, rows), F32), ((nt, rows), F32)],
        images + texts,
        scratch=[pltpu.VMEM((ni * rows, wide), BF16), pltpu.VMEM((nt * rows, wide), BF16)],
        flops=2 * ni * nt * rows * rows * wide,
    )
    row_parts = [row_lse] + [swap(row_lse, o, n) for o in img_span[1:]]
    col_parts = [col_lse] + [swap(col_lse, o, n) for o in txt_span[1:]]
    img_low, img_side_t, txt_low, txt_side_t, img_base, txt_base = call(
        functools.partial(factors_kernel, ni, nt),
        [
            ((ni * rows, low), F32),
            ((low, ni * rows), BF16),
            ((nt * rows, low), BF16),
            ((low, nt * rows), F32),
            ((rows, low), F32),
            ((rows, low), F32),
        ],
        images + texts + [b_img, b_txt],
        flops=4 * (ni + nt) * rows * wide * low,
    )
    parts = call(
        functools.partial(weights_kernel, ni, nt),
        [((rows, low), F32)] * (ni + nt),
        row_parts + col_parts + [raw, img_low, img_side_t, txt_low, txt_side_t],
        scratch=[pltpu.VMEM((ni * rows, nt * rows), BF16)],
        flops=4 * ni * nt * rows * rows * low,
    )
    img_parts, txt_parts = parts[:ni], parts[ni:]
    img_parts = [img_parts[0]] + [swap(p, o, n) for p, o in zip(img_parts[1:], img_span[1:])]
    txt_parts = [txt_parts[0]] + [swap(p, o, n) for p, o in zip(txt_parts[1:], txt_span[1:])]
    return tuple(
        call(
            functools.partial(sketch_kernel, ni, nt),
            [((rows, img_keys.shape[1] * low), BF16), ((rows, txt_keys.shape[1] * low), BF16)],
            img_parts + txt_parts + [img_base, txt_base, img_keys, txt_keys],
        )
    )


def solution(mesh):
    n = mesh.shape["dp"]
    rows = P(("ckpt", "dp"), None)
    part = P("ckpt", None)
    return jax.shard_map(
        lambda *args: body(n, *args),
        mesh=mesh,
        in_specs=(rows, rows, part, part, P(), P(), P(), P()),
        out_specs=(rows, rows),
        check_vma=False,
    )
```

time: 73.5 us -> 65 us (0.88)
  Pallas kernels: 0 us -> 17.5 us
  matrix products: 13.8 us -> 0 us
  other arithmetic: 10.2 us -> 0 us
  waiting for transfers between devices: 25.2 us -> 16.1 us
  starting transfers between devices: 14.3 us -> 22.3 us
    pallas_call x0 -> x9, Pallas kernels: none -> 17.5 us  [call(): pl.pallas_call(kernel, out_shape=[jax.ShapeDtypeStruct(s, d) for s, d in...]
    dot_general x11 -> x0, matrix products: 13.8 us -> none  [the longest x2 4.05 us: embed(): raw = jnp.dot(feats, weight, preferred_element_type=jnp.float32)]
    ppermute x14 -> x18, waiting for transfers between devices: 25.2 us -> 16.1 us  [swap(): return lax.ppermute(x, 'dp', [(i, i ^ offset) for i in range(n)])]
    ppermute x14 -> x18, starting transfers between devices: 14.3 us -> 22.3 us  [swap(): return lax.ppermute(x, 'dp', [(i, i ^ offset) for i in range(n)])]
    rev x4 -> x0, local copies, waits for them, and re-layouts: 5.04 us -> none  [merge_lse(): lse = jnp.logaddexp(lse, cut[:, ::-1].reshape(lse.shape))]
    unnamed x44 -> x18, local copies, waits for them, and re-layouts: 3.5 us -> 7.97 us
    select_n x4 -> x0, other arithmetic: 4.02 us -> none  [merge_lse(): lse = jnp.logaddexp(lse, cut[:, ::-1].reshape(lse.shape))]
    reduce_sum x4 -> x0, other arithmetic: 3.12 us -> none  [the longest x1 1.77 us: body(): jnp.sum(weighted, axis=0)[:, None] * txt_side]
  transfers between devices with their start and end apart: 14 -> 18, of which waited for: 7 -> 3; matrix products, arithmetic and copies ran while one was open for 19% -> 4% of each run, Pallas kernels for 0% -> 18%
where the time goes in v2:
time: 65 us; the launch traced here: 64.5 us
  starting transfers between devices  22.3 us (34%)
  Pallas kernels  17.5 us (27%)
  waiting for transfers between devices  16.1 us (25%)
  local copies, waits for them, and re-layouts  7.97 us (12%)
  between operations  0.78 us (1%)
    ppermute x18, starting transfers between devices, swap(): return lax.ppermute(x, 'dp', [(i, i ^ offset) for i in range(n)])  22.3 us
    pallas_call x9, Pallas kernels, call(): pl.pallas_call(kernel, out_shape=[jax.ShapeDtypeStruct(s, d) for s, d in...  17.5 us
    ppermute x18, waiting for transfers between devices, swap(): return lax.ppermute(x, 'dp', [(i, i ^ offset) for i in range(n)])  16.1 us
    unnamed x18, local copies, waits for them, and re-layouts  7.97 us
  transfers between devices with their start and end apart: 18, of which 3 were waited for; matrix products, arithmetic and copies ran while one was open for 4% of the time, Pallas kernels for 18%

profile of v2, /device:TPU:0, one launch (start us, length us, event | category | flops | bytes accessed | tf_op | source)
XLA Modules:
  0.0 64.5 jit_solution(12703196103834662092)
XLA Ops:
  0.6 0.0 copy-start
  0.6 3.1 %collective-permute-start.3 = (bf16[128,1280]{1,0:T(8,128)(2,1)}, bf16[128,1280]{1,0:T(8,128)(2,1)}, u32[]{:S(2)}, u32[]{:S(2)}) collective-permute-start(bf16[128,1280]{1,0:T(8,128)(2,1)} %feats.3), channel_id=1, source_target_pairs={{0,4},{1,5},{2,6},{3,7},{4,0},{5,1},{6,2},{7,3},{8,12},{9,13},{10,... | collective-permute-start | bytes 983048 | tf_op jit(solution)/shard_map/ppermute | solution.py:51
  3.7 1.9 %copy.10.rest_0_ = bf16[1664,32]{1,0:T(8,128)(2,1)} copy(bf16[1664,32]{0,1:T(8,128)(2,1)} %param.12) | data formatting | bytes 212992 | tf_op args[4]
  5.6 0.0 copy-start.1
  5.6 2.2 %copy-done.1 = bf16[1664,1280]{1,0:T(8,128)(2,1)S(1)} copy-done((bf16[1664,1280]{1,0:T(8,128)(2,1)S(1)}, bf16[1664,1280]{1,0:T(8,128)(2,1)}, u32[]{:S(2)}) %copy-start.1) | copy-done | bytes 4259864
  7.8 0.0 copy-start.2
  7.8 1.0 %copy-done.2 = bf16[1664,32]{1,0:T(8,128)(2,1)S(1)} copy-done((bf16[1664,32]{1,0:T(8,128)(2,1)S(1)}, bf16[1664,32]{1,0:T(8,128)(2,1)}, u32[]{:S(2)}) %copy-start.2) | copy-done | bytes 106520
  8.8 0.0 copy-start.4
  8.8 1.0 %copy-done.4 = bf16[128,1664]{1,0:T(8,128)(2,1)S(1)} copy-done((bf16[128,1664]{1,0:T(8,128)(2,1)S(1)}, bf16[128,1664]{1,0:T(8,128)(2,1)}, u32[]{:S(2)}) %copy-start.4) | copy-done | bytes 426008
  9.8 0.0 copy-start.7
  9.8 1.7 %shard_map.95 = (bf16[128,1280]{1,0:T(8,128)(2,1)}, f32[128,32]{1,0:T(8,128)S(1)}) custom-call(bf16[128,1664]{1,0:T(8,128)(2,1)S(1)} %copy-done.4, bf16[1664,1280]{1,0:T(8,128)(2,1)S(1)} %copy-done.1, bf16[1664,32]{1,0:T(8,128)(2,1)S(1)} %copy-done.2), custom_call_target="tpu_custom_call" | custom-call | flops 545259520 | bytes 4792320 | tf_op jit(solution)/shard_map/pallas_call | solution.py:25
  11.5 2.6 %collective-permute-start = (bf16[128,1280]{1,0:T(8,128)(2,1)}, bf16[128,1280]{1,0:T(8,128)(2,1)}, u32[]{:S(2)}, u32[]{:S(2)}) collective-permute-start(bf16[128,1280]{1,0:T(8,128)(2,1)} %get-tuple-element.23.refs_0_), channel_id=1, source_target_pairs={{0,8},{1,9},{2,10},{3,11},{4,12},{5,13},{6,14},{7,15},{8,0},{9,1},... | collective-permute-start | bytes 983048 | tf_op jit(solution)/shard_map/ppermute | solution.py:51
  14.1 1.5 %collective-permute-start.4 = (bf16[128,1280]{1,0:T(8,128)(2,1)}, bf16[128,1280]{1,0:T(8,128)(2,1)}, u32[]{:S(2)}, u32[]{:S(2)}) collective-permute-start(bf16[128,1280]{1,0:T(8,128)(2,1)} %feats.3), channel_id=1, source_target_pairs={{0,2},{1,3},{2,0},{3,1},{4,6},{5,7},{6,4},{7,5},{8,10},{9,11},{10,... | collective-permute-start | bytes 983048 | tf_op jit(solution)/shard_map/ppermute | solution.py:51
  15.6 0.0 collective-permute-done.3.feats
  15.6 0.5 collective-permute-start.5
  16.1 0.0 collective-permute-start.1
  16.1 12.8 %collective-permute-done.refs_1_ = bf16[128,1280]{1,0:T(8,128)(2,1)} collective-permute-done((bf16[128,1280]{1,0:T(8,128)(2,1)}, bf16[128,1280]{1,0:T(8,128)(2,1)}, u32[]{:S(2)}, u32[]{:S(2)}) %collective-permute-start) | collective-permute-done | bytes 327712 | tf_op jit(solution)/shard_map/ppermute | solution.py:51
  28.9 0.0 collective-permute-start.2
  28.9 0.0 copy-done.7
  28.9 0.9 %copy.11.rest_0_ = bf16[1280,32]{1,0:T(8,128)(2,1)} copy(bf16[1280,32]{0,1:T(8,128)(2,1)S(1)} %copy-done.7) | data formatting | bytes 163840 | tf_op args[6]
  29.8 0.0 copy-done
  29.8 0.0 copy-start.3
  29.8 1.0 %copy-done.3 = bf16[1280,32]{1,0:T(8,128)(2,1)S(1)} copy-done((bf16[1280,32]{1,0:T(8,128)(2,1)S(1)}, bf16[1280,32]{1,0:T(8,128)(2,1)}, u32[]{:S(2)}) %copy-start.3) | copy-done | bytes 81944
  30.8 1.7 %shard_map.96 = (bf16[128,1280]{1,0:T(8,128)(2,1)S(1)}, f32[128,32]{1,0:T(8,128)S(1)}) custom-call(bf16[128,1280]{1,0:T(8,128)(2,1)} %feats.3, bf16[1280,1280]{1,0:T(8,128)(2,1)S(1)} %copy-done, bf16[1280,32]{1,0:T(8,128)(2,1)S(1)} %copy-done.3), custom_call_target="tpu_custom_call" | custom-call | flops 419430400 | bytes 3686400 | tf_op jit(solution)/shard_map/pallas_call | solution.py:25
  32.6 1.7 %shard_map.97.refs_5_ = bf16[128,1280]{1,0:T(8,128)(2,1)S(1)} custom-call(bf16[128,1280]{1,0:T(8,128)(2,1)} %collective-permute-done.3.feats, bf16[1280,1280]{1,0:T(8,128)(2,1)S(1)} %copy-done), custom_call_target="tpu_custom_call" | custom-call | flops 419430400 | bytes 3604480 | tf_op jit(solution)/shard_map/pallas_call | solution.py:25
  34.2 0.0 collective-permute-done.4.feats
  34.3 1.7 %shard_map.98.refs_6_ = bf16[128,1280]{1,0:T(8,128)(2,1)S(1)} custom-call(bf16[128,1280]{1,0:T(8,128)(2,1)} %collective-permute-done.4.feats, bf16[1280,1280]{1,0:T(8,128)(2,1)S(1)} %copy-done), custom_call_target="tpu_custom_call" | custom-call | flops 419430400 | bytes 3604480 | tf_op jit(solution)/shard_map/pallas_call | solution.py:25
  35.9 0.0 copy-start.5
  36.0 0.0 copy-start.6
  36.0 0.0 collective-permute-done.5.feats
  36.0 1.7 %shard_map.99.refs_7_ = bf16[128,1280]{1,0:T(8,128)(2,1)S(1)} custom-call(bf16[128,1280]{1,0:T(8,128)(2,1)} %collective-permute-done.5.feats, bf16[1280,1280]{1,0:T(8,128)(2,1)S(1)} %copy-done), custom_call_target="tpu_custom_call" | custom-call | flops 419430400 | bytes 3604480 | tf_op jit(solution)/shard_map/pallas_call | solution.py:25
  37.7 0.0 collective-permute-done.1.refs_2_
  37.7 0.0 collective-permute-done.2.refs_3_
  37.7 2.7 %shard_map.100 = (f32[512,512]{1,0:T(8,128)S(1)}, f32[4,128]{1,0:T(4,128)S(1)}, f32[4,128]{1,0:T(4,128)S(1)}) custom-call(bf16[128,1280]{1,0:T(8,128)(2,1)} %get-tuple-element.23.refs_0_, bf16[128,1280]{1,0:T(8,128)(2,1)} %collective-permute-done.refs_1_, bf16[128,1280]{1,0:T(8,128)(2,1)} %collective-permute-done.1.refs_2_, ...), custom_call_target="tpu_custom_call" | custom-call | flops 671088640 | bytes 2621440 | tf_op jit(solution)/shard_map/pallas_call | solution.py:25
  40.4 0.0 collective-permute-start.8
  40.5 0.6 collective-permute-start.7
  41.0 2.5 %collective-permute-start.6 = (f32[4,128]{1,0:T(4,128)S(1)}, f32[4,128]{1,0:T(4,128)S(1)}, u32[]{:S(2)}, u32[]{:S(2)}) collective-permute-start(f32[4,128]{1,0:T(4,128)S(1)} %get-tuple-element.25.refs_0_), channel_id=1, source_target_pairs={{0,8},{1,9},{2,10},{3,11},{4,12},{5,13},{6,14},{7,15},{8,0},{9,1},... | collective-permute-start | bytes 6152 | tf_op jit(solution)/shard_map/ppermute | solution.py:51
  43.5 1.7 %collective-permute-start.11 = (f32[4,128]{1,0:T(4,128)S(1)}, f32[4,128]{1,0:T(4,128)S(1)}, u32[]{:S(2)}, u32[]{:S(2)}) collective-permute-start(f32[4,128]{1,0:T(4,128)S(1)} %get-tuple-element.26.refs_4_), channel_id=1, source_target_pairs={{0,6},{1,7},{2,4},{3,5},{4,2},{5,3},{6,0},{7,1},{8,14},{9,15},{10,... | collective-permute-start | bytes 6152 | tf_op jit(solution)/shard_map/ppermute | solution.py:51
  45.2 0.5 collective-permute-start.10
  45.7 0.0 collective-permute-done.8.refs_3_
  45.7 1.3 %collective-permute-start.9 = (f32[4,128]{1,0:T(4,128)S(1)}, f32[4,128]{1,0:T(4,128)S(1)}, u32[]{:S(2)}, u32[]{:S(2)}) collective-permute-start(f32[4,128]{1,0:T(4,128)S(1)} %get-tuple-element.26.refs_4_), channel_id=1, source_target_pairs={{0,4},{1,5},{2,6},{3,7},{4,0},{5,1},{6,2},{7,3},{8,12},{9,13},{10,... | collective-permute-start | bytes 6152 | tf_op jit(solution)/shard_map/ppermute | solution.py:51
  47.0 0.0 copy-done.5
  47.0 0.0 copy-done.6
  47.0 2.9 %shard_map.101 = (f32[512,128]{1,0:T(8,128)S(1)}, bf16[128,512]{1,0:T(8,128)(2,1)S(1)}, bf16[512,128]{1,0:T(8,128)(2,1)S(1)}, f32[128,512]{1,0:T(8,128)S(1)}, f3...) custom-call(bf16[128,1280]{1,0:T(8,128)(2,1)} %get-tuple-element.23.refs_0_, ...), custom_call_target="tpu_custom_call" | custom-call | flops 671088640 | bytes 3276800 | tf_op jit(solution)/shard_map/pallas_call | solution.py:25
  49.9 0.0 collective-permute-done.7.refs_2_
  49.9 0.0 collective-permute-done.6.refs_1_
  49.9 0.0 collective-permute-done.11.refs_7_
  49.9 0.0 collective-permute-done.10.refs_6_
  49.9 0.0 collective-permute-done.9.refs_5_
  49.9 0.9 %shard_map.102 = (f32[128,128]{1,0:T(8,128)S(1)}, f32[128,128]{1,0:T(8,128)S(1)}, f32[128,128]{1,0:T(8,128)S(1)}, f32[128,128]{1,0:T(8,128)S(1)}, f32[128,128]{1...) custom-call(f32[4,128]{1,0:T(4,128)S(1)} %get-tuple-element.25.refs_0_, ...), custom_call_target="tpu_custom_call" | custom-call | flops 134217728 | bytes 1851392 | tf_op jit(solution)/shard_map/pallas_call | solution.py:25
  50.8 1.9 %collective-permute-start.12 = (f32[128,128]{1,0:T(8,128)S(1)}, f32[128,128]{1,0:T(8,128)S(1)}, u32[]{:S(2)}, u32[]{:S(2)}) collective-permute-start(f32[128,128]{1,0:T(8,128)S(1)} %get-tuple-element.33), channel_id=1, source_target_pairs={{0,8},{1,9},{2,10},{3,11},{4,12},{5,13},{6,14},{7,15},{8,0},{9,1},... | collective-permute-start | bytes 196616 | tf_op jit(solution)/shard_map/ppermute | solution.py:51
  52.7 0.0 collective-permute-start.13
  52.7 1.2 %collective-permute-start.14 = (f32[128,128]{1,0:T(8,128)S(1)}, f32[128,128]{1,0:T(8,128)S(1)}, u32[]{:S(2)}, u32[]{:S(2)}) collective-permute-start(f32[128,128]{1,0:T(8,128)S(1)} %get-tuple-element.35), channel_id=1, source_target_pairs={{0,9},{1,8},{2,11},{3,10},{4,13},{5,12},{6,15},{7,14},{8,1},{9,0},... | collective-permute-start | bytes 196616 | tf_op jit(solution)/shard_map/ppermute | solution.py:51
  53.9 0.7 %collective-permute-start.15 = (f32[128,128]{1,0:T(8,128)S(1)}, f32[128,128]{1,0:T(8,128)S(1)}, u32[]{:S(2)}, u32[]{:S(2)}) collective-permute-start(f32[128,128]{1,0:T(8,128)S(1)} %get-tuple-element.37), channel_id=1, source_target_pairs={{0,4},{1,5},{2,6},{3,7},{4,0},{5,1},{6,2},{7,3},{8,12},{9,13},{10,... | collective-permute-start | bytes 196616 | tf_op jit(solution)/shard_map/ppermute | solution.py:51
  54.6 1.5 %collective-permute-start.16 = (f32[128,128]{1,0:T(8,128)S(1)}, f32[128,128]{1,0:T(8,128)S(1)}, u32[]{:S(2)}, u32[]{:S(2)}) collective-permute-start(f32[128,128]{1,0:T(8,128)S(1)} %get-tuple-element.38), channel_id=1, source_target_pairs={{0,2},{1,3},{2,0},{3,1},{4,6},{5,7},{6,4},{7,5},{8,10},{9,11},{10,... | collective-permute-start | bytes 196616 | tf_op jit(solution)/shard_map/ppermute | solution.py:51
  56.2 0.7 %collective-permute-done.12.refs_1_ = f32[128,128]{1,0:T(8,128)S(1)} collective-permute-done((f32[128,128]{1,0:T(8,128)S(1)}, f32[128,128]{1,0:T(8,128)S(1)}, u32[]{:S(2)}, u32[]{:S(2)}) %collective-permute-start.12) | collective-permute-done | bytes 65568 | tf_op jit(solution)/shard_map/ppermute | solution.py:51
  56.9 2.6 %collective-permute-start.17 = (f32[128,128]{1,0:T(8,128)S(1)}, f32[128,128]{1,0:T(8,128)S(1)}, u32[]{:S(2)}, u32[]{:S(2)}) collective-permute-start(f32[128,128]{1,0:T(8,128)S(1)} %get-tuple-element.39), channel_id=1, source_target_pairs={{0,6},{1,7},{2,4},{3,5},{4,2},{5,3},{6,0},{7,1},{8,14},{9,15},{10,... | collective-permute-start | bytes 196616 | tf_op jit(solution)/shard_map/ppermute | solution.py:51
  59.5 0.0 collective-permute-done.13.refs_2_
  59.5 0.0 collective-permute-done.14.refs_3_
  59.5 0.0 collective-permute-done.15.refs_5_
  59.5 0.0 collective-permute-done.16.refs_6_
  59.5 2.5 %collective-permute-done.17.refs_7_ = f32[128,128]{1,0:T(8,128)S(1)} collective-permute-done((f32[128,128]{1,0:T(8,128)S(1)}, f32[128,128]{1,0:T(8,128)S(1)}, u32[]{:S(2)}, u32[]{:S(2)}) %collective-permute-start.17) | collective-permute-done | bytes 65568 | tf_op jit(solution)/shard_map/ppermute | solution.py:51
  62.1 2.5 %shard_map.103 = (bf16[128,4096]{1,0:T(8,128)(2,1)}, bf16[128,4096]{1,0:T(8,128)(2,1)}) custom-call(f32[128,128]{1,0:T(8,128)S(1)} %get-tuple-element.32.refs_0_, f32[128,128]{1,0:T(8,128)S(1)} %collective-permute-done.12.refs_1_, f32[128,128]{1,0:T(8,128)S(1)} %collective-permute-done.13.refs_2_, f32[128,128]{1,0:T(8,128)S(1)} %collective-permute-done.14.refs_3_, ...), custom_call_target="tpu_custom_call" | custom-call | bytes 688128 | tf_op jit(solution)/shard_map/pallas_call | solution.py:25
Async XLA Ops:
  0.6 29.2 %copy-start = (bf16[1280,1280]{1,0:T(8,128)(2,1)S(1)}, bf16[1280,1280]{1,0:T(8,128)(2,1)}, u32[]{:S(2)}) copy-start(bf16[1280,1280]{1,0:T(8,128)(2,1)} %weight.9) | copy-start | bytes 9830404
  0.6 15.0 %collective-permute-start.3 = (bf16[128,1280]{1,0:T(8,128)(2,1)}, bf16[128,1280]{1,0:T(8,128)(2,1)}, u32[]{:S(2)}, u32[]{:S(2)}) collective-permute-start(bf16[128,1280]{1,0:T(8,128)(2,1)} %feats.3), channel_id=1, source_target_pairs={{0,4},{1,5},{2,6},{3,7},{4,0},{5,1},{6,2},{7,3},{8,12},{9,13},{10,... | collective-permute-start | bytes 983048 | tf_op jit(solution)/shard_map/ppermute | solution.py:51
  5.6 2.2 %copy-start.1 = (bf16[1664,1280]{1,0:T(8,128)(2,1)S(1)}, bf16[1664,1280]{1,0:T(8,128)(2,1)}, u32[]{:S(2)}) copy-start(bf16[1664,1280]{1,0:T(8,128)(2,1)} %weight.5) | copy-start | bytes 12779524
  7.8 1.0 %copy-start.2 = (bf16[1664,32]{1,0:T(8,128)(2,1)S(1)}, bf16[1664,32]{1,0:T(8,128)(2,1)}, u32[]{:S(2)}) copy-start(bf16[1664,32]{1,0:T(8,128)(2,1)} %copy.10.rest_0_) | copy-start | bytes 319492
  8.8 1.0 %copy-start.4 = (bf16[128,1664]{1,0:T(8,128)(2,1)S(1)}, bf16[128,1664]{1,0:T(8,128)(2,1)}, u32[]{:S(2)}) copy-start(bf16[128,1664]{1,0:T(8,128)(2,1)} %feats.2) | copy-start | bytes 1277956
  9.8 19.1 %copy-start.7 = (bf16[1280,32]{0,1:T(8,128)(2,1)S(1)}, bf16[1280,32]{0,1:T(8,128)(2,1)}, u32[]{:S(2)}) copy-start(bf16[1280,32]{0,1:T(8,128)(2,1)} %param.14) | copy-start | bytes 245764
  11.5 17.4 %collective-permute-start = (bf16[128,1280]{1,0:T(8,128)(2,1)}, bf16[128,1280]{1,0:T(8,128)(2,1)}, u32[]{:S(2)}, u32[]{:S(2)}) collective-permute-start(bf16[128,1280]{1,0:T(8,128)(2,1)} %get-tuple-element.23.refs_0_), channel_id=1, source_target_pairs={{0,8},{1,9},{2,10},{3,11},{4,12},{5,13},{6,14},{7,15},{8,0},{9,1},... | collective-permute-start | bytes 983048 | tf_op jit(solution)/shard_map/ppermute | solution.py:51
  14.1 20.1 %collective-permute-start.4 = (bf16[128,1280]{1,0:T(8,128)(2,1)}, bf16[128,1280]{1,0:T(8,128)(2,1)}, u32[]{:S(2)}, u32[]{:S(2)}) collective-permute-start(bf16[128,1280]{1,0:T(8,128)(2,1)} %feats.3), channel_id=1, source_target_pairs={{0,2},{1,3},{2,0},{3,1},{4,6},{5,7},{6,4},{7,5},{8,10},{9,11},{10,... | collective-permute-start | bytes 983048 | tf_op jit(solution)/shard_map/ppermute | solution.py:51
  15.6 20.3 %collective-permute-start.5 = (bf16[128,1280]{1,0:T(8,128)(2,1)}, bf16[128,1280]{1,0:T(8,128)(2,1)}, u32[]{:S(2)}, u32[]{:S(2)}) collective-permute-start(bf16[128,1280]{1,0:T(8,128)(2,1)} %collective-permute-done.3.feats), channel_id=1, source_target_pairs={{0,2},{1,3},{2,0},{3,1},{4,6},{5,7},{6,4},{7,5},{8,10},{9,11},{10,... | collective-permute-start | bytes 983048 | tf_op jit(solution)/shard_map/ppermute | solution.py:51
  16.1 21.6 %collective-permute-start.1 = (bf16[128,1280]{1,0:T(8,128)(2,1)}, bf16[128,1280]{1,0:T(8,128)(2,1)}, u32[]{:S(2)}, u32[]{:S(2)}) collective-permute-start(bf16[128,1280]{1,0:T(8,128)(2,1)} %get-tuple-element.23.refs_0_), channel_id=1, source_target_pairs={{0,1},{1,0},{2,3},{3,2},{4,5},{5,4},{6,7},{7,6},{8,9},{9,8},{10,11... | collective-permute-start | bytes 983048 | tf_op jit(solution)/shard_map/ppermute | solution.py:51
  28.9 8.8 %collective-permute-start.2 = (bf16[128,1280]{1,0:T(8,128)(2,1)}, bf16[128,1280]{1,0:T(8,128)(2,1)}, u32[]{:S(2)}, u32[]{:S(2)}) collective-permute-start(bf16[128,1280]{1,0:T(8,128)(2,1)} %collective-permute-done.refs_1_), channel_id=1, source_target_pairs={{0,1},{1,0},{2,3},{3,2},{4,5},{5,4},{6,7},{7,6},{8,9},{9,8},{10,11... | collective-permute-start | bytes 983048 | tf_op jit(solution)/shard_map/ppermute | solution.py:51
  29.8 1.0 %copy-start.3 = (bf16[1280,32]{1,0:T(8,128)(2,1)S(1)}, bf16[1280,32]{1,0:T(8,128)(2,1)}, u32[]{:S(2)}) copy-start(bf16[1280,32]{1,0:T(8,128)(2,1)} %copy.11.rest_0_) | copy-start | bytes 245764
  35.9 11.1 %copy-start.5 = (bf16[1280,128]{1,0:T(8,128)(2,1)S(1)}, bf16[1280,128]{1,0:T(8,128)(2,1)}, u32[]{:S(2)}) copy-start(bf16[1280,128]{1,0:T(8,128)(2,1)} %refs_8_.1) | copy-start | bytes 983044
  36.0 11.0 %copy-start.6 = (bf16[1280,128]{1,0:T(8,128)(2,1)S(1)}, bf16[1280,128]{1,0:T(8,128)(2,1)}, u32[]{:S(2)}) copy-start(bf16[1280,128]{1,0:T(8,128)(2,1)} %refs_9_.1) | copy-start | bytes 983044
  40.4 5.3 %collective-permute-start.8 = (f32[4,128]{1,0:T(4,128)S(1)}, f32[4,128]{1,0:T(4,128)S(1)}, u32[]{:S(2)}, u32[]{:S(2)}) collective-permute-start(f32[4,128]{1,0:T(4,128)S(1)} %get-tuple-element.25.refs_0_), channel_id=1, source_target_pairs={{0,9},{1,8},{2,11},{3,10},{4,13},{5,12},{6,15},{7,14},{8,1},{9,0},... | collective-permute-start | bytes 6152 | tf_op jit(solution)/shard_map/ppermute | solution.py:51
  40.5 9.4 %collective-permute-start.7 = (f32[4,128]{1,0:T(4,128)S(1)}, f32[4,128]{1,0:T(4,128)S(1)}, u32[]{:S(2)}, u32[]{:S(2)}) collective-permute-start(f32[4,128]{1,0:T(4,128)S(1)} %get-tuple-element.25.refs_0_), channel_id=1, source_target_pairs={{0,1},{1,0},{2,3},{3,2},{4,5},{5,4},{6,7},{7,6},{8,9},{9,8},{10,11... | collective-permute-start | bytes 6152 | tf_op jit(solution)/shard_map/ppermute | solution.py:51
  41.0 8.9 %collective-permute-start.6 = (f32[4,128]{1,0:T(4,128)S(1)}, f32[4,128]{1,0:T(4,128)S(1)}, u32[]{:S(2)}, u32[]{:S(2)}) collective-permute-start(f32[4,128]{1,0:T(4,128)S(1)} %get-tuple-element.25.refs_0_), channel_id=1, source_target_pairs={{0,8},{1,9},{2,10},{3,11},{4,12},{5,13},{6,14},{7,15},{8,0},{9,1},... | collective-permute-start | bytes 6152 | tf_op jit(solution)/shard_map/ppermute | solution.py:51
  43.5 6.4 %collective-permute-start.11 = (f32[4,128]{1,0:T(4,128)S(1)}, f32[4,128]{1,0:T(4,128)S(1)}, u32[]{:S(2)}, u32[]{:S(2)}) collective-permute-start(f32[4,128]{1,0:T(4,128)S(1)} %get-tuple-element.26.refs_4_), channel_id=1, source_target_pairs={{0,6},{1,7},{2,4},{3,5},{4,2},{5,3},{6,0},{7,1},{8,14},{9,15},{10,... | collective-permute-start | bytes 6152 | tf_op jit(solution)/shard_map/ppermute | solution.py:51
  45.2 4.7 %collective-permute-start.10 = (f32[4,128]{1,0:T(4,128)S(1)}, f32[4,128]{1,0:T(4,128)S(1)}, u32[]{:S(2)}, u32[]{:S(2)}) collective-permute-start(f32[4,128]{1,0:T(4,128)S(1)} %get-tuple-element.26.refs_4_), channel_id=1, source_target_pairs={{0,2},{1,3},{2,0},{3,1},{4,6},{5,7},{6,4},{7,5},{8,10},{9,11},{10,... | collective-permute-start | bytes 6152 | tf_op jit(solution)/shard_map/ppermute | solution.py:51
  45.7 4.2 %collective-permute-start.9 = (f32[4,128]{1,0:T(4,128)S(1)}, f32[4,128]{1,0:T(4,128)S(1)}, u32[]{:S(2)}, u32[]{:S(2)}) collective-permute-start(f32[4,128]{1,0:T(4,128)S(1)} %get-tuple-element.26.refs_4_), channel_id=1, source_target_pairs={{0,4},{1,5},{2,6},{3,7},{4,0},{5,1},{6,2},{7,3},{8,12},{9,13},{10,... | collective-permute-start | bytes 6152 | tf_op jit(solution)/shard_map/ppermute | solution.py:51
  50.8 6.1 %collective-permute-start.12 = (f32[128,128]{1,0:T(8,128)S(1)}, f32[128,128]{1,0:T(8,128)S(1)}, u32[]{:S(2)}, u32[]{:S(2)}) collective-permute-start(f32[128,128]{1,0:T(8,128)S(1)} %get-tuple-element.33), channel_id=1, source_target_pairs={{0,8},{1,9},{2,10},{3,11},{4,12},{5,13},{6,14},{7,15},{8,0},{9,1},... | collective-permute-start | bytes 196616 | tf_op jit(solution)/shard_map/ppermute | solution.py:51
  52.7 6.8 %collective-permute-start.13 = (f32[128,128]{1,0:T(8,128)S(1)}, f32[128,128]{1,0:T(8,128)S(1)}, u32[]{:S(2)}, u32[]{:S(2)}) collective-permute-start(f32[128,128]{1,0:T(8,128)S(1)} %get-tuple-element.34), channel_id=1, source_target_pairs={{0,1},{1,0},{2,3},{3,2},{4,5},{5,4},{6,7},{7,6},{8,9},{9,8},{10,11... | collective-permute-start | bytes 196616 | tf_op jit(solution)/shard_map/ppermute | solution.py:51
  52.7 6.8 %collective-permute-start.14 = (f32[128,128]{1,0:T(8,128)S(1)}, f32[128,128]{1,0:T(8,128)S(1)}, u32[]{:S(2)}, u32[]{:S(2)}) collective-permute-start(f32[128,128]{1,0:T(8,128)S(1)} %get-tuple-element.35), channel_id=1, source_target_pairs={{0,9},{1,8},{2,11},{3,10},{4,13},{5,12},{6,15},{7,14},{8,1},{9,0},... | collective-permute-start | bytes 196616 | tf_op jit(solution)/shard_map/ppermute | solution.py:51
  53.9 5.6 %collective-permute-start.15 = (f32[128,128]{1,0:T(8,128)S(1)}, f32[128,128]{1,0:T(8,128)S(1)}, u32[]{:S(2)}, u32[]{:S(2)}) collective-permute-start(f32[128,128]{1,0:T(8,128)S(1)} %get-tuple-element.37), channel_id=1, source_target_pairs={{0,4},{1,5},{2,6},{3,7},{4,0},{5,1},{6,2},{7,3},{8,12},{9,13},{10,... | collective-permute-start | bytes 196616 | tf_op jit(solution)/shard_map/ppermute | solution.py:51
  54.6 4.9 %collective-permute-start.16 = (f32[128,128]{1,0:T(8,128)S(1)}, f32[128,128]{1,0:T(8,128)S(1)}, u32[]{:S(2)}, u32[]{:S(2)}) collective-permute-start(f32[128,128]{1,0:T(8,128)S(1)} %get-tuple-element.38), channel_id=1, source_target_pairs={{0,2},{1,3},{2,0},{3,1},{4,6},{5,7},{6,4},{7,5},{8,10},{9,11},{10,... | collective-permute-start | bytes 196616 | tf_op jit(solution)/shard_map/ppermute | solution.py:51
  56.9 5.2 %collective-permute-start.17 = (f32[128,128]{1,0:T(8,128)S(1)}, f32[128,128]{1,0:T(8,128)S(1)}, u32[]{:S(2)}, u32[]{:S(2)}) collective-permute-start(f32[128,128]{1,0:T(8,128)S(1)} %get-tuple-element.39), channel_id=1, source_target_pairs={{0,6},{1,7},{2,4},{3,5},{4,2},{5,3},{6,0},{7,1},{8,14},{9,15},{10,... | collective-permute-start | bytes 196616 | tf_op jit(solution)/shard_map/ppermute | solution.py:51

commit v3 on v2

--- a/solution.py
+++ b/solution.py
@@ -11,6 +11,7 @@
 F32 = jnp.float32
 BF16 = jnp.bfloat16
 LANES = 128
+PIECES = 4
 
 
 def dot(left, right, left_dim=1, right_dim=0):
@@ -19,13 +20,21 @@
     )
 
 
-def call(kernel, outs, args, scratch=(), flops=0, limit=32):
-    args = [pltpu.with_memory_space_constraint(a, pltpu.VMEM) for a in args]
+def skip(kernel, first, count, *refs):
+    kernel(*refs[:first], *refs[first + count :])
+
+
+def call(kernel, outs, args, after=(), free=(), scratch=(), flops=0, limit=16):
+    args = [a if k in free else pltpu.with_memory_space_constraint(a, pltpu.VMEM) for k, a in enumerate(args)]
     size = sum(a.size * a.dtype.itemsize for a in args)
+    specs = [pl.BlockSpec(memory_space=pltpu.VMEM)] * len(args)
+    if after:
+        kernel = functools.partial(skip, kernel, len(args), len(after))
+        args, specs = args + list(after), specs + [pl.BlockSpec(memory_space=pl.ANY)] * len(after)
     return pl.pallas_call(
         kernel,
         out_shape=[jax.ShapeDtypeStruct(s, d) for s, d in outs],
-        in_specs=[pl.BlockSpec(memory_space=pltpu.VMEM)] * len(args),
+        in_specs=specs,
         out_specs=[pl.BlockSpec(memory_space=pltpu.VMEM)] * len(outs),
         scratch_shapes=list(scratch),
         compiler_params=pltpu.CompilerParams(vmem_limit_bytes=limit << 20),
@@ -51,32 +60,98 @@
     return lax.ppermute(x, "dp", [(i, i ^ offset) for i in range(n)])
 
 
-def gather(block, bits, n):
-    blocks = [block]
+def gather(block, bits, n, ready=lambda x: x):
+    blocks, sent = [block], [block]
     for bit in bits:
-        blocks = blocks + [swap(b, bit, n) for b in blocks]
+        new = [swap(b, bit, n) for b in sent]
+        blocks, sent = blocks + new, sent + [ready(b) for b in new]
     return blocks
 
 
-def embed_kernel(feats, weight, *rest):
-    raw = dot(feats[...], weight[...])
+def normalised(raw):
     inverse = lax.rsqrt(jnp.sum(raw * raw, axis=1, keepdims=True) + EPSILON)
-    if len(rest) == 3:
-        factor, emb, keys = rest
-        keys[...] = dot(feats[...], factor[...]) * inverse
-    else:
-        (emb,) = rest
-    emb[...] = (raw * inverse).astype(BF16)
-
-
-def embed(feats, weight, factor=None):
-    rows, emb = feats.shape[0], weight.shape[1]
-    outs = [((rows, emb), BF16)]
-    args = [feats, weight]
-    if factor is not None:
-        outs.append(((rows, factor.shape[1]), F32))
-        args.append(factor)
-    return call(embed_kernel, outs, args, flops=2 * rows * weight.size)
+    return (raw * inverse).astype(BF16), inverse
+
+
+def embed_kernel(blocks, *refs):
+    feats, weight, embs = refs[:blocks], refs[blocks], refs[blocks + 1 :]
+    for b in range(blocks):
+        embs[b][...] = normalised(dot(feats[b][...], weight[...]))[0]
+
+
+def embed(feats, weight):
+    rows, blocks = feats[0].shape[0], len(feats)
+    return list(
+        call(
+            functools.partial(embed_kernel, blocks),
+            [((rows, weight.shape[1]), BF16)] * blocks,
+            [*feats, weight],
+            flops=2 * blocks * rows * weight.size,
+        )
+    )
+
+
+def stream_kernel(blocks, cuts, *refs):
+    feats, weight, embs = refs[:blocks], refs[blocks], refs[blocks + 1 : 2 * blocks + 1]
+    inverse, weight_v, own_v, sems = refs[2 * blocks + 1 :]
+    own = pltpu.make_async_copy(feats[0], own_v, sems.at[0])
+    pieces = [slice(lo, hi) for lo, hi in zip(cuts, cuts[1:])]
+    copies = [
+        pltpu.make_async_copy(weight.at[p], weight_v.at[p], sems.at[1 + k]) for k, p in enumerate(pieces)
+    ]
+    for copy in [own, *copies]:
+        copy.start()
+    own.wait()
+    raws = [0.0] * blocks
+    for p, copy in zip(pieces, copies):
+        copy.wait()
+        for b in range(blocks):
+            left = own_v[:, p] if b == 0 else feats[b][:, p]
+            raws[b] = raws[b] + dot(left, weight_v[p])
+    embs[0][...], inverse[...] = normalised(raws[0])
+    for b in range(1, blocks):
+        embs[b][...] = normalised(raws[b])[0]
+
+
+def stream_embed(feats, weight, keep):
+    (rows, depth), blocks = feats[0].shape, len(feats)
+    cuts = [depth // LANES * k // PIECES * LANES for k in range(PIECES)] + [depth]
+    far = [pltpu.with_memory_space_constraint(a, pltpu.HBM) for a in (feats[0], weight)]
+    near = [pltpu.with_memory_space_constraint(a, pltpu.VMEM) for a in feats[1:]]
+    hbm, vmem = pl.BlockSpec(memory_space=pltpu.HBM), pl.BlockSpec(memory_space=pltpu.VMEM)
+    outs = [((rows, weight.shape[1]), BF16)] * blocks + [((rows, 1), F32)] + [(weight.shape, BF16)] * keep
+    out = pl.pallas_call(
+        functools.partial(stream_kernel, blocks, cuts),
+        out_shape=[jax.ShapeDtypeStruct(*o) for o in outs],
+        in_specs=[hbm] + [vmem] * (blocks - 1) + [hbm],
+        out_specs=[vmem] * len(outs),
+        scratch_shapes=[pltpu.VMEM(weight.shape, BF16)] * (not keep)
+        + [pltpu.VMEM((rows, depth), BF16), pltpu.SemaphoreType.DMA((PIECES + 1,))],
+        compiler_params=pltpu.CompilerParams(vmem_limit_bytes=16 << 20),
+        cost_estimate=pl.CostEstimate(
+            flops=2 * blocks * rows * weight.size, bytes_accessed=2 * weight.size, transcendentals=0
+        ),
+    )(far[0], *near, far[1])
+    return list(out[:blocks]), *out[blocks:]
+
+
+def keys_kernel(*refs):
+    for feats, factor, inverse, wide in zip(refs[:2], refs[2:4], refs[4:6], refs[6:8]):
+        keys = dot(feats[...], factor[...], 1, 1) * inverse[...]
+        for a in range(keys.shape[1]):
+            wide[:, a * LANES : (a + 1) * LANES] = jnp.broadcast_to(keys[:, a : a + 1], (keys.shape[0], LANES))
+
+
+def hold(x, after):
+    args = [pltpu.with_memory_space_constraint(a, pltpu.VMEM) for a in [x, *after]]
+    return pl.pallas_call(
+        lambda *refs: None,
+        out_shape=jax.ShapeDtypeStruct(x.shape, x.dtype),
+        in_specs=[pl.BlockSpec(memory_space=pltpu.VMEM)] * len(args),
+        out_specs=pl.BlockSpec(memory_space=pltpu.VMEM),
+        input_output_aliases={0: 0},
+        compiler_params=pltpu.CompilerParams(vmem_limit_bytes=1 << 20),
+    )(*args)
 
 
 def column_of(row):
@@ -163,24 +238,44 @@
             inner_row = inner_row + weighted
             inner_col[t] = inner_col[t] + jnp.sum(weighted, axis=0, keepdims=True)
         inner = jnp.sum(inner_row, axis=1, keepdims=True)
-        img_parts[a][...] = (
+        part = (
             dot(weights_bf[a * rows : (a + 1) * rows], txt_low[...])
             - inner * img_low[a * rows : (a + 1) * rows]
         )
+        img_parts[a][...] = part.astype(img_parts[a].dtype)
     for t in range(nt):
         here = slice(t * rows, (t + 1) * rows)
-        txt_parts[t][...] = dot(img_side_t[...], weights_bf[:, here]) - inner_col[t] * txt_side_t[:, here]
-
-
-def sketch_kernel(ni, nt, *refs):
-    img_parts, txt_parts = refs[:ni], refs[ni : ni + nt]
-    img_base, txt_base, img_keys, txt_keys, img_out, txt_out = refs[ni + nt :]
-    img_grad = sum((p[...] for p in img_parts), img_base[...])
-    txt_grad = sum((p[...] for p in txt_parts[1:]), txt_parts[0][...]).T + txt_base[...]
-    for keys, grad, out in ((img_keys, img_grad, img_out), (txt_keys, txt_grad, txt_out)):
-        width = grad.shape[1]
-        for a in range(keys.shape[1]):
-            out[:, a * width : (a + 1) * width] = (keys[:, a : a + 1] * grad).astype(BF16)
+        part = dot(img_side_t[...], weights_bf[:, here]) - inner_col[t] * txt_side_t[:, here]
+        txt_parts[t][...] = part.astype(txt_parts[t].dtype)
+
+
+def sketch_kernel(count, turned, *refs):
+    parts, (base, keys, out, made, sems) = refs[:count], refs[count:]
+    rows = base.shape[0]
+    grad = sum((part[...].astype(F32) for part in parts[1:]), parts[0][...])
+    grad = (grad.T if turned else grad) + base[...]
+    copies, step = [], rows // 2
+    for k in range(2):
+        here = slice(k * step, (k + 1) * step)
+        for a in range(0, made.shape[1], LANES):
+            made[here, a : a + LANES] = (keys[here, a : a + LANES] * grad[here]).astype(BF16)
+        copies.append(pltpu.make_async_copy(made.at[here], out.at[here], sems.at[k]))
+        copies[-1].start()
+    for copy in copies:
+        copy.wait()
+
+
+def sketch(parts, base, keys, turned):
+    args = [pltpu.with_memory_space_constraint(a, pltpu.VMEM) for a in [*parts, base, keys]]
+    return pl.pallas_call(
+        functools.partial(sketch_kernel, len(parts), turned),
+        out_shape=jax.ShapeDtypeStruct(keys.shape, BF16),
+        in_specs=[pl.BlockSpec(memory_space=pltpu.VMEM)] * len(args),
+        out_specs=pl.BlockSpec(memory_space=pltpu.HBM),
+        scratch_shapes=[pltpu.VMEM(keys.shape, BF16), pltpu.SemaphoreType.DMA((2,))],
+        compiler_params=pltpu.CompilerParams(vmem_limit_bytes=16 << 20),
+        cost_estimate=pl.CostEstimate(flops=keys.size, bytes_accessed=6 * keys.size, transcendentals=0),
+    )(*args)
 
 
 def body(n, img_feats, txt_feats, w_img, w_txt, a_img, b_img, a_txt, b_txt):
@@ -190,11 +285,16 @@
     img_bits, txt_bits = split_bits(n)
     img_span, txt_span = span(img_bits), span(txt_bits)
     ni, nt = len(img_span), len(txt_span)
+    (img_emb,), img_inv = stream_embed([img_feats], w_img, False)
     feats = gather(txt_feats, txt_bits, n)
-    img_emb, img_keys = embed(img_feats, w_img, a_img)
-    images = gather(img_emb, img_bits, n)
-    txt_emb, txt_keys = embed(txt_feats, w_txt, a_txt)
-    texts = [txt_emb] + [embed(f, w_txt)[0] for f in feats[1:]]
+    texts, txt_inv, w_txt_v = stream_embed(feats[:-1], w_txt, True)
+    img_keys, txt_keys = call(
+        keys_kernel,
+        [((rows, a_img.shape[1] * LANES), F32), ((rows, a_txt.shape[1] * LANES), F32)],
+        [img_feats, txt_feats, a_img.T, a_txt.T, img_inv, txt_inv],
+    )
+    images = gather(img_emb, img_bits, n, lambda x: hold(x, [texts[0], img_keys]))
+    texts = texts + embed(feats[-1:], w_txt_v)
     raw, row_lse, col_lse = call(
         functools.partial(scores_kernel, ni, nt),
         [((ni * rows, nt * rows), F32), ((ni, rows), F32), ((nt, rows), F32)],
@@ -202,7 +302,7 @@
         scratch=[pltpu.VMEM((ni * rows, wide), BF16), pltpu.VMEM((nt * rows, wide), BF16)],
         flops=2 * ni * nt * rows * rows * wide,
     )
-    row_parts = [row_lse] + [swap(row_lse, o, n) for o in img_span[1:]]
+    row_parts = gather(row_lse, img_bits, n)
     col_parts = [col_lse] + [swap(col_lse, o, n) for o in txt_span[1:]]
     img_low, img_side_t, txt_low, txt_side_t, img_base, txt_base = call(
         functools.partial(factors_kernel, ni, nt),
@@ -219,20 +319,18 @@
     )
     parts = call(
         functools.partial(weights_kernel, ni, nt),
-        [((rows, low), F32)] * (ni + nt),
+        [((rows, low), F32 if k in (0, ni) else BF16) for k in range(ni + nt)],
         row_parts + col_parts + [raw, img_low, img_side_t, txt_low, txt_side_t],
         scratch=[pltpu.VMEM((ni * rows, nt * rows), BF16)],
         flops=4 * ni * nt * rows * rows * low,
     )
-    img_parts, txt_parts = parts[:ni], parts[ni:]
-    img_parts = [img_parts[0]] + [swap(p, o, n) for p, o in zip(img_parts[1:], img_span[1:])]
-    txt_parts = [txt_parts[0]] + [swap(p, o, n) for p, o in zip(txt_parts[1:], txt_span[1:])]
-    return tuple(
-        call(
-            functools.partial(sketch_kernel, ni, nt),
-            [((rows, img_keys.shape[1] * low), BF16), ((rows, txt_keys.shape[1] * low), BF16)],
-            img_parts + txt_parts + [img_base, txt_base, img_keys, txt_keys],
-        )
+    img_parts, txt_parts = [
+        [own] + [swap(p, o, n) for p, o in zip(sent, offsets[1:])]
+        for (own, *sent), offsets in ((parts[:ni], img_span), (parts[ni:], txt_span))
+    ]
+    return (
+        sketch(img_parts, img_base, img_keys, False),
+        sketch(txt_parts, txt_base, txt_keys, True),
     )
 
 

time: 65 us -> 48.5 us (0.75)
  local copies, waits for them, and re-layouts: 7.97 us -> 0.06 us
  waiting for transfers between devices: 16.1 us -> 11.7 us
  Pallas kernels: 17.5 us -> 15.4 us
  starting transfers between devices: 22.3 us -> 20.4 us
    pallas_call x9 -> x5, Pallas kernels: 17.5 us -> 6.76 us  [call(): pl.pallas_call(kernel, out_shape=[jax.ShapeDtypeStruct(s, d) for s, d in...]
    pallas_call x0 -> x5, Pallas kernels: none -> 8.62 us  [the longest x2 6.37 us: stream_embed(): pl.pallas_call(functools.partial(stream_kernel, blocks, cuts), out_shape=...]
    unnamed x18 -> x13, local copies, waits for them, and re-layouts: 7.97 us -> 0.06 us
    ppermute x18, waiting for transfers between devices: 16.1 us -> 11.7 us  [swap(): return lax.ppermute(x, 'dp', [(i, i ^ offset) for i in range(n)])]
    ppermute x18, starting transfers between devices: 22.3 us -> 20.4 us  [swap(): return lax.ppermute(x, 'dp', [(i, i ^ offset) for i in range(n)])]
  transfers between devices with their start and end apart: 18 -> 18, of which waited for: 3 -> 7; matrix products, arithmetic and copies ran while one was open for 4% -> 0% of each run, Pallas kernels for 18% -> 25%
where the time goes in v3:
time: 48.5 us; the launch traced here: 48.4 us
  starting transfers between devices  20.4 us (42%)
  Pallas kernels  15.4 us (32%)
  waiting for transfers between devices  11.7 us (24%)
  between operations  0.84 us (2%)
    ppermute x18, starting transfers between devices, swap(): return lax.ppermute(x, 'dp', [(i, i ^ offset) for i in range(n)])  20.4 us
    ppermute x18, waiting for transfers between devices, swap(): return lax.ppermute(x, 'dp', [(i, i ^ offset) for i in range(n)])  11.7 us
    pallas_call x5, Pallas kernels, call(): pl.pallas_call(kernel, out_shape=[jax.ShapeDtypeStruct(s, d) for s, d in...  6.76 us
    pallas_call x2, Pallas kernels, stream_embed(): pl.pallas_call(functools.partial(stream_kernel, blocks, cuts), out_shape=...  6.37 us
    pallas_call x2, Pallas kernels, sketch(): pl.pallas_call(functools.partial(sketch_kernel, len(parts), turned), out_...  2.24 us
  transfers between devices with their start and end apart: 18, of which 7 were waited for; matrix products, arithmetic and copies ran while one was open for 0% of the time, Pallas kernels for 25%

profile of v3, /device:TPU:0, one launch (start us, length us, event | category | flops | bytes accessed | tf_op | source)
XLA Modules:
  0.0 48.4 jit_solution(17504119252628420915)
XLA Ops:
  0.6 3.1 %collective-permute-start.2 = (bf16[128,1280]{1,0:T(8,128)(2,1)}, bf16[128,1280]{1,0:T(8,128)(2,1)S(1)}, u32[]{:S(2)}, u32[]{:S(2)}) collective-permute-start(bf16[128,1280]{1,0:T(8,128)(2,1)} %refs_1_.3), channel_id=1, source_target_pairs={{0,4},{1,5},{2,6},{3,7},{4,0},{5,1},{6,2},{7,3},{8,12},{9,13},{10,... | collective-permute-start | bytes 983048 | tf_op jit(solution)/shard_map/ppermute | solution.py:60
  3.7 1.5 %collective-permute-start.3 = (bf16[128,1280]{1,0:T(8,128)(2,1)}, bf16[128,1280]{1,0:T(8,128)(2,1)S(1)}, u32[]{:S(2)}, u32[]{:S(2)}) collective-permute-start(bf16[128,1280]{1,0:T(8,128)(2,1)} %refs_1_.3), channel_id=1, source_target_pairs={{0,2},{1,3},{2,0},{3,1},{4,6},{5,7},{6,4},{7,5},{8,10},{9,11},{10,... | collective-permute-start | bytes 983048 | tf_op jit(solution)/shard_map/ppermute | solution.py:60
  5.2 2.8 %shard_map.95 = (bf16[128,1280]{1,0:T(8,128)(2,1)S(1)}, f32[128,1]{1,0:T(8,128)S(1)}) custom-call(bf16[128,1664]{1,0:T(8,128)(2,1)} %refs_0_.5, bf16[1664,1280]{1,0:T(8,128)(2,1)} %refs_1_.2), custom_call_target="tpu_custom_call" | custom-call | flops 545259520 | bytes 4259840 | tf_op jit(solution)/shard_map/pallas_call | solution.py:123
  8.1 0.0 copy-start
  8.1 0.0 copy-start.3
  8.1 0.0 copy-start.4
  8.1 0.0 copy-start.5
  8.1 2.7 %collective-permute-start = (bf16[128,1280]{1,0:T(8,128)(2,1)S(1)}, bf16[128,1280]{1,0:T(8,128)(2,1)S(1)}, u32[]{:S(2)}, u32[]{:S(2)}) collective-permute-start(bf16[128,1280]{1,0:T(8,128)(2,1)S(1)} %get-tuple-element.28.refs_0_), channel_id=1, source_target_pairs={{0,8},{1,9},{2,10},{3,11},{4,12},{5,13},{6,14},{7,15},{8,0},{9,1},... | collective-permute-start | bytes 983048 | tf_op jit(solution)/shard_map/ppermute | solution.py:60
  10.8 0.0 collective-permute-start.1
  10.8 3.2 %collective-permute-done.2.refs_1_ = bf16[128,1280]{1,0:T(8,128)(2,1)S(1)} collective-permute-done((bf16[128,1280]{1,0:T(8,128)(2,1)}, bf16[128,1280]{1,0:T(8,128)(2,1)S(1)}, u32[]{:S(2)}, u32[]{:S(2)}) %collective-permute-start.2) | collective-permute-done | bytes 327712 | tf_op jit(solution)/shard_map/ppermute | solution.py:60
  13.9 3.3 %collective-permute-start.5 = (bf16[128,1280]{1,0:T(8,128)(2,1)S(1)}, bf16[128,1280]{1,0:T(8,128)(2,1)S(1)}, u32[]{:S(2)}, u32[]{:S(2)}) collective-permute-start(bf16[128,1280]{1,0:T(8,128)(2,1)S(1)} %collective-permute-done.2.refs_1_), channel_id=1, source_target_pairs={{0,2},{1,3},{2,0},{3,1},{4,6},{5,7},{6,4},{7,5},{8,10},{9,11},{10,... | collective-permute-start | bytes 983048 | tf_op jit(solution)/shard_map/ppermute | solution.py:60
  17.3 0.0 collective-permute-done.3.refs_2_
  17.3 3.5 %shard_map.96 = (bf16[128,1280]{1,0:T(8,128)(2,1)S(1)}, bf16[128,1280]{1,0:T(8,128)(2,1)S(1)}, bf16[128,1280]{1,0:T(8,128)(2,1)S(1)}, f32[128,1]{1,0:T(8,128)S(1)}, bf16[1280,1280]{1,0:T(8,128)(2,1)S(1)}) custom-call(bf16[128,1280]{1,0:T(8,128)(2,1)} %refs_1_.3, bf16[128,1280]{1,0:T(8,128)(2,1)S(1)} %collective-permute-done.2.refs_1_, ...), custom_call_target="tpu_custom_call" | custom-call | flops 1258291200 | bytes 3276800 | tf_op jit(solution)/shard_map/pallas_call | solution.py:123
  20.8 0.0 copy-done
  20.8 0.0 copy-done.3
  20.8 0.0 copy-done.4
  20.8 0.0 copy-done.5
  20.9 2.1 %shard_map.97 = (f32[128,4096]{1,0:T(8,128)S(1)}, f32[128,4096]{1,0:T(8,128)S(1)}) custom-call(bf16[128,1664]{1,0:T(8,128)(2,1)S(1)} %copy-done, bf16[128,1280]{1,0:T(8,128)(2,1)S(1)} %copy-done.3, bf16[32,1664]{1,0:T(8,128)(2,1)S(1)} %bitcast.2, bf16[32,1280]{1,0:T(8,128)(2,1)S(1)} %bitcast.3, f32[128,1]{1,0:T(8,128)S(1)} %get-tuple-element.30.refs_4_, ...), custom_call_target="tpu_custom_call" | custom-call | bytes 943104 | tf_op jit(solution)/shard_map/pallas_call | solution.py:34
  23.0 2.1 %collective-permute-done.refs_1_ = bf16[128,1280]{1,0:T(8,128)(2,1)S(1)} collective-permute-done((bf16[128,1280]{1,0:T(8,128)(2,1)S(1)}, bf16[128,1280]{1,0:T(8,128)(2,1)S(1)}, u32[]{:S(2)}, u32[]{:S(2)}) %collective-permute-start) | collective-permute-done | bytes 327712 | tf_op jit(solution)/shard_map/ppermute | solution.py:60
  25.1 0.1 collective-permute-start.4
  25.2 0.0 collective-permute-done.5.refs_0_
  25.2 0.0 copy-start.1
  25.2 0.0 copy-start.2
  25.2 0.7 %shard_map.99.refs_7_ = bf16[128,1280]{1,0:T(8,128)(2,1)S(1)} custom-call(bf16[128,1280]{1,0:T(8,128)(2,1)S(1)} %collective-permute-done.5.refs_0_, bf16[1280,1280]{1,0:T(8,128)(2,1)S(1)} %get-tuple-element.35.refs_1_), custom_call_target="tpu_custom_call" | custom-call | flops 419430400 | bytes 3604480 | tf_op jit(solution)/shard_map/pallas_call | solution.py:34
  25.9 0.0 collective-permute-done.1.refs_2_
  25.9 0.8 %collective-permute-done.4.refs_3_ = bf16[128,1280]{1,0:T(8,128)(2,1)S(1)} collective-permute-done((bf16[128,1280]{1,0:T(8,128)(2,1)S(1)}, bf16[128,1280]{1,0:T(8,128)(2,1)S(1)}, u32[]{:S(2)}, u32[]{:S(2)}) %collective-permute-start.4) | collective-permute-done | bytes 327712 | tf_op jit(solution)/shard_map/ppermute | solution.py:60
  26.8 1.4 %shard_map.100 = (f32[512,512]{1,0:T(8,128)S(1)}, f32[4,128]{1,0:T(4,128)S(1)}, f32[4,128]{1,0:T(4,128)S(1)}) custom-call(bf16[128,1280]{1,0:T(8,128)(2,1)S(1)} %get-tuple-element.28.refs_0_, bf16[128,1280]{1,0:T(8,128)(2,1)S(1)} %collective-permute-done.refs_1_, bf16[128,1280]{1,0:T(8,128)(2,1)S(1)} %collective-permute-done.1.refs_2_, ...), custom_call_target="tpu_custom_call" | custom-call | flops 671088640 | bytes 2621440 | tf_op jit(solution)/shard_map/pallas_call | solution.py:34
  28.2 0.0 collective-permute-start.6
  28.2 0.2 collective-permute-start.7
  28.4 2.8 %collective-permute-start.11 = (f32[4,128]{1,0:T(4,128)S(1)}, f32[4,128]{1,0:T(4,128)S(1)}, u32[]{:S(2)}, u32[]{:S(2)}) collective-permute-start(f32[4,128]{1,0:T(4,128)S(1)} %get-tuple-element.37.refs_4_), channel_id=1, source_target_pairs={{0,6},{1,7},{2,4},{3,5},{4,2},{5,3},{6,0},{7,1},{8,14},{9,15},{10,... | collective-permute-start | bytes 6152 | tf_op jit(solution)/shard_map/ppermute | solution.py:60
  31.2 1.5 %collective-permute-start.10 = (f32[4,128]{1,0:T(4,128)S(1)}, f32[4,128]{1,0:T(4,128)S(1)}, u32[]{:S(2)}, u32[]{:S(2)}) collective-permute-start(f32[4,128]{1,0:T(4,128)S(1)} %get-tuple-element.37.refs_4_), channel_id=1, source_target_pairs={{0,2},{1,3},{2,0},{3,1},{4,6},{5,7},{6,4},{7,5},{8,10},{9,11},{10,... | collective-permute-start | bytes 6152 | tf_op jit(solution)/shard_map/ppermute | solution.py:60
  32.7 0.0 collective-permute-start.9
  32.7 0.0 collective-permute-done.6.refs_1_
  32.7 0.0 collective-permute-start.8
  32.8 0.0 copy-done.1
  32.8 0.0 copy-done.2
  32.8 1.7 %shard_map.101 = (f32[512,128]{1,0:T(8,128)S(1)}, bf16[128,512]{1,0:T(8,128)(2,1)S(1)}, bf16[512,128]{1,0:T(8,128)(2,1)S(1)}, f32[128,512]{1,0:T(8,128)S(1)}, f3...) custom-call(bf16[128,1280]{1,0:T(8,128)(2,1)S(1)} %get-tuple-element.28.refs_0_, ...), custom_call_target="tpu_custom_call" | custom-call | flops 671088640 | bytes 3276800 | tf_op jit(solution)/shard_map/pallas_call | solution.py:34
  34.4 0.0 collective-permute-done.7.refs_2_
  34.4 0.0 collective-permute-done.11.refs_7_
  34.4 0.4 collective-permute-done.10.refs_6_
  34.8 1.5 %collective-permute-done.9.refs_5_ = f32[4,128]{1,0:T(4,128)S(1)} collective-permute-done((f32[4,128]{1,0:T(4,128)S(1)}, f32[4,128]{1,0:T(4,128)S(1)}, u32[]{:S(2)}, u32[]{:S(2)}) %collective-permute-start.9) | collective-permute-done | bytes 2080 | tf_op jit(solution)/shard_map/ppermute | solution.py:60
  36.3 0.0 collective-permute-done.8.refs_3_
  36.3 0.9 %shard_map.102 = (f32[128,128]{1,0:T(8,128)S(1)}, bf16[128,128]{1,0:T(8,128)(2,1)S(1)}, bf16[128,128]{1,0:T(8,128)(2,1)S(1)}, bf16[128,128]{1,0:T(8,128)(2,1)S(1...) custom-call(f32[4,128]{1,0:T(4,128)S(1)} %get-tuple-element.36.refs_, ...), custom_call_target="tpu_custom_call" | custom-call | flops 134217728 | bytes 1851392 | tf_op jit(solution)/shard_map/pallas_call | solution.py:34
  37.2 0.3 collective-permute-start.12
  37.5 0.0 collective-permute-start.13
  37.5 2.8 %collective-permute-start.14 = (bf16[128,128]{1,0:T(8,128)(2,1)S(1)}, bf16[128,128]{1,0:T(8,128)(2,1)S(1)}, u32[]{:S(2)}, u32[]{:S(2)}) collective-permute-start(bf16[128,128]{1,0:T(8,128)(2,1)S(1)} %get-tuple-element.46), channel_id=1, source_target_pairs={{0,9},{1,8},{2,11},{3,10},{4,13},{5,12},{6,15},{7,14},{8,1},{9,0},... | collective-permute-start | bytes 98312 | tf_op jit(solution)/shard_map/ppermute | solution.py:60
  40.3 0.2 collective-permute-start.15
  40.5 0.5 %collective-permute-start.16 = (bf16[128,128]{1,0:T(8,128)(2,1)S(1)}, bf16[128,128]{1,0:T(8,128)(2,1)S(1)}, u32[]{:S(2)}, u32[]{:S(2)}) collective-permute-start(bf16[128,128]{1,0:T(8,128)(2,1)S(1)} %get-tuple-element.50), channel_id=1, source_target_pairs={{0,2},{1,3},{2,0},{3,1},{4,6},{5,7},{6,4},{7,5},{8,10},{9,11},{10,... | collective-permute-start | bytes 98312 | tf_op jit(solution)/shard_map/ppermute | solution.py:60
  41.0 1.4 %collective-permute-done.12.refs_1_ = bf16[128,128]{1,0:T(8,128)(2,1)S(1)} collective-permute-done((bf16[128,128]{1,0:T(8,128)(2,1)S(1)}, bf16[128,128]{1,0:T(8,128)(2,1)S(1)}, u32[]{:S(2)}, u32[]{:S(2)}) %collective-permute-start.12) | collective-permute-done | bytes 32800 | tf_op jit(solution)/shard_map/ppermute | solution.py:60
  42.4 1.4 %collective-permute-start.17 = (bf16[128,128]{1,0:T(8,128)(2,1)S(1)}, bf16[128,128]{1,0:T(8,128)(2,1)S(1)}, u32[]{:S(2)}, u32[]{:S(2)}) collective-permute-start(bf16[128,128]{1,0:T(8,128)(2,1)S(1)} %get-tuple-element.51), channel_id=1, source_target_pairs={{0,6},{1,7},{2,4},{3,5},{4,2},{5,3},{6,0},{7,1},{8,14},{9,15},{10,... | collective-permute-start | bytes 98312 | tf_op jit(solution)/shard_map/ppermute | solution.py:60
  43.8 0.0 collective-permute-done.13.refs_2_
  43.8 0.0 collective-permute-done.14.refs_3_
  43.8 1.1 %shard_map.103 = bf16[128,4096]{1,0:T(8,128)(2,1)} custom-call(f32[128,128]{1,0:T(8,128)S(1)} %get-tuple-element.43.refs_0_, bf16[128,128]{1,0:T(8,128)(2,1)S(1)} %collective-permute-done.12.refs_1_, bf16[128,128]{1,0:T(8,128)(2,1)S(1)} %collective-permute-done.13.refs_2_, bf16[128,128]{1,0:T(8,128)(2,1)S(1)} %collective-permute-done.14.refs_3_, ...), custom_call_target="tpu_custom_call" | custom-call | flops 524288 | bytes 3145728 | tf_op jit(solution)/shard_map/pallas_call | solution.py:270
  44.9 0.0 collective-permute-done.15.refs_1_
  44.9 0.0 collective-permute-done.16.refs_2_
  44.9 2.3 %collective-permute-done.17.refs_3_ = bf16[128,128]{1,0:T(8,128)(2,1)S(1)} collective-permute-done((bf16[128,128]{1,0:T(8,128)(2,1)S(1)}, bf16[128,128]{1,0:T(8,128)(2,1)S(1)}, u32[]{:S(2)}, u32[]{:S(2)}) %collective-permute-start.17) | collective-permute-done | bytes 32800 | tf_op jit(solution)/shard_map/ppermute | solution.py:60
  47.2 1.1 %shard_map.104 = bf16[128,4096]{1,0:T(8,128)(2,1)} custom-call(f32[128,128]{1,0:T(8,128)S(1)} %get-tuple-element.48.refs_0_, bf16[128,128]{1,0:T(8,128)(2,1)S(1)} %collective-permute-done.15.refs_1_, bf16[128,128]{1,0:T(8,128)(2,1)S(1)} %collective-permute-done.16.refs_2_, bf16[128,128]{1,0:T(8,128)(2,1)S(1)} %collective-permute-done.17.refs_3_, ...), custom_call_target="tpu_custom_call" | custom-call | flops 524288 | bytes 3145728 | tf_op jit(solution)/shard_map/pallas_call | solution.py:270
  (2 shorter events, 0.0 us)
Async XLA Ops:
  0.6 13.3 %collective-permute-start.2 = (bf16[128,1280]{1,0:T(8,128)(2,1)}, bf16[128,1280]{1,0:T(8,128)(2,1)S(1)}, u32[]{:S(2)}, u32[]{:S(2)}) collective-permute-start(bf16[128,1280]{1,0:T(8,128)(2,1)} %refs_1_.3), channel_id=1, source_target_pairs={{0,4},{1,5},{2,6},{3,7},{4,0},{5,1},{6,2},{7,3},{8,12},{9,13},{10,... | collective-permute-start | bytes 983048 | tf_op jit(solution)/shard_map/ppermute | solution.py:60
  3.7 13.5 %collective-permute-start.3 = (bf16[128,1280]{1,0:T(8,128)(2,1)}, bf16[128,1280]{1,0:T(8,128)(2,1)S(1)}, u32[]{:S(2)}, u32[]{:S(2)}) collective-permute-start(bf16[128,1280]{1,0:T(8,128)(2,1)} %refs_1_.3), channel_id=1, source_target_pairs={{0,2},{1,3},{2,0},{3,1},{4,6},{5,7},{6,4},{7,5},{8,10},{9,11},{10,... | collective-permute-start | bytes 983048 | tf_op jit(solution)/shard_map/ppermute | solution.py:60
  8.1 12.7 %copy-start = (bf16[128,1664]{1,0:T(8,128)(2,1)S(1)}, bf16[128,1664]{1,0:T(8,128)(2,1)}, u32[]{:S(2)}) copy-start(bf16[128,1664]{1,0:T(8,128)(2,1)} %refs_0_.5) | copy-start | bytes 1277956
  8.1 12.7 %copy-start.3 = (bf16[128,1280]{1,0:T(8,128)(2,1)S(1)}, bf16[128,1280]{1,0:T(8,128)(2,1)}, u32[]{:S(2)}) copy-start(bf16[128,1280]{1,0:T(8,128)(2,1)} %refs_1_.3) | copy-start | bytes 983044
  8.1 12.7 %copy-start.4 = (bf16[1664,32]{0,1:T(8,128)(2,1)S(1)}, bf16[1664,32]{0,1:T(8,128)(2,1)}, u32[]{:S(2)}) copy-start(bf16[1664,32]{0,1:T(8,128)(2,1)} %param.12) | copy-start | bytes 319492
  8.1 12.7 %copy-start.5 = (bf16[1280,32]{0,1:T(8,128)(2,1)S(1)}, bf16[1280,32]{0,1:T(8,128)(2,1)}, u32[]{:S(2)}) copy-start(bf16[1280,32]{0,1:T(8,128)(2,1)} %param.14) | copy-start | bytes 245764
  8.1 16.9 %collective-permute-start = (bf16[128,1280]{1,0:T(8,128)(2,1)S(1)}, bf16[128,1280]{1,0:T(8,128)(2,1)S(1)}, u32[]{:S(2)}, u32[]{:S(2)}) collective-permute-start(bf16[128,1280]{1,0:T(8,128)(2,1)S(1)} %get-tuple-element.28.refs_0_), channel_id=1, source_target_pairs={{0,8},{1,9},{2,10},{3,11},{4,12},{5,13},{6,14},{7,15},{8,0},{9,1},... | collective-permute-start | bytes 983048 | tf_op jit(solution)/shard_map/ppermute | solution.py:60
  10.8 15.1 %collective-permute-start.1 = (bf16[128,1280]{1,0:T(8,128)(2,1)S(1)}, bf16[128,1280]{1,0:T(8,128)(2,1)S(1)}, u32[]{:S(2)}, u32[]{:S(2)}) collective-permute-start(bf16[128,1280]{1,0:T(8,128)(2,1)S(1)} %get-tuple-element.28.refs_0_), channel_id=1, source_target_pairs={{0,1},{1,0},{2,3},{3,2},{4,5},{5,4},{6,7},{7,6},{8,9},{9,8},{10,11... | collective-permute-start | bytes 983048 | tf_op jit(solution)/shard_map/ppermute | solution.py:60
  13.9 11.2 %collective-permute-start.5 = (bf16[128,1280]{1,0:T(8,128)(2,1)S(1)}, bf16[128,1280]{1,0:T(8,128)(2,1)S(1)}, u32[]{:S(2)}, u32[]{:S(2)}) collective-permute-start(bf16[128,1280]{1,0:T(8,128)(2,1)S(1)} %collective-permute-done.2.refs_1_), channel_id=1, source_target_pairs={{0,2},{1,3},{2,0},{3,1},{4,6},{5,7},{6,4},{7,5},{8,10},{9,11},{10,... | collective-permute-start | bytes 983048 | tf_op jit(solution)/shard_map/ppermute | solution.py:60
  25.1 1.7 %collective-permute-start.4 = (bf16[128,1280]{1,0:T(8,128)(2,1)S(1)}, bf16[128,1280]{1,0:T(8,128)(2,1)S(1)}, u32[]{:S(2)}, u32[]{:S(2)}) collective-permute-start(bf16[128,1280]{1,0:T(8,128)(2,1)S(1)} %shard_map.98), channel_id=1, source_target_pairs={{0,1},{1,0},{2,3},{3,2},{4,5},{5,4},{6,7},{7,6},{8,9},{9,8},{10,11... | collective-permute-start | bytes 983048 | tf_op jit(solution)/shard_map/ppermute | solution.py:60
  25.2 7.6 %copy-start.1 = (bf16[1280,128]{1,0:T(8,128)(2,1)S(1)}, bf16[1280,128]{1,0:T(8,128)(2,1)}, u32[]{:S(2)}) copy-start(bf16[1280,128]{1,0:T(8,128)(2,1)} %refs_8_.1) | copy-start | bytes 983044
  25.2 7.6 %copy-start.2 = (bf16[1280,128]{1,0:T(8,128)(2,1)S(1)}, bf16[1280,128]{1,0:T(8,128)(2,1)}, u32[]{:S(2)}) copy-start(bf16[1280,128]{1,0:T(8,128)(2,1)} %refs_9_.1) | copy-start | bytes 983044
  28.2 4.6 %collective-permute-start.6 = (f32[4,128]{1,0:T(4,128)S(1)}, f32[4,128]{1,0:T(4,128)S(1)}, u32[]{:S(2)}, u32[]{:S(2)}) collective-permute-start(f32[4,128]{1,0:T(4,128)S(1)} %get-tuple-element.36.refs_0_), channel_id=1, source_target_pairs={{0,8},{1,9},{2,10},{3,11},{4,12},{5,13},{6,14},{7,15},{8,0},{9,1},... | collective-permute-start | bytes 6152 | tf_op jit(solution)/shard_map/ppermute | solution.py:60
  28.2 6.2 %collective-permute-start.7 = (f32[4,128]{1,0:T(4,128)S(1)}, f32[4,128]{1,0:T(4,128)S(1)}, u32[]{:S(2)}, u32[]{:S(2)}) collective-permute-start(f32[4,128]{1,0:T(4,128)S(1)} %get-tuple-element.36.refs_0_), channel_id=1, source_target_pairs={{0,1},{1,0},{2,3},{3,2},{4,5},{5,4},{6,7},{7,6},{8,9},{9,8},{10,11... | collective-permute-start | bytes 6152 | tf_op jit(solution)/shard_map/ppermute | solution.py:60
  28.4 6.0 %collective-permute-start.11 = (f32[4,128]{1,0:T(4,128)S(1)}, f32[4,128]{1,0:T(4,128)S(1)}, u32[]{:S(2)}, u32[]{:S(2)}) collective-permute-start(f32[4,128]{1,0:T(4,128)S(1)} %get-tuple-element.37.refs_4_), channel_id=1, source_target_pairs={{0,6},{1,7},{2,4},{3,5},{4,2},{5,3},{6,0},{7,1},{8,14},{9,15},{10,... | collective-permute-start | bytes 6152 | tf_op jit(solution)/shard_map/ppermute | solution.py:60
  31.2 3.6 %collective-permute-start.10 = (f32[4,128]{1,0:T(4,128)S(1)}, f32[4,128]{1,0:T(4,128)S(1)}, u32[]{:S(2)}, u32[]{:S(2)}) collective-permute-start(f32[4,128]{1,0:T(4,128)S(1)} %get-tuple-element.37.refs_4_), channel_id=1, source_target_pairs={{0,2},{1,3},{2,0},{3,1},{4,6},{5,7},{6,4},{7,5},{8,10},{9,11},{10,... | collective-permute-start | bytes 6152 | tf_op jit(solution)/shard_map/ppermute | solution.py:60
  32.7 3.6 %collective-permute-start.9 = (f32[4,128]{1,0:T(4,128)S(1)}, f32[4,128]{1,0:T(4,128)S(1)}, u32[]{:S(2)}, u32[]{:S(2)}) collective-permute-start(f32[4,128]{1,0:T(4,128)S(1)} %get-tuple-element.37.refs_4_), channel_id=1, source_target_pairs={{0,4},{1,5},{2,6},{3,7},{4,0},{5,1},{6,2},{7,3},{8,12},{9,13},{10,... | collective-permute-start | bytes 6152 | tf_op jit(solution)/shard_map/ppermute | solution.py:60
  32.7 3.6 %collective-permute-start.8 = (f32[4,128]{1,0:T(4,128)S(1)}, f32[4,128]{1,0:T(4,128)S(1)}, u32[]{:S(2)}, u32[]{:S(2)}) collective-permute-start(f32[4,128]{1,0:T(4,128)S(1)} %collective-permute-done.6.refs_1_), channel_id=1, source_target_pairs={{0,1},{1,0},{2,3},{3,2},{4,5},{5,4},{6,7},{7,6},{8,9},{9,8},{10,11... | collective-permute-start | bytes 6152 | tf_op jit(solution)/shard_map/ppermute | solution.py:60
  37.2 5.2 %collective-permute-start.12 = (bf16[128,128]{1,0:T(8,128)(2,1)S(1)}, bf16[128,128]{1,0:T(8,128)(2,1)S(1)}, u32[]{:S(2)}, u32[]{:S(2)}) collective-permute-start(bf16[128,128]{1,0:T(8,128)(2,1)S(1)} %get-tuple-element.44), channel_id=1, source_target_pairs={{0,8},{1,9},{2,10},{3,11},{4,12},{5,13},{6,14},{7,15},{8,0},{9,1},... | collective-permute-start | bytes 98312 | tf_op jit(solution)/shard_map/ppermute | solution.py:60
  37.5 6.3 %collective-permute-start.13 = (bf16[128,128]{1,0:T(8,128)(2,1)S(1)}, bf16[128,128]{1,0:T(8,128)(2,1)S(1)}, u32[]{:S(2)}, u32[]{:S(2)}) collective-permute-start(bf16[128,128]{1,0:T(8,128)(2,1)S(1)} %get-tuple-element.45), channel_id=1, source_target_pairs={{0,1},{1,0},{2,3},{3,2},{4,5},{5,4},{6,7},{7,6},{8,9},{9,8},{10,11... | collective-permute-start | bytes 98312 | tf_op jit(solution)/shard_map/ppermute | solution.py:60
  37.5 6.3 %collective-permute-start.14 = (bf16[128,128]{1,0:T(8,128)(2,1)S(1)}, bf16[128,128]{1,0:T(8,128)(2,1)S(1)}, u32[]{:S(2)}, u32[]{:S(2)}) collective-permute-start(bf16[128,128]{1,0:T(8,128)(2,1)S(1)} %get-tuple-element.46), channel_id=1, source_target_pairs={{0,9},{1,8},{2,11},{3,10},{4,13},{5,12},{6,15},{7,14},{8,1},{9,0},... | collective-permute-start | bytes 98312 | tf_op jit(solution)/shard_map/ppermute | solution.py:60
  40.3 4.6 %collective-permute-start.15 = (bf16[128,128]{1,0:T(8,128)(2,1)S(1)}, bf16[128,128]{1,0:T(8,128)(2,1)S(1)}, u32[]{:S(2)}, u32[]{:S(2)}) collective-permute-start(bf16[128,128]{1,0:T(8,128)(2,1)S(1)} %get-tuple-element.49), channel_id=1, source_target_pairs={{0,4},{1,5},{2,6},{3,7},{4,0},{5,1},{6,2},{7,3},{8,12},{9,13},{10,... | collective-permute-start | bytes 98312 | tf_op jit(solution)/shard_map/ppermute | solution.py:60
  40.5 4.4 %collective-permute-start.16 = (bf16[128,128]{1,0:T(8,128)(2,1)S(1)}, bf16[128,128]{1,0:T(8,128)(2,1)S(1)}, u32[]{:S(2)}, u32[]{:S(2)}) collective-permute-start(bf16[128,128]{1,0:T(8,128)(2,1)S(1)} %get-tuple-element.50), channel_id=1, source_target_pairs={{0,2},{1,3},{2,0},{3,1},{4,6},{5,7},{6,4},{7,5},{8,10},{9,11},{10,... | collective-permute-start | bytes 98312 | tf_op jit(solution)/shard_map/ppermute | solution.py:60
  42.4 4.8 %collective-permute-start.17 = (bf16[128,128]{1,0:T(8,128)(2,1)S(1)}, bf16[128,128]{1,0:T(8,128)(2,1)S(1)}, u32[]{:S(2)}, u32[]{:S(2)}) collective-permute-start(bf16[128,128]{1,0:T(8,128)(2,1)S(1)} %get-tuple-element.51), channel_id=1, source_target_pairs={{0,6},{1,7},{2,4},{3,5},{4,2},{5,3},{6,0},{7,1},{8,14},{9,15},{10,... | collective-permute-start | bytes 98312 | tf_op jit(solution)/shard_map/ppermute | solution.py:60

commit v4 on v3

--- a/solution.py
+++ b/solution.py
@@ -216,12 +216,38 @@
     return top + jnp.log(sum(jnp.exp(p - top) for p in lined))
 
 
+def add_kernel(count, *refs):
+    own, got, sent = refs[:count], refs[count:-1], refs[-1]
+    rows = own[0].shape[0]
+    for k in range(count):
+        part = own[k][...]
+        for arrived in got:
+            at = (count + k) * rows
+            part = part + arrived[at : at + rows].astype(F32)
+        sent[k * rows : (k + 1) * rows] = part.astype(sent.dtype)
+
+
+def halve(kept, sent, bits, n):
+    rows = kept[0].shape[0]
+    got = [swap(sent, bits[-1], n)]
+    for bit in bits[-2::-1]:
+        upper = kept[len(kept) // 2 :]
+        (sent,) = call(
+            functools.partial(add_kernel, len(upper)),
+            [((len(upper) * rows, kept[0].shape[1]), BF16)],
+            [*upper, *got],
+        )
+        kept = kept[: len(kept) // 2]
+        got.append(swap(sent, bit, n))
+    return [kept[0], *got], sent
+
+
 def weights_kernel(ni, nt, *refs):
     row_parts, col_parts = refs[:ni], refs[ni : ni + nt]
     raw, img_low, img_side_t, txt_low, txt_side_t = refs[ni + nt : ni + nt + 5]
-    img_parts = refs[ni + nt + 5 : 2 * ni + nt + 5]
-    txt_parts = refs[2 * ni + nt + 5 : 2 * ni + 2 * nt + 5]
-    weights_bf = refs[-1]
+    half = ni // 2
+    img_kept, img_sent = refs[ni + nt + 5 : ni + nt + 5 + half], refs[ni + nt + 5 + half]
+    txt_parts, weights_bf = refs[-1 - nt : -1], refs[-1]
     rows = LANES
     row_lse = merge(row_parts)
     col_lse = merge(col_parts)
@@ -242,7 +268,10 @@
             dot(weights_bf[a * rows : (a + 1) * rows], txt_low[...])
             - inner * img_low[a * rows : (a + 1) * rows]
         )
-        img_parts[a][...] = part.astype(img_parts[a].dtype)
+        if a < half:
+            img_kept[a][...] = part
+        else:
+            img_sent[(a - half) * rows : (a - half + 1) * rows] = part.astype(img_sent.dtype)
     for t in range(nt):
         here = slice(t * rows, (t + 1) * rows)
         part = dot(img_side_t[...], weights_bf[:, here]) - inner_col[t] * txt_side_t[:, here]
@@ -252,7 +281,7 @@
 def sketch_kernel(count, turned, *refs):
     parts, (base, keys, out, made, sems) = refs[:count], refs[count:]
     rows = base.shape[0]
-    grad = sum((part[...].astype(F32) for part in parts[1:]), parts[0][...])
+    grad = sum((part[:rows].astype(F32) for part in parts[1:]), parts[0][...])
     grad = (grad.T if turned else grad) + base[...]
     copies, step = [], rows // 2
     for k in range(2):
@@ -317,17 +346,20 @@
         images + texts + [b_img, b_txt],
         flops=4 * (ni + nt) * rows * wide * low,
     )
+    half = ni // 2
     parts = call(
         functools.partial(weights_kernel, ni, nt),
-        [((rows, low), F32 if k in (0, ni) else BF16) for k in range(ni + nt)],
+        [((rows, low), F32)] * half
+        + [((half * rows, low), BF16), ((rows, low), F32)]
+        + [((rows, low), BF16)] * (nt - 1),
         row_parts + col_parts + [raw, img_low, img_side_t, txt_low, txt_side_t],
         scratch=[pltpu.VMEM((ni * rows, nt * rows), BF16)],
         flops=4 * ni * nt * rows * rows * low,
     )
-    img_parts, txt_parts = [
-        [own] + [swap(p, o, n) for p, o in zip(sent, offsets[1:])]
-        for (own, *sent), offsets in ((parts[:ni], img_span), (parts[ni:], txt_span))
-    ]
+    img_parts, last = halve(list(parts[:half]), parts[half], img_bits, n)
+    txt_parts = list(parts[half + 1 :])
+    txt_parts[2:] = [hold(p, [last]) for p in txt_parts[2:]]
+    txt_parts = txt_parts[:1] + [swap(p, o, n) for p, o in zip(txt_parts[1:], txt_span[1:])]
     return (
         sketch(img_parts, img_base, img_keys, False),
         sketch(txt_parts, txt_base, txt_keys, True),

time: 48.5 us -> 47.1 us (0.971)
  starting transfers between devices: 20.4 us -> 19.1 us
    ppermute x18 -> x17, starting transfers between devices: 20.4 us -> 19.1 us  [swap(): return lax.ppermute(x, 'dp', [(i, i ^ offset) for i in range(n)])]
    ppermute x18 -> x17, waiting for transfers between devices: 11.7 us -> 11.7 us  [swap(): return lax.ppermute(x, 'dp', [(i, i ^ offset) for i in range(n)])]
    pallas_call x5 -> x6, Pallas kernels: 6.76 us -> 6.77 us  [call(): pl.pallas_call(kernel, out_shape=[jax.ShapeDtypeStruct(s, d) for s, d in...]
  transfers between devices with their start and end apart: 18 -> 17, of which waited for: 7 -> 8; matrix products, arithmetic and copies ran while one was open for 0% -> 0% of each run, Pallas kernels for 25% -> 25%
where the time goes in v4:
time: 47.1 us; the launch traced here: 47 us
  starting transfers between devices  19.1 us (41%)
  Pallas kernels  15.4 us (33%)
  waiting for transfers between devices  11.7 us (25%)
  between operations  0.85 us (2%)
    ppermute x17, starting transfers between devices, swap(): return lax.ppermute(x, 'dp', [(i, i ^ offset) for i in range(n)])  19.1 us
    ppermute x17, waiting for transfers between devices, swap(): return lax.ppermute(x, 'dp', [(i, i ^ offset) for i in range(n)])  11.7 us
    pallas_call x6, Pallas kernels, call(): pl.pallas_call(kernel, out_shape=[jax.ShapeDtypeStruct(s, d) for s, d in...  6.77 us
    pallas_call x2, Pallas kernels, stream_embed(): pl.pallas_call(functools.partial(stream_kernel, blocks, cuts), out_shape=...  6.37 us
    pallas_call x2, Pallas kernels, sketch(): pl.pallas_call(functools.partial(sketch_kernel, len(parts), turned), out_...  2.22 us
  transfers between devices with their start and end apart: 17, of which 8 were waited for; matrix products, arithmetic and copies ran while one was open for 0% of the time, Pallas kernels for 25%

profile of v4, /device:TPU:0, one launch (start us, length us, event | category | flops | bytes accessed | tf_op | source)
XLA Modules:
  0.0 47.0 jit_solution(2917471908735221231)
XLA Ops:
  0.6 3.1 %collective-permute-start.2 = (bf16[128,1280]{1,0:T(8,128)(2,1)}, bf16[128,1280]{1,0:T(8,128)(2,1)S(1)}, u32[]{:S(2)}, u32[]{:S(2)}) collective-permute-start(bf16[128,1280]{1,0:T(8,128)(2,1)} %refs_1_.3), channel_id=1, source_target_pairs={{0,4},{1,5},{2,6},{3,7},{4,0},{5,1},{6,2},{7,3},{8,12},{9,13},{10,... | collective-permute-start | bytes 983048 | tf_op jit(solution)/shard_map/ppermute | solution.py:60
  3.7 1.5 %collective-permute-start.3 = (bf16[128,1280]{1,0:T(8,128)(2,1)}, bf16[128,1280]{1,0:T(8,128)(2,1)S(1)}, u32[]{:S(2)}, u32[]{:S(2)}) collective-permute-start(bf16[128,1280]{1,0:T(8,128)(2,1)} %refs_1_.3), channel_id=1, source_target_pairs={{0,2},{1,3},{2,0},{3,1},{4,6},{5,7},{6,4},{7,5},{8,10},{9,11},{10,... | collective-permute-start | bytes 983048 | tf_op jit(solution)/shard_map/ppermute | solution.py:60
  5.2 2.8 %shard_map.95 = (bf16[128,1280]{1,0:T(8,128)(2,1)S(1)}, f32[128,1]{1,0:T(8,128)S(1)}) custom-call(bf16[128,1664]{1,0:T(8,128)(2,1)} %refs_0_.5, bf16[1664,1280]{1,0:T(8,128)(2,1)} %refs_1_.2), custom_call_target="tpu_custom_call" | custom-call | flops 545259520 | bytes 4259840 | tf_op jit(solution)/shard_map/pallas_call | solution.py:123
  8.1 0.0 copy-start
  8.1 0.0 copy-start.3
  8.1 0.0 copy-start.4
  8.1 0.0 copy-start.5
  8.1 2.7 %collective-permute-start = (bf16[128,1280]{1,0:T(8,128)(2,1)S(1)}, bf16[128,1280]{1,0:T(8,128)(2,1)S(1)}, u32[]{:S(2)}, u32[]{:S(2)}) collective-permute-start(bf16[128,1280]{1,0:T(8,128)(2,1)S(1)} %get-tuple-element.27.refs_0_), channel_id=1, source_target_pairs={{0,8},{1,9},{2,10},{3,11},{4,12},{5,13},{6,14},{7,15},{8,0},{9,1},... | collective-permute-start | bytes 983048 | tf_op jit(solution)/shard_map/ppermute | solution.py:60
  10.8 0.0 collective-permute-start.1
  10.8 3.2 %collective-permute-done.2.refs_1_ = bf16[128,1280]{1,0:T(8,128)(2,1)S(1)} collective-permute-done((bf16[128,1280]{1,0:T(8,128)(2,1)}, bf16[128,1280]{1,0:T(8,128)(2,1)S(1)}, u32[]{:S(2)}, u32[]{:S(2)}) %collective-permute-start.2) | collective-permute-done | bytes 327712 | tf_op jit(solution)/shard_map/ppermute | solution.py:60
  13.9 3.3 %collective-permute-start.5 = (bf16[128,1280]{1,0:T(8,128)(2,1)S(1)}, bf16[128,1280]{1,0:T(8,128)(2,1)S(1)}, u32[]{:S(2)}, u32[]{:S(2)}) collective-permute-start(bf16[128,1280]{1,0:T(8,128)(2,1)S(1)} %collective-permute-done.2.refs_1_), channel_id=1, source_target_pairs={{0,2},{1,3},{2,0},{3,1},{4,6},{5,7},{6,4},{7,5},{8,10},{9,11},{10,... | collective-permute-start | bytes 983048 | tf_op jit(solution)/shard_map/ppermute | solution.py:60
  17.3 0.0 collective-permute-done.3.refs_2_
  17.3 3.5 %shard_map.96 = (bf16[128,1280]{1,0:T(8,128)(2,1)S(1)}, bf16[128,1280]{1,0:T(8,128)(2,1)S(1)}, bf16[128,1280]{1,0:T(8,128)(2,1)S(1)}, f32[128,1]{1,0:T(8,128)S(1)}, bf16[1280,1280]{1,0:T(8,128)(2,1)S(1)}) custom-call(bf16[128,1280]{1,0:T(8,128)(2,1)} %refs_1_.3, bf16[128,1280]{1,0:T(8,128)(2,1)S(1)} %collective-permute-done.2.refs_1_, ...), custom_call_target="tpu_custom_call" | custom-call | flops 1258291200 | bytes 3276800 | tf_op jit(solution)/shard_map/pallas_call | solution.py:123
  20.8 0.0 copy-done
  20.8 0.0 copy-done.3
  20.8 0.0 copy-done.4
  20.8 0.0 copy-done.5
  20.9 2.1 %shard_map.97 = (f32[128,4096]{1,0:T(8,128)S(1)}, f32[128,4096]{1,0:T(8,128)S(1)}) custom-call(bf16[128,1664]{1,0:T(8,128)(2,1)S(1)} %copy-done, bf16[128,1280]{1,0:T(8,128)(2,1)S(1)} %copy-done.3, bf16[32,1664]{1,0:T(8,128)(2,1)S(1)} %bitcast.2, bf16[32,1280]{1,0:T(8,128)(2,1)S(1)} %bitcast.3, f32[128,1]{1,0:T(8,128)S(1)} %get-tuple-element.29.refs_4_, ...), custom_call_target="tpu_custom_call" | custom-call | bytes 943104 | tf_op jit(solution)/shard_map/pallas_call | solution.py:34
  23.0 2.1 %collective-permute-done.refs_1_ = bf16[128,1280]{1,0:T(8,128)(2,1)S(1)} collective-permute-done((bf16[128,1280]{1,0:T(8,128)(2,1)S(1)}, bf16[128,1280]{1,0:T(8,128)(2,1)S(1)}, u32[]{:S(2)}, u32[]{:S(2)}) %collective-permute-start) | collective-permute-done | bytes 327712 | tf_op jit(solution)/shard_map/ppermute | solution.py:60
  25.1 0.1 collective-permute-start.4
  25.2 0.0 collective-permute-done.5.refs_0_
  25.2 0.0 copy-start.1
  25.2 0.0 copy-start.2
  25.2 0.7 %shard_map.99.refs_7_ = bf16[128,1280]{1,0:T(8,128)(2,1)S(1)} custom-call(bf16[128,1280]{1,0:T(8,128)(2,1)S(1)} %collective-permute-done.5.refs_0_, bf16[1280,1280]{1,0:T(8,128)(2,1)S(1)} %get-tuple-element.34.refs_1_), custom_call_target="tpu_custom_call" | custom-call | flops 419430400 | bytes 3604480 | tf_op jit(solution)/shard_map/pallas_call | solution.py:34
  25.9 0.0 collective-permute-done.1.refs_2_
  25.9 0.8 %collective-permute-done.4.refs_3_ = bf16[128,1280]{1,0:T(8,128)(2,1)S(1)} collective-permute-done((bf16[128,1280]{1,0:T(8,128)(2,1)S(1)}, bf16[128,1280]{1,0:T(8,128)(2,1)S(1)}, u32[]{:S(2)}, u32[]{:S(2)}) %collective-permute-start.4) | collective-permute-done | bytes 327712 | tf_op jit(solution)/shard_map/ppermute | solution.py:60
  26.8 1.4 %shard_map.100 = (f32[512,512]{1,0:T(8,128)S(1)}, f32[4,128]{1,0:T(4,128)S(1)}, f32[4,128]{1,0:T(4,128)S(1)}) custom-call(bf16[128,1280]{1,0:T(8,128)(2,1)S(1)} %get-tuple-element.27.refs_0_, bf16[128,1280]{1,0:T(8,128)(2,1)S(1)} %collective-permute-done.refs_1_, bf16[128,1280]{1,0:T(8,128)(2,1)S(1)} %collective-permute-done.1.refs_2_, ...), custom_call_target="tpu_custom_call" | custom-call | flops 671088640 | bytes 2621440 | tf_op jit(solution)/shard_map/pallas_call | solution.py:34
  28.2 0.0 collective-permute-start.6
  28.2 0.2 collective-permute-start.7
  28.4 2.8 %collective-permute-start.11 = (f32[4,128]{1,0:T(4,128)S(1)}, f32[4,128]{1,0:T(4,128)S(1)}, u32[]{:S(2)}, u32[]{:S(2)}) collective-permute-start(f32[4,128]{1,0:T(4,128)S(1)} %get-tuple-element.36.refs_4_), channel_id=1, source_target_pairs={{0,6},{1,7},{2,4},{3,5},{4,2},{5,3},{6,0},{7,1},{8,14},{9,15},{10,... | collective-permute-start | bytes 6152 | tf_op jit(solution)/shard_map/ppermute | solution.py:60
  31.2 1.5 %collective-permute-start.10 = (f32[4,128]{1,0:T(4,128)S(1)}, f32[4,128]{1,0:T(4,128)S(1)}, u32[]{:S(2)}, u32[]{:S(2)}) collective-permute-start(f32[4,128]{1,0:T(4,128)S(1)} %get-tuple-element.36.refs_4_), channel_id=1, source_target_pairs={{0,2},{1,3},{2,0},{3,1},{4,6},{5,7},{6,4},{7,5},{8,10},{9,11},{10,... | collective-permute-start | bytes 6152 | tf_op jit(solution)/shard_map/ppermute | solution.py:60
  32.7 0.0 collective-permute-start.9
  32.7 0.0 collective-permute-done.6.refs_1_
  32.7 0.0 collective-permute-start.8
  32.8 0.0 copy-done.1
  32.8 0.0 copy-done.2
  32.8 1.7 %shard_map.101 = (f32[512,128]{1,0:T(8,128)S(1)}, bf16[128,512]{1,0:T(8,128)(2,1)S(1)}, bf16[512,128]{1,0:T(8,128)(2,1)S(1)}, f32[128,512]{1,0:T(8,128)S(1)}, f3...) custom-call(bf16[128,1280]{1,0:T(8,128)(2,1)S(1)} %get-tuple-element.27.refs_0_, ...), custom_call_target="tpu_custom_call" | custom-call | flops 671088640 | bytes 3276800 | tf_op jit(solution)/shard_map/pallas_call | solution.py:34
  34.4 0.0 collective-permute-done.7.refs_2_
  34.4 0.0 collective-permute-done.11.refs_7_
  34.4 0.4 collective-permute-done.10.refs_6_
  34.8 1.5 %collective-permute-done.9.refs_5_ = f32[4,128]{1,0:T(4,128)S(1)} collective-permute-done((f32[4,128]{1,0:T(4,128)S(1)}, f32[4,128]{1,0:T(4,128)S(1)}, u32[]{:S(2)}, u32[]{:S(2)}) %collective-permute-start.9) | collective-permute-done | bytes 2080 | tf_op jit(solution)/shard_map/ppermute | solution.py:60
  36.3 0.0 collective-permute-done.8.refs_3_
  36.3 0.9 %shard_map.102 = (f32[128,128]{1,0:T(8,128)S(1)}, f32[128,128]{1,0:T(8,128)S(1)}, bf16[256,128]{1,0:T(8,128)(2,1)S(1)}, f32[128,128]{1,0:T(8,128)S(1)}, bf16[128...) custom-call(f32[4,128]{1,0:T(4,128)S(1)} %get-tuple-element.35.refs_0_, ...), custom_call_target="tpu_custom_call" | custom-call | flops 134217728 | bytes 1851392 | tf_op jit(solution)/shard_map/pallas_call | solution.py:34
  37.2 0.1 collective-permute-start.12
  37.3 1.2 %collective-permute-done.12.refs_1_ = bf16[256,128]{1,0:T(8,128)(2,1)S(1)} collective-permute-done((bf16[256,128]{1,0:T(8,128)(2,1)S(1)}, bf16[256,128]{1,0:T(8,128)(2,1)S(1)}, u32[]{:S(2)}, u32[]{:S(2)}) %collective-permute-start.12) | collective-permute-done | bytes 65568 | tf_op jit(solution)/shard_map/ppermute | solution.py:60
  38.5 0.3 collective-permute-start.13
  38.8 1.7 %collective-permute-start.14 = (bf16[128,128]{1,0:T(8,128)(2,1)S(1)}, bf16[128,128]{1,0:T(8,128)(2,1)S(1)}, u32[]{:S(2)}, u32[]{:S(2)}) collective-permute-start(bf16[128,128]{1,0:T(8,128)(2,1)S(1)} %get-tuple-element.47), channel_id=1, source_target_pairs={{0,4},{1,5},{2,6},{3,7},{4,0},{5,1},{6,2},{7,3},{8,12},{9,13},{10,... | collective-permute-start | bytes 98312 | tf_op jit(solution)/shard_map/ppermute | solution.py:60
  40.5 0.5 %collective-permute-start.15 = (bf16[128,128]{1,0:T(8,128)(2,1)S(1)}, bf16[128,128]{1,0:T(8,128)(2,1)S(1)}, u32[]{:S(2)}, u32[]{:S(2)}) collective-permute-start(bf16[128,128]{1,0:T(8,128)(2,1)S(1)} %shard_map.105), channel_id=1, source_target_pairs={{0,2},{1,3},{2,0},{3,1},{4,6},{5,7},{6,4},{7,5},{8,10},{9,11},{10,... | collective-permute-start | bytes 98312 | tf_op jit(solution)/shard_map/ppermute | solution.py:60
  41.0 1.3 %collective-permute-start.16 = (bf16[128,128]{1,0:T(8,128)(2,1)S(1)}, bf16[128,128]{1,0:T(8,128)(2,1)S(1)}, u32[]{:S(2)}, u32[]{:S(2)}) collective-permute-start(bf16[128,128]{1,0:T(8,128)(2,1)S(1)} %shard_map.106), channel_id=1, source_target_pairs={{0,6},{1,7},{2,4},{3,5},{4,2},{5,3},{6,0},{7,1},{8,14},{9,15},{10,... | collective-permute-start | bytes 98312 | tf_op jit(solution)/shard_map/ppermute | solution.py:60
  42.3 1.3 %collective-permute-done.13.refs_2_ = bf16[128,128]{1,0:T(8,128)(2,1)S(1)} collective-permute-done((bf16[128,128]{1,0:T(8,128)(2,1)S(1)}, bf16[128,128]{1,0:T(8,128)(2,1)S(1)}, u32[]{:S(2)}, u32[]{:S(2)}) %collective-permute-start.13) | collective-permute-done | bytes 32800 | tf_op jit(solution)/shard_map/ppermute | solution.py:60
  43.6 1.1 %shard_map.104 = bf16[128,4096]{1,0:T(8,128)(2,1)} custom-call(f32[128,128]{1,0:T(8,128)S(1)} %get-tuple-element.42.refs_0_, bf16[256,128]{1,0:T(8,128)(2,1)S(1)} %collective-permute-done.12.refs_1_, bf16[128,128]{1,0:T(8,128)(2,1)S(1)} %collective-permute-done.13.refs_2_, f32[128,128]{1,0:T(8,128)S(1)} %get-tuple-element.45.refs_3_, ...), custom_call_target="tpu_custom_call" | custom-call | flops 524288 | bytes 3145728 | tf_op jit(solution)/shard_map/pallas_call | solution.py:299
  44.7 0.0 collective-permute-done.14.refs_1_
  44.7 0.0 collective-permute-done.15.refs_2_
  44.7 1.1 %collective-permute-done.16.refs_3_ = bf16[128,128]{1,0:T(8,128)(2,1)S(1)} collective-permute-done((bf16[128,128]{1,0:T(8,128)(2,1)S(1)}, bf16[128,128]{1,0:T(8,128)(2,1)S(1)}, u32[]{:S(2)}, u32[]{:S(2)}) %collective-permute-start.16) | collective-permute-done | bytes 32800 | tf_op jit(solution)/shard_map/ppermute | solution.py:60
  45.8 1.1 %shard_map.107 = bf16[128,4096]{1,0:T(8,128)(2,1)} custom-call(f32[128,128]{1,0:T(8,128)S(1)} %get-tuple-element.46.refs_0_, bf16[128,128]{1,0:T(8,128)(2,1)S(1)} %collective-permute-done.14.refs_1_, bf16[128,128]{1,0:T(8,128)(2,1)S(1)} %collective-permute-done.15.refs_2_, bf16[128,128]{1,0:T(8,128)(2,1)S(1)} %collective-permute-done.16.refs_3_, ...), custom_call_target="tpu_custom_call" | custom-call | flops 524288 | bytes 3145728 | tf_op jit(solution)/shard_map/pallas_call | solution.py:299
  (5 shorter events, 0.0 us)
Async XLA Ops:
  0.6 13.3 %collective-permute-start.2 = (bf16[128,1280]{1,0:T(8,128)(2,1)}, bf16[128,1280]{1,0:T(8,128)(2,1)S(1)}, u32[]{:S(2)}, u32[]{:S(2)}) collective-permute-start(bf16[128,1280]{1,0:T(8,128)(2,1)} %refs_1_.3), channel_id=1, source_target_pairs={{0,4},{1,5},{2,6},{3,7},{4,0},{5,1},{6,2},{7,3},{8,12},{9,13},{10,... | collective-permute-start | bytes 983048 | tf_op jit(solution)/shard_map/ppermute | solution.py:60
  3.7 13.5 %collective-permute-start.3 = (bf16[128,1280]{1,0:T(8,128)(2,1)}, bf16[128,1280]{1,0:T(8,128)(2,1)S(1)}, u32[]{:S(2)}, u32[]{:S(2)}) collective-permute-start(bf16[128,1280]{1,0:T(8,128)(2,1)} %refs_1_.3), channel_id=1, source_target_pairs={{0,2},{1,3},{2,0},{3,1},{4,6},{5,7},{6,4},{7,5},{8,10},{9,11},{10,... | collective-permute-start | bytes 983048 | tf_op jit(solution)/shard_map/ppermute | solution.py:60
  8.1 12.7 %copy-start = (bf16[128,1664]{1,0:T(8,128)(2,1)S(1)}, bf16[128,1664]{1,0:T(8,128)(2,1)}, u32[]{:S(2)}) copy-start(bf16[128,1664]{1,0:T(8,128)(2,1)} %refs_0_.5) | copy-start | bytes 1277956
  8.1 12.7 %copy-start.3 = (bf16[128,1280]{1,0:T(8,128)(2,1)S(1)}, bf16[128,1280]{1,0:T(8,128)(2,1)}, u32[]{:S(2)}) copy-start(bf16[128,1280]{1,0:T(8,128)(2,1)} %refs_1_.3) | copy-start | bytes 983044
  8.1 12.7 %copy-start.4 = (bf16[1664,32]{0,1:T(8,128)(2,1)S(1)}, bf16[1664,32]{0,1:T(8,128)(2,1)}, u32[]{:S(2)}) copy-start(bf16[1664,32]{0,1:T(8,128)(2,1)} %param.12) | copy-start | bytes 319492
  8.1 12.7 %copy-start.5 = (bf16[1280,32]{0,1:T(8,128)(2,1)S(1)}, bf16[1280,32]{0,1:T(8,128)(2,1)}, u32[]{:S(2)}) copy-start(bf16[1280,32]{0,1:T(8,128)(2,1)} %param.14) | copy-start | bytes 245764
  8.1 16.9 %collective-permute-start = (bf16[128,1280]{1,0:T(8,128)(2,1)S(1)}, bf16[128,1280]{1,0:T(8,128)(2,1)S(1)}, u32[]{:S(2)}, u32[]{:S(2)}) collective-permute-start(bf16[128,1280]{1,0:T(8,128)(2,1)S(1)} %get-tuple-element.27.refs_0_), channel_id=1, source_target_pairs={{0,8},{1,9},{2,10},{3,11},{4,12},{5,13},{6,14},{7,15},{8,0},{9,1},... | collective-permute-start | bytes 983048 | tf_op jit(solution)/shard_map/ppermute | solution.py:60
  10.8 15.1 %collective-permute-start.1 = (bf16[128,1280]{1,0:T(8,128)(2,1)S(1)}, bf16[128,1280]{1,0:T(8,128)(2,1)S(1)}, u32[]{:S(2)}, u32[]{:S(2)}) collective-permute-start(bf16[128,1280]{1,0:T(8,128)(2,1)S(1)} %get-tuple-element.27.refs_0_), channel_id=1, source_target_pairs={{0,1},{1,0},{2,3},{3,2},{4,5},{5,4},{6,7},{7,6},{8,9},{9,8},{10,11... | collective-permute-start | bytes 983048 | tf_op jit(solution)/shard_map/ppermute | solution.py:60
  13.9 11.2 %collective-permute-start.5 = (bf16[128,1280]{1,0:T(8,128)(2,1)S(1)}, bf16[128,1280]{1,0:T(8,128)(2,1)S(1)}, u32[]{:S(2)}, u32[]{:S(2)}) collective-permute-start(bf16[128,1280]{1,0:T(8,128)(2,1)S(1)} %collective-permute-done.2.refs_1_), channel_id=1, source_target_pairs={{0,2},{1,3},{2,0},{3,1},{4,6},{5,7},{6,4},{7,5},{8,10},{9,11},{10,... | collective-permute-start | bytes 983048 | tf_op jit(solution)/shard_map/ppermute | solution.py:60
  25.1 1.7 %collective-permute-start.4 = (bf16[128,1280]{1,0:T(8,128)(2,1)S(1)}, bf16[128,1280]{1,0:T(8,128)(2,1)S(1)}, u32[]{:S(2)}, u32[]{:S(2)}) collective-permute-start(bf16[128,1280]{1,0:T(8,128)(2,1)S(1)} %shard_map.98), channel_id=1, source_target_pairs={{0,1},{1,0},{2,3},{3,2},{4,5},{5,4},{6,7},{7,6},{8,9},{9,8},{10,11... | collective-permute-start | bytes 983048 | tf_op jit(solution)/shard_map/ppermute | solution.py:60
  25.2 7.6 %copy-start.1 = (bf16[1280,128]{1,0:T(8,128)(2,1)S(1)}, bf16[1280,128]{1,0:T(8,128)(2,1)}, u32[]{:S(2)}) copy-start(bf16[1280,128]{1,0:T(8,128)(2,1)} %refs_8_.1) | copy-start | bytes 983044
  25.2 7.6 %copy-start.2 = (bf16[1280,128]{1,0:T(8,128)(2,1)S(1)}, bf16[1280,128]{1,0:T(8,128)(2,1)}, u32[]{:S(2)}) copy-start(bf16[1280,128]{1,0:T(8,128)(2,1)} %refs_9_.1) | copy-start | bytes 983044
  28.2 4.6 %collective-permute-start.6 = (f32[4,128]{1,0:T(4,128)S(1)}, f32[4,128]{1,0:T(4,128)S(1)}, u32[]{:S(2)}, u32[]{:S(2)}) collective-permute-start(f32[4,128]{1,0:T(4,128)S(1)} %get-tuple-element.35.refs_0_), channel_id=1, source_target_pairs={{0,8},{1,9},{2,10},{3,11},{4,12},{5,13},{6,14},{7,15},{8,0},{9,1},... | collective-permute-start | bytes 6152 | tf_op jit(solution)/shard_map/ppermute | solution.py:60
  28.2 6.2 %collective-permute-start.7 = (f32[4,128]{1,0:T(4,128)S(1)}, f32[4,128]{1,0:T(4,128)S(1)}, u32[]{:S(2)}, u32[]{:S(2)}) collective-permute-start(f32[4,128]{1,0:T(4,128)S(1)} %get-tuple-element.35.refs_0_), channel_id=1, source_target_pairs={{0,1},{1,0},{2,3},{3,2},{4,5},{5,4},{6,7},{7,6},{8,9},{9,8},{10,11... | collective-permute-start | bytes 6152 | tf_op jit(solution)/shard_map/ppermute | solution.py:60
  28.4 6.0 %collective-permute-start.11 = (f32[4,128]{1,0:T(4,128)S(1)}, f32[4,128]{1,0:T(4,128)S(1)}, u32[]{:S(2)}, u32[]{:S(2)}) collective-permute-start(f32[4,128]{1,0:T(4,128)S(1)} %get-tuple-element.36.refs_4_), channel_id=1, source_target_pairs={{0,6},{1,7},{2,4},{3,5},{4,2},{5,3},{6,0},{7,1},{8,14},{9,15},{10,... | collective-permute-start | bytes 6152 | tf_op jit(solution)/shard_map/ppermute | solution.py:60
  31.2 3.6 %collective-permute-start.10 = (f32[4,128]{1,0:T(4,128)S(1)}, f32[4,128]{1,0:T(4,128)S(1)}, u32[]{:S(2)}, u32[]{:S(2)}) collective-permute-start(f32[4,128]{1,0:T(4,128)S(1)} %get-tuple-element.36.refs_4_), channel_id=1, source_target_pairs={{0,2},{1,3},{2,0},{3,1},{4,6},{5,7},{6,4},{7,5},{8,10},{9,11},{10,... | collective-permute-start | bytes 6152 | tf_op jit(solution)/shard_map/ppermute | solution.py:60
  32.7 3.6 %collective-permute-start.9 = (f32[4,128]{1,0:T(4,128)S(1)}, f32[4,128]{1,0:T(4,128)S(1)}, u32[]{:S(2)}, u32[]{:S(2)}) collective-permute-start(f32[4,128]{1,0:T(4,128)S(1)} %get-tuple-element.36.refs_4_), channel_id=1, source_target_pairs={{0,4},{1,5},{2,6},{3,7},{4,0},{5,1},{6,2},{7,3},{8,12},{9,13},{10,... | collective-permute-start | bytes 6152 | tf_op jit(solution)/shard_map/ppermute | solution.py:60
  32.7 3.6 %collective-permute-start.8 = (f32[4,128]{1,0:T(4,128)S(1)}, f32[4,128]{1,0:T(4,128)S(1)}, u32[]{:S(2)}, u32[]{:S(2)}) collective-permute-start(f32[4,128]{1,0:T(4,128)S(1)} %collective-permute-done.6.refs_1_), channel_id=1, source_target_pairs={{0,1},{1,0},{2,3},{3,2},{4,5},{5,4},{6,7},{7,6},{8,9},{9,8},{10,11... | collective-permute-start | bytes 6152 | tf_op jit(solution)/shard_map/ppermute | solution.py:60
  37.2 1.3 %collective-permute-start.12 = (bf16[256,128]{1,0:T(8,128)(2,1)S(1)}, bf16[256,128]{1,0:T(8,128)(2,1)S(1)}, u32[]{:S(2)}, u32[]{:S(2)}) collective-permute-start(bf16[256,128]{1,0:T(8,128)(2,1)S(1)} %get-tuple-element.43), channel_id=1, source_target_pairs={{0,1},{1,0},{2,3},{3,2},{4,5},{5,4},{6,7},{7,6},{8,9},{9,8},{10,11... | collective-permute-start | bytes 196616 | tf_op jit(solution)/shard_map/ppermute | solution.py:60
  38.5 5.1 %collective-permute-start.13 = (bf16[128,128]{1,0:T(8,128)(2,1)S(1)}, bf16[128,128]{1,0:T(8,128)(2,1)S(1)}, u32[]{:S(2)}, u32[]{:S(2)}) collective-permute-start(bf16[128,128]{1,0:T(8,128)(2,1)S(1)} %shard_map.103.refs_1_), channel_id=1, source_target_pairs={{0,8},{1,9},{2,10},{3,11},{4,12},{5,13},{6,14},{7,15},{8,0},{9,1},... | collective-permute-start | bytes 98312 | tf_op jit(solution)/shard_map/ppermute | solution.py:60
  38.8 5.9 %collective-permute-start.14 = (bf16[128,128]{1,0:T(8,128)(2,1)S(1)}, bf16[128,128]{1,0:T(8,128)(2,1)S(1)}, u32[]{:S(2)}, u32[]{:S(2)}) collective-permute-start(bf16[128,128]{1,0:T(8,128)(2,1)S(1)} %get-tuple-element.47), channel_id=1, source_target_pairs={{0,4},{1,5},{2,6},{3,7},{4,0},{5,1},{6,2},{7,3},{8,12},{9,13},{10,... | collective-permute-start | bytes 98312 | tf_op jit(solution)/shard_map/ppermute | solution.py:60
  40.5 4.2 %collective-permute-start.15 = (bf16[128,128]{1,0:T(8,128)(2,1)S(1)}, bf16[128,128]{1,0:T(8,128)(2,1)S(1)}, u32[]{:S(2)}, u32[]{:S(2)}) collective-permute-start(bf16[128,128]{1,0:T(8,128)(2,1)S(1)} %shard_map.105), channel_id=1, source_target_pairs={{0,2},{1,3},{2,0},{3,1},{4,6},{5,7},{6,4},{7,5},{8,10},{9,11},{10,... | collective-permute-start | bytes 98312 | tf_op jit(solution)/shard_map/ppermute | solution.py:60
  41.0 4.8 %collective-permute-start.16 = (bf16[128,128]{1,0:T(8,128)(2,1)S(1)}, bf16[128,128]{1,0:T(8,128)(2,1)S(1)}, u32[]{:S(2)}, u32[]{:S(2)}) collective-permute-start(bf16[128,128]{1,0:T(8,128)(2,1)S(1)} %shard_map.106), channel_id=1, source_target_pairs={{0,6},{1,7},{2,4},{3,5},{4,2},{5,3},{6,0},{7,1},{8,14},{9,15},{10,... | collective-permute-start | bytes 98312 | tf_op jit(solution)/shard_map/ppermute | solution.py:60

commit v5 on v4

--- a/solution.py
+++ b/solution.py
@@ -158,9 +158,14 @@
     return jnp.broadcast_to(row, (LANES, LANES)).T
 
 
+def lse_parts(scores, axis):
+    top = jnp.max(scores, axis=axis, keepdims=True)
+    return top, jnp.sum(jnp.exp(scores - top), axis=axis, keepdims=True)
+
+
 def scores_kernel(ni, nt, *refs):
     images, texts = refs[:ni], refs[ni : ni + nt]
-    raw, row_lse, col_lse, all_images, all_texts = refs[ni + nt :]
+    raw, row_lse, col_top, col_total, all_images, all_texts = refs[ni + nt :]
     rows = images[0].shape[0]
     for a in range(ni):
         all_images[a * rows : (a + 1) * rows] = images[a][...]
@@ -168,14 +173,27 @@
         all_texts[t * rows : (t + 1) * rows] = texts[t][...]
     raw[...] = dot(all_images[...], all_texts[...], 1, 1)
     for a in range(ni):
-        scores = LOGIT_SCALE * raw[a * rows : (a + 1) * rows]
-        top = jnp.max(scores, axis=1, keepdims=True)
-        lse = top + jnp.log(jnp.sum(jnp.exp(scores - top), axis=1, keepdims=True))
-        row_lse[a : a + 1] = jnp.broadcast_to(lse, (rows, LANES)).T[:1]
-    for t in range(nt):
-        scores = LOGIT_SCALE * raw[:, t * rows : (t + 1) * rows]
-        top = jnp.max(scores, axis=0, keepdims=True)
-        col_lse[t : t + 1] = top + jnp.log(jnp.sum(jnp.exp(scores - top), axis=0, keepdims=True))
+        top, total = lse_parts(LOGIT_SCALE * raw[a * rows : (a + 1) * rows], 1)
+        row_lse[a : a + 1] = jnp.broadcast_to(top + jnp.log(total), (rows, LANES)).T[:1]
+    for t in range(nt):
+        col_top[t : t + 1], col_total[t : t + 1] = lse_parts(LOGIT_SCALE * raw[:, t * rows : (t + 1) * rows], 0)
+
+
+def last_scores_kernel(ni, nt, *refs):
+    image, texts, (rows_lse, tops, totals) = refs[0], refs[1 : 1 + nt], refs[1 + nt : 4 + nt]
+    raw, row_lse, col_lse, all_texts = refs[4 + nt :]
+    rows = image.shape[0]
+    for t in range(nt):
+        all_texts[t * rows : (t + 1) * rows] = texts[t][...]
+    raw[...] = dot(image[...], all_texts[...], 1, 1)
+    top, total = lse_parts(LOGIT_SCALE * raw[...], 1)
+    row_lse[: ni - 1] = rows_lse[...]
+    row_lse[ni - 1 :] = jnp.broadcast_to(top + jnp.log(total), (rows, LANES)).T[:1]
+    for t in range(nt):
+        top, total = lse_parts(LOGIT_SCALE * raw[:, t * rows : (t + 1) * rows], 0)
+        high = jnp.maximum(top, tops[t : t + 1])
+        total = total * jnp.exp(top - high) + totals[t : t + 1] * jnp.exp(tops[t : t + 1] - high)
+        col_lse[t : t + 1] = high + jnp.log(total)
 
 
 def factors_kernel(ni, nt, *refs):
@@ -205,15 +223,25 @@
     txt_base[...] = 2.0 * (diagonal * own_txt_side - own_img_side)
 
 
-def merge(parts):
+def merge(parts, flips):
     slots = parts[0].shape[0]
     lined = [parts[0][...]]
     for k in range(1, len(parts)):
         lined.append(
-            jnp.concatenate([parts[k][s ^ k : (s ^ k) + 1] for s in range(slots)], axis=0)
+            jnp.concatenate([parts[k][s ^ flips[k] :][:1] for s in range(slots)], axis=0)
         )
     top = functools.reduce(jnp.maximum, lined)
     return top + jnp.log(sum(jnp.exp(p - top) for p in lined))
+
+
+def merge_kernel(flips, *refs):
+    refs[-1][...] = merge(refs[:-1], flips)
+
+
+def gather_lse(lse, bits, n):
+    for j, bit in enumerate(bits[:-1]):
+        (lse,) = call(functools.partial(merge_kernel, (0, 1 << j)), [(lse.shape, F32)], [lse, swap(lse, bit, n)])
+    return [lse, swap(lse, bits[-1], n)], (0, 1 << len(bits) - 1)
 
 
 def add_kernel(count, *refs):
@@ -242,21 +270,22 @@
     return [kept[0], *got], sent
 
 
-def weights_kernel(ni, nt, *refs):
-    row_parts, col_parts = refs[:ni], refs[ni : ni + nt]
-    raw, img_low, img_side_t, txt_low, txt_side_t = refs[ni + nt : ni + nt + 5]
+def weights_kernel(ni, nt, row_flips, col_flips, *refs):
+    row_parts, refs = refs[: len(row_flips)], refs[len(row_flips) :]
+    col_parts, refs = refs[: len(col_flips)], refs[len(col_flips) :]
+    raw, last_raw, img_low, txt_low = refs[:4]
     half = ni // 2
-    img_kept, img_sent = refs[ni + nt + 5 : ni + nt + 5 + half], refs[ni + nt + 5 + half]
-    txt_parts, weights_bf = refs[-1 - nt : -1], refs[-1]
+    *img_kept, img_sent, weights_bf, inners = refs[4:]
     rows = LANES
-    row_lse = merge(row_parts)
-    col_lse = merge(col_parts)
+    row_lse = merge(row_parts, row_flips)
+    col_lse = merge(col_parts, col_flips)
     inner_col = [jnp.zeros((1, rows), F32) for _ in range(nt)]
     for a in range(ni):
         row = column_of(row_lse[a : a + 1])
         inner_row = jnp.zeros((rows, rows), F32)
         for t in range(nt):
-            here = raw[a * rows : (a + 1) * rows, t * rows : (t + 1) * rows]
+            cols = slice(t * rows, (t + 1) * rows)
+            here = raw[a * rows : (a + 1) * rows, cols] if a < ni - 1 else last_raw[:, cols]
             scores = LOGIT_SCALE * here
             weights = jnp.exp(scores - row) + jnp.exp(scores - col_lse[t : t + 1])
             weights_bf[a * rows : (a + 1) * rows, t * rows : (t + 1) * rows] = weights.astype(BF16)
@@ -273,9 +302,18 @@
         else:
             img_sent[(a - half) * rows : (a - half + 1) * rows] = part.astype(img_sent.dtype)
     for t in range(nt):
+        inners[t : t + 1] = inner_col[t]
+
+
+def columns_kernel(nt, weights_bf, inners, img_side_t, txt_side_t, *refs):
+    rows, kept, sent = LANES, refs[:-1], refs[-1]
+    for t in range(nt):
         here = slice(t * rows, (t + 1) * rows)
-        part = dot(img_side_t[...], weights_bf[:, here]) - inner_col[t] * txt_side_t[:, here]
-        txt_parts[t][...] = part.astype(txt_parts[t].dtype)
+        part = dot(img_side_t[...], weights_bf[:, here]) - inners[t : t + 1] * txt_side_t[:, here]
+        if t < nt // 2:
+            kept[t][...] = part
+        else:
+            sent[(t - nt // 2) * rows : (t - nt // 2 + 1) * rows] = part.astype(sent.dtype)
 
 
 def sketch_kernel(count, turned, *refs):
@@ -324,15 +362,22 @@
     )
     images = gather(img_emb, img_bits, n, lambda x: hold(x, [texts[0], img_keys]))
     texts = texts + embed(feats[-1:], w_txt_v)
-    raw, row_lse, col_lse = call(
-        functools.partial(scores_kernel, ni, nt),
-        [((ni * rows, nt * rows), F32), ((ni, rows), F32), ((nt, rows), F32)],
-        images + texts,
-        scratch=[pltpu.VMEM((ni * rows, wide), BF16), pltpu.VMEM((nt * rows, wide), BF16)],
-        flops=2 * ni * nt * rows * rows * wide,
+    raw, rows_lse, tops, totals = call(
+        functools.partial(scores_kernel, ni - 1, nt),
+        [(((ni - 1) * rows, nt * rows), F32), ((ni - 1, rows), F32), ((nt, rows), F32), ((nt, rows), F32)],
+        images[:-1] + texts,
+        scratch=[pltpu.VMEM(((ni - 1) * rows, wide), BF16), pltpu.VMEM((nt * rows, wide), BF16)],
+        flops=2 * (ni - 1) * nt * rows * rows * wide,
+    )
+    last_raw, row_lse, col_lse = call(
+        functools.partial(last_scores_kernel, ni, nt),
+        [((rows, nt * rows), F32), ((ni, rows), F32), ((nt, rows), F32)],
+        images[-1:] + texts + [rows_lse, tops, totals],
+        scratch=[pltpu.VMEM((nt * rows, wide), BF16)],
+        flops=2 * nt * rows * rows * wide,
     )
     row_parts = gather(row_lse, img_bits, n)
-    col_parts = [col_lse] + [swap(col_lse, o, n) for o in txt_span[1:]]
+    col_parts, col_flips = gather_lse(col_lse, txt_bits, n)
     img_low, img_side_t, txt_low, txt_side_t, img_base, txt_base = call(
         functools.partial(factors_kernel, ni, nt),
         [
@@ -347,19 +392,21 @@
         flops=4 * (ni + nt) * rows * wide * low,
     )
     half = ni // 2
-    parts = call(
-        functools.partial(weights_kernel, ni, nt),
+    *img_kept, img_sent, weights_bf, inners = call(
+        functools.partial(weights_kernel, ni, nt, tuple(range(ni)), col_flips),
         [((rows, low), F32)] * half
-        + [((half * rows, low), BF16), ((rows, low), F32)]
-        + [((rows, low), BF16)] * (nt - 1),
-        row_parts + col_parts + [raw, img_low, img_side_t, txt_low, txt_side_t],
-        scratch=[pltpu.VMEM((ni * rows, nt * rows), BF16)],
-        flops=4 * ni * nt * rows * rows * low,
-    )
-    img_parts, last = halve(list(parts[:half]), parts[half], img_bits, n)
-    txt_parts = list(parts[half + 1 :])
-    txt_parts[2:] = [hold(p, [last]) for p in txt_parts[2:]]
-    txt_parts = txt_parts[:1] + [swap(p, o, n) for p, o in zip(txt_parts[1:], txt_span[1:])]
+        + [((half * rows, low), BF16), ((ni * rows, nt * rows), BF16), ((nt, rows), F32)],
+        row_parts + col_parts + [raw, last_raw, img_low, txt_low],
+        flops=2 * ni * nt * rows * rows * low,
+    )
+    *txt_kept, txt_sent = call(
+        functools.partial(columns_kernel, nt),
+        [((rows, low), F32)] * (nt // 2) + [((nt // 2 * rows, low), BF16)],
+        [weights_bf, inners, img_side_t, txt_side_t],
+        flops=2 * ni * nt * rows * rows * low,
+    )
+    img_parts, _ = halve(img_kept, img_sent, img_bits, n)
+    txt_parts, _ = halve(txt_kept, txt_sent, txt_bits, n)
     return (
         sketch(img_parts, img_base, img_keys, False),
         sketch(txt_parts, txt_base, txt_keys, True),

time: 47.1 us -> 46.1 us (0.979)
  waiting for transfers between devices: 11.7 us -> 10.2 us
  Pallas kernels: 15.4 us -> 16.1 us
    ppermute x17 -> x15, waiting for transfers between devices: 11.7 us -> 10.2 us  [swap(): return lax.ppermute(x, 'dp', [(i, i ^ offset) for i in range(n)])]
    pallas_call x6 -> x10, Pallas kernels: 6.77 us -> 7.49 us  [call(): pl.pallas_call(kernel, out_shape=[jax.ShapeDtypeStruct(s, d) for s, d in...]
    ppermute x17 -> x15, starting transfers between devices: 19.1 us -> 18.7 us  [swap(): return lax.ppermute(x, 'dp', [(i, i ^ offset) for i in range(n)])]
  transfers between devices with their start and end apart: 17 -> 15, of which waited for: 8 -> 9; matrix products, arithmetic and copies ran while one was open for 0% -> 0% of each run, Pallas kernels for 25% -> 29%
where the time goes in v5:
time: 46.1 us; the launch traced here: 46 us
  starting transfers between devices  18.7 us (41%)
  Pallas kernels  16.1 us (35%)
  waiting for transfers between devices  10.2 us (22%)
  between operations  0.83 us (2%)
    ppermute x15, starting transfers between devices, swap(): return lax.ppermute(x, 'dp', [(i, i ^ offset) for i in range(n)])  18.7 us
    ppermute x15, waiting for transfers between devices, swap(): return lax.ppermute(x, 'dp', [(i, i ^ offset) for i in range(n)])  10.2 us
    pallas_call x10, Pallas kernels, call(): pl.pallas_call(kernel, out_shape=[jax.ShapeDtypeStruct(s, d) for s, d in...  7.49 us
    pallas_call x2, Pallas kernels, stream_embed(): pl.pallas_call(functools.partial(stream_kernel, blocks, cuts), out_shape=...  6.38 us
    pallas_call x2, Pallas kernels, sketch(): pl.pallas_call(functools.partial(sketch_kernel, len(parts), turned), out_...  2.22 us
  transfers between devices with their start and end apart: 15, of which 9 were waited for; matrix products, arithmetic and copies ran while one was open for 0% of the time, Pallas kernels for 29%

profile of v5, /device:TPU:0, one launch (start us, length us, event | category | flops | bytes accessed | tf_op | source)
XLA Modules:
  0.0 46.0 jit_solution(1177033841040797737)
XLA Ops:
  0.6 3.1 %collective-permute-start.1 = (bf16[128,1280]{1,0:T(8,128)(2,1)}, bf16[128,1280]{1,0:T(8,128)(2,1)S(1)}, u32[]{:S(2)}, u32[]{:S(2)}) collective-permute-start(bf16[128,1280]{1,0:T(8,128)(2,1)} %refs_1_.3), channel_id=1, source_target_pairs={{0,4},{1,5},{2,6},{3,7},{4,0},{5,1},{6,2},{7,3},{8,12},{9,13},{10,... | collective-permute-start | bytes 983048 | tf_op jit(solution)/shard_map/ppermute | solution.py:60
  3.7 1.5 %collective-permute-start.2 = (bf16[128,1280]{1,0:T(8,128)(2,1)}, bf16[128,1280]{1,0:T(8,128)(2,1)S(1)}, u32[]{:S(2)}, u32[]{:S(2)}) collective-permute-start(bf16[128,1280]{1,0:T(8,128)(2,1)} %refs_1_.3), channel_id=1, source_target_pairs={{0,2},{1,3},{2,0},{3,1},{4,6},{5,7},{6,4},{7,5},{8,10},{9,11},{10,... | collective-permute-start | bytes 983048 | tf_op jit(solution)/shard_map/ppermute | solution.py:60
  5.2 2.8 %shard_map.95 = (bf16[128,1280]{1,0:T(8,128)(2,1)S(1)}, f32[128,1]{1,0:T(8,128)S(1)}) custom-call(bf16[128,1664]{1,0:T(8,128)(2,1)} %refs_0_.5, bf16[1664,1280]{1,0:T(8,128)(2,1)} %refs_1_.2), custom_call_target="tpu_custom_call" | custom-call | flops 545259520 | bytes 4259840 | tf_op jit(solution)/shard_map/pallas_call | solution.py:123
  8.1 0.0 copy-start
  8.1 0.0 copy-start.3
  8.1 0.0 copy-start.4
  8.1 0.0 copy-start.5
  8.1 2.7 %collective-permute-start = (bf16[128,1280]{1,0:T(8,128)(2,1)S(1)}, bf16[128,1280]{1,0:T(8,128)(2,1)S(1)}, u32[]{:S(2)}, u32[]{:S(2)}) collective-permute-start(bf16[128,1280]{1,0:T(8,128)(2,1)S(1)} %get-tuple-element.32.refs_0_), channel_id=1, source_target_pairs={{0,8},{1,9},{2,10},{3,11},{4,12},{5,13},{6,14},{7,15},{8,0},{9,1},... | collective-permute-start | bytes 983048 | tf_op jit(solution)/shard_map/ppermute | solution.py:60
  10.8 0.0 collective-permute-start.5
  10.8 3.2 %collective-permute-done.1.refs_1_ = bf16[128,1280]{1,0:T(8,128)(2,1)S(1)} collective-permute-done((bf16[128,1280]{1,0:T(8,128)(2,1)}, bf16[128,1280]{1,0:T(8,128)(2,1)S(1)}, u32[]{:S(2)}, u32[]{:S(2)}) %collective-permute-start.1) | collective-permute-done | bytes 327712 | tf_op jit(solution)/shard_map/ppermute | solution.py:60
  13.9 3.3 %collective-permute-start.4 = (bf16[128,1280]{1,0:T(8,128)(2,1)S(1)}, bf16[128,1280]{1,0:T(8,128)(2,1)S(1)}, u32[]{:S(2)}, u32[]{:S(2)}) collective-permute-start(bf16[128,1280]{1,0:T(8,128)(2,1)S(1)} %collective-permute-done.1.refs_1_), channel_id=1, source_target_pairs={{0,2},{1,3},{2,0},{3,1},{4,6},{5,7},{6,4},{7,5},{8,10},{9,11},{10,... | collective-permute-start | bytes 983048 | tf_op jit(solution)/shard_map/ppermute | solution.py:60
  17.3 0.0 collective-permute-done.2.refs_2_
  17.3 3.5 %shard_map.96 = (bf16[128,1280]{1,0:T(8,128)(2,1)S(1)}, bf16[128,1280]{1,0:T(8,128)(2,1)S(1)}, bf16[128,1280]{1,0:T(8,128)(2,1)S(1)}, f32[128,1]{1,0:T(8,128)S(1)}, bf16[1280,1280]{1,0:T(8,128)(2,1)S(1)}) custom-call(bf16[128,1280]{1,0:T(8,128)(2,1)} %refs_1_.3, bf16[128,1280]{1,0:T(8,128)(2,1)S(1)} %collective-permute-done.1.refs_1_, ...), custom_call_target="tpu_custom_call" | custom-call | flops 1258291200 | bytes 3276800 | tf_op jit(solution)/shard_map/pallas_call | solution.py:123
  20.8 0.0 copy-done
  20.8 0.0 copy-done.3
  20.8 0.0 copy-done.4
  20.9 0.0 copy-done.5
  20.9 2.1 %shard_map.97 = (f32[128,4096]{1,0:T(8,128)S(1)}, f32[128,4096]{1,0:T(8,128)S(1)}) custom-call(bf16[128,1664]{1,0:T(8,128)(2,1)S(1)} %copy-done, bf16[128,1280]{1,0:T(8,128)(2,1)S(1)} %copy-done.3, bf16[32,1664]{1,0:T(8,128)(2,1)S(1)} %bitcast.2, bf16[32,1280]{1,0:T(8,128)(2,1)S(1)} %bitcast.3, f32[128,1]{1,0:T(8,128)S(1)} %get-tuple-element.34.refs_4_, ...), custom_call_target="tpu_custom_call" | custom-call | bytes 943104 | tf_op jit(solution)/shard_map/pallas_call | solution.py:34
  23.0 2.1 %collective-permute-done.refs_1_ = bf16[128,1280]{1,0:T(8,128)(2,1)S(1)} collective-permute-done((bf16[128,1280]{1,0:T(8,128)(2,1)S(1)}, bf16[128,1280]{1,0:T(8,128)(2,1)S(1)}, u32[]{:S(2)}, u32[]{:S(2)}) %collective-permute-start) | collective-permute-done | bytes 327712 | tf_op jit(solution)/shard_map/ppermute | solution.py:60
  25.1 0.1 collective-permute-start.3
  25.2 0.0 collective-permute-done.4.refs_0_
  25.2 0.0 copy-start.1
  25.2 0.0 copy-start.2
  25.2 0.7 %shard_map.99.refs_6_.refs_4_.refs_7_ = bf16[128,1280]{1,0:T(8,128)(2,1)S(1)} custom-call(bf16[128,1280]{1,0:T(8,128)(2,1)S(1)} %collective-permute-done.4.refs_0_, bf16[1280,1280]{1,0:T(8,128)(2,1)S(1)} %get-tuple-element.39.refs_1_), custom_call_target="tpu_custom_call" | custom-call | flops 419430400 | bytes 3604480 | tf_op jit(solution)/shard_map/pallas_call | solution.py:34
  25.9 0.0 collective-permute-done.5.refs_2_
  25.9 1.1 %shard_map.100 = (f32[384,512]{1,0:T(8,128)S(1)}, f32[3,128]{1,0:T(4,128)S(1)}, f32[4,128]{1,0:T(4,128)S(1)}, f32[4,128]{1,0:T(4,128)S(1)}) custom-call(bf16[128,1280]{1,0:T(8,128)(2,1)S(1)} %get-tuple-element.32.refs_0_, bf16[128,1280]{1,0:T(8,128)(2,1)S(1)} %collective-permute-done.refs_1_, bf16[128,1280]{1,0:T(8,128)(2,1)S(1)} %collective-permute-done.5.refs_2_, ...), custom_call_target="tpu_custom_call" | custom-call | flops 503316480 | bytes 2293760 | tf_op jit(solution)/shard_map/pallas_call | solution.py:34
  27.1 0.0 collective-permute-done.3.refs_0_.refs_3_
  27.1 0.8 %shard_map.101 = (f32[128,512]{1,0:T(8,128)S(1)}, f32[4,128]{1,0:T(4,128)S(1)}, f32[4,128]{1,0:T(4,128)S(1)}) custom-call(bf16[128,1280]{1,0:T(8,128)(2,1)S(1)} %collective-permute-done.3.refs_0_.refs_3_, bf16[128,1280]{1,0:T(8,128)(2,1)S(1)} %get-tuple-element.33.refs_1_.refs_3_.refs_4_, bf16[128,1280]{1,0:T(8,128)(2,1)S(1)} %get-tuple-element.37.refs_4_.refs_2_.refs_5_, ...), custom_call_target="tpu_custom_call" | custom-call | flops 167772160 | bytes 1644032 | tf_op jit(solution)/shard_map/pallas_call | solution.py:34
  27.9 0.0 collective-permute-start.9
  27.9 3.0 %collective-permute-start.6 = (f32[4,128]{1,0:T(4,128)S(1)}, f32[4,128]{1,0:T(4,128)S(1)}, u32[]{:S(2)}, u32[]{:S(2)}) collective-permute-start(f32[4,128]{1,0:T(4,128)S(1)} %get-tuple-element.43.refs_0_), channel_id=1, source_target_pairs={{0,8},{1,9},{2,10},{3,11},{4,12},{5,13},{6,14},{7,15},{8,0},{9,1},... | collective-permute-start | bytes 6152 | tf_op jit(solution)/shard_map/ppermute | solution.py:60
  31.0 0.0 collective-permute-start.7
  31.0 0.5 %collective-permute-done.9.refs_1_ = f32[4,128]{1,0:T(4,128)S(1)} collective-permute-done((f32[4,128]{1,0:T(4,128)S(1)}, f32[4,128]{1,0:T(4,128)S(1)}, u32[]{:S(2)}, u32[]{:S(2)}) %collective-permute-start.9) | collective-permute-done | bytes 2080 | tf_op jit(solution)/shard_map/ppermute | solution.py:60
  31.5 0.6 %collective-permute-start.10 = (f32[4,128]{1,0:T(4,128)S(1)}, f32[4,128]{1,0:T(4,128)S(1)}, u32[]{:S(2)}, u32[]{:S(2)}) collective-permute-start(f32[4,128]{1,0:T(4,128)S(1)} %shard_map.102.refs_4_), channel_id=1, source_target_pairs={{0,2},{1,3},{2,0},{3,1},{4,6},{5,7},{6,4},{7,5},{8,10},{9,11},{10,... | collective-permute-start | bytes 6152 | tf_op jit(solution)/shard_map/ppermute | solution.py:60
  32.1 0.4 collective-permute-done.6.refs_1_
  32.5 0.0 collective-permute-start.8
  32.5 0.0 copy-done.1
  32.5 0.0 copy-done.2
  32.5 1.7 %shard_map.103 = (f32[512,128]{1,0:T(8,128)S(1)}, bf16[128,512]{1,0:T(8,128)(2,1)S(1)}, bf16[512,128]{1,0:T(8,128)(2,1)S(1)}, f32[128,512]{1,0:T(8,128)S(1)}, f3...) custom-call(bf16[128,1280]{1,0:T(8,128)(2,1)S(1)} %get-tuple-element.32.refs_0_, ...), custom_call_target="tpu_custom_call" | custom-call | flops 671088640 | bytes 3276800 | tf_op jit(solution)/shard_map/pallas_call | solution.py:34
  34.2 0.0 collective-permute-done.7.refs_2_
  34.2 0.9 %collective-permute-done.10.refs_5_ = f32[4,128]{1,0:T(4,128)S(1)} collective-permute-done((f32[4,128]{1,0:T(4,128)S(1)}, f32[4,128]{1,0:T(4,128)S(1)}, u32[]{:S(2)}, u32[]{:S(2)}) %collective-permute-start.10) | collective-permute-done | bytes 2080 | tf_op jit(solution)/shard_map/ppermute | solution.py:60
  35.2 0.0 collective-permute-done.8.refs_3_
  35.2 0.7 %shard_map.104 = (f32[128,128]{1,0:T(8,128)S(1)}, f32[128,128]{1,0:T(8,128)S(1)}, bf16[256,128]{1,0:T(8,128)(2,1)S(1)}, bf16[512,512]{1,0:T(8,128)(2,1)S(1)}, f32[4,128]{1,0:T(4,128)S(1)}) custom-call(f32[4,128]{1,0:T(4,128)S(1)} %get-tuple-element.43.refs_0_, f32[4,128]{1,0:T(4,128)S(1)} %collective-permute-done.6.refs_1_, ...), custom_call_target="tpu_custom_call" | custom-call | flops 67108864 | bytes 1454080 | tf_op jit(solution)/shard_map/pallas_call | solution.py:34
  35.9 0.1 collective-permute-start.11
  36.0 0.3 shard_map.107
  36.3 0.7 %collective-permute-start.13 = (bf16[256,128]{1,0:T(8,128)(2,1)S(1)}, bf16[256,128]{1,0:T(8,128)(2,1)S(1)}, u32[]{:S(2)}, u32[]{:S(2)}) collective-permute-start(bf16[256,128]{1,0:T(8,128)(2,1)S(1)} %get-tuple-element.58), channel_id=1, source_target_pairs={{0,2},{1,3},{2,0},{3,1},{4,6},{5,7},{6,4},{7,5},{8,10},{9,11},{10,... | collective-permute-start | bytes 196616 | tf_op jit(solution)/shard_map/ppermute | solution.py:60
  37.0 0.2 collective-permute-done.11.refs_1_
  37.2 2.3 %collective-permute-start.12 = (bf16[128,128]{1,0:T(8,128)(2,1)S(1)}, bf16[128,128]{1,0:T(8,128)(2,1)S(1)}, u32[]{:S(2)}, u32[]{:S(2)}) collective-permute-start(bf16[128,128]{1,0:T(8,128)(2,1)S(1)} %shard_map.105), channel_id=1, source_target_pairs={{0,8},{1,9},{2,10},{3,11},{4,12},{5,13},{6,14},{7,15},{8,0},{9,1},... | collective-permute-start | bytes 98312 | tf_op jit(solution)/shard_map/ppermute | solution.py:60
  39.5 1.3 %collective-permute-done.13.refs_1_ = bf16[256,128]{1,0:T(8,128)(2,1)S(1)} collective-permute-done((bf16[256,128]{1,0:T(8,128)(2,1)S(1)}, bf16[256,128]{1,0:T(8,128)(2,1)S(1)}, u32[]{:S(2)}, u32[]{:S(2)}) %collective-permute-start.13) | collective-permute-done | bytes 65568 | tf_op jit(solution)/shard_map/ppermute | solution.py:60
  40.8 1.3 %collective-permute-start.14 = (bf16[128,128]{1,0:T(8,128)(2,1)S(1)}, bf16[128,128]{1,0:T(8,128)(2,1)S(1)}, u32[]{:S(2)}, u32[]{:S(2)}) collective-permute-start(bf16[128,128]{1,0:T(8,128)(2,1)S(1)} %shard_map.108), channel_id=1, source_target_pairs={{0,4},{1,5},{2,6},{3,7},{4,0},{5,1},{6,2},{7,3},{8,12},{9,13},{10,... | collective-permute-start | bytes 98312 | tf_op jit(solution)/shard_map/ppermute | solution.py:60
  42.2 0.6 %collective-permute-done.12.refs_2_ = bf16[128,128]{1,0:T(8,128)(2,1)S(1)} collective-permute-done((bf16[128,128]{1,0:T(8,128)(2,1)S(1)}, bf16[128,128]{1,0:T(8,128)(2,1)S(1)}, u32[]{:S(2)}, u32[]{:S(2)}) %collective-permute-start.12) | collective-permute-done | bytes 32800 | tf_op jit(solution)/shard_map/ppermute | solution.py:60
  42.8 1.1 %shard_map.106 = bf16[128,4096]{1,0:T(8,128)(2,1)} custom-call(f32[128,128]{1,0:T(8,128)S(1)} %get-tuple-element.49.refs_0_, bf16[256,128]{1,0:T(8,128)(2,1)S(1)} %collective-permute-done.11.refs_1_, bf16[128,128]{1,0:T(8,128)(2,1)S(1)} %collective-permute-done.12.refs_2_, f32[128,128]{1,0:T(8,128)S(1)} %get-tuple-element.52.refs_3_, ...), custom_call_target="tpu_custom_call" | custom-call | flops 524288 | bytes 3145728 | tf_op jit(solution)/shard_map/pallas_call | solution.py:337
  43.8 1.0 %collective-permute-done.14.refs_2_ = bf16[128,128]{1,0:T(8,128)(2,1)S(1)} collective-permute-done((bf16[128,128]{1,0:T(8,128)(2,1)S(1)}, bf16[128,128]{1,0:T(8,128)(2,1)S(1)}, u32[]{:S(2)}, u32[]{:S(2)}) %collective-permute-start.14) | collective-permute-done | bytes 32800 | tf_op jit(solution)/shard_map/ppermute | solution.py:60
  44.8 1.1 %shard_map.109 = bf16[128,4096]{1,0:T(8,128)(2,1)} custom-call(f32[128,128]{1,0:T(8,128)S(1)} %get-tuple-element.57.refs_0_, bf16[256,128]{1,0:T(8,128)(2,1)S(1)} %collective-permute-done.13.refs_1_, bf16[128,128]{1,0:T(8,128)(2,1)S(1)} %collective-permute-done.14.refs_2_, f32[128,128]{1,0:T(8,128)S(1)} %get-tuple-element.60.refs_3_, ...), custom_call_target="tpu_custom_call" | custom-call | flops 524288 | bytes 3145728 | tf_op jit(solution)/shard_map/pallas_call | solution.py:337
  (5 shorter events, 0.1 us)
Async XLA Ops:
  0.6 13.3 %collective-permute-start.1 = (bf16[128,1280]{1,0:T(8,128)(2,1)}, bf16[128,1280]{1,0:T(8,128)(2,1)S(1)}, u32[]{:S(2)}, u32[]{:S(2)}) collective-permute-start(bf16[128,1280]{1,0:T(8,128)(2,1)} %refs_1_.3), channel_id=1, source_target_pairs={{0,4},{1,5},{2,6},{3,7},{4,0},{5,1},{6,2},{7,3},{8,12},{9,13},{10,... | collective-permute-start | bytes 983048 | tf_op jit(solution)/shard_map/ppermute | solution.py:60
  3.7 13.5 %collective-permute-start.2 = (bf16[128,1280]{1,0:T(8,128)(2,1)}, bf16[128,1280]{1,0:T(8,128)(2,1)S(1)}, u32[]{:S(2)}, u32[]{:S(2)}) collective-permute-start(bf16[128,1280]{1,0:T(8,128)(2,1)} %refs_1_.3), channel_id=1, source_target_pairs={{0,2},{1,3},{2,0},{3,1},{4,6},{5,7},{6,4},{7,5},{8,10},{9,11},{10,... | collective-permute-start | bytes 983048 | tf_op jit(solution)/shard_map/ppermute | solution.py:60
  8.1 12.7 %copy-start = (bf16[128,1664]{1,0:T(8,128)(2,1)S(1)}, bf16[128,1664]{1,0:T(8,128)(2,1)}, u32[]{:S(2)}) copy-start(bf16[128,1664]{1,0:T(8,128)(2,1)} %refs_0_.5) | copy-start | bytes 1277956
  8.1 12.7 %copy-start.3 = (bf16[128,1280]{1,0:T(8,128)(2,1)S(1)}, bf16[128,1280]{1,0:T(8,128)(2,1)}, u32[]{:S(2)}) copy-start(bf16[128,1280]{1,0:T(8,128)(2,1)} %refs_1_.3) | copy-start | bytes 983044
  8.1 12.7 %copy-start.4 = (bf16[1664,32]{0,1:T(8,128)(2,1)S(1)}, bf16[1664,32]{0,1:T(8,128)(2,1)}, u32[]{:S(2)}) copy-start(bf16[1664,32]{0,1:T(8,128)(2,1)} %param.12) | copy-start | bytes 319492
  8.1 12.7 %copy-start.5 = (bf16[1280,32]{0,1:T(8,128)(2,1)S(1)}, bf16[1280,32]{0,1:T(8,128)(2,1)}, u32[]{:S(2)}) copy-start(bf16[1280,32]{0,1:T(8,128)(2,1)} %param.14) | copy-start | bytes 245764
  8.1 16.9 %collective-permute-start = (bf16[128,1280]{1,0:T(8,128)(2,1)S(1)}, bf16[128,1280]{1,0:T(8,128)(2,1)S(1)}, u32[]{:S(2)}, u32[]{:S(2)}) collective-permute-start(bf16[128,1280]{1,0:T(8,128)(2,1)S(1)} %get-tuple-element.32.refs_0_), channel_id=1, source_target_pairs={{0,8},{1,9},{2,10},{3,11},{4,12},{5,13},{6,14},{7,15},{8,0},{9,1},... | collective-permute-start | bytes 983048 | tf_op jit(solution)/shard_map/ppermute | solution.py:60
  10.8 15.1 %collective-permute-start.5 = (bf16[128,1280]{1,0:T(8,128)(2,1)S(1)}, bf16[128,1280]{1,0:T(8,128)(2,1)S(1)}, u32[]{:S(2)}, u32[]{:S(2)}) collective-permute-start(bf16[128,1280]{1,0:T(8,128)(2,1)S(1)} %get-tuple-element.32.refs_0_), channel_id=1, source_target_pairs={{0,1},{1,0},{2,3},{3,2},{4,5},{5,4},{6,7},{7,6},{8,9},{9,8},{10,11... | collective-permute-start | bytes 983048 | tf_op jit(solution)/shard_map/ppermute | solution.py:60
  13.9 11.2 %collective-permute-start.4 = (bf16[128,1280]{1,0:T(8,128)(2,1)S(1)}, bf16[128,1280]{1,0:T(8,128)(2,1)S(1)}, u32[]{:S(2)}, u32[]{:S(2)}) collective-permute-start(bf16[128,1280]{1,0:T(8,128)(2,1)S(1)} %collective-permute-done.1.refs_1_), channel_id=1, source_target_pairs={{0,2},{1,3},{2,0},{3,1},{4,6},{5,7},{6,4},{7,5},{8,10},{9,11},{10,... | collective-permute-start | bytes 983048 | tf_op jit(solution)/shard_map/ppermute | solution.py:60
  25.1 2.0 %collective-permute-start.3 = (bf16[128,1280]{1,0:T(8,128)(2,1)S(1)}, bf16[128,1280]{1,0:T(8,128)(2,1)S(1)}, u32[]{:S(2)}, u32[]{:S(2)}) collective-permute-start(bf16[128,1280]{1,0:T(8,128)(2,1)S(1)} %shard_map.98), channel_id=1, source_target_pairs={{0,1},{1,0},{2,3},{3,2},{4,5},{5,4},{6,7},{7,6},{8,9},{9,8},{10,11... | collective-permute-start | bytes 983048 | tf_op jit(solution)/shard_map/ppermute | solution.py:60
  25.2 7.3 %copy-start.1 = (bf16[1280,128]{1,0:T(8,128)(2,1)S(1)}, bf16[1280,128]{1,0:T(8,128)(2,1)}, u32[]{:S(2)}) copy-start(bf16[1280,128]{1,0:T(8,128)(2,1)} %refs_8_.1) | copy-start | bytes 983044
  25.2 7.3 %copy-start.2 = (bf16[1280,128]{1,0:T(8,128)(2,1)S(1)}, bf16[1280,128]{1,0:T(8,128)(2,1)}, u32[]{:S(2)}) copy-start(bf16[1280,128]{1,0:T(8,128)(2,1)} %refs_9_.1) | copy-start | bytes 983044
  27.9 3.6 %collective-permute-start.9 = (f32[4,128]{1,0:T(4,128)S(1)}, f32[4,128]{1,0:T(4,128)S(1)}, u32[]{:S(2)}, u32[]{:S(2)}) collective-permute-start(f32[4,128]{1,0:T(4,128)S(1)} %get-tuple-element.44.refs_0_), channel_id=1, source_target_pairs={{0,4},{1,5},{2,6},{3,7},{4,0},{5,1},{6,2},{7,3},{8,12},{9,13},{10,... | collective-permute-start | bytes 6152 | tf_op jit(solution)/shard_map/ppermute | solution.py:60
  27.9 4.6 %collective-permute-start.6 = (f32[4,128]{1,0:T(4,128)S(1)}, f32[4,128]{1,0:T(4,128)S(1)}, u32[]{:S(2)}, u32[]{:S(2)}) collective-permute-start(f32[4,128]{1,0:T(4,128)S(1)} %get-tuple-element.43.refs_0_), channel_id=1, source_target_pairs={{0,8},{1,9},{2,10},{3,11},{4,12},{5,13},{6,14},{7,15},{8,0},{9,1},... | collective-permute-start | bytes 6152 | tf_op jit(solution)/shard_map/ppermute | solution.py:60
  31.0 3.3 %collective-permute-start.7 = (f32[4,128]{1,0:T(4,128)S(1)}, f32[4,128]{1,0:T(4,128)S(1)}, u32[]{:S(2)}, u32[]{:S(2)}) collective-permute-start(f32[4,128]{1,0:T(4,128)S(1)} %get-tuple-element.43.refs_0_), channel_id=1, source_target_pairs={{0,1},{1,0},{2,3},{3,2},{4,5},{5,4},{6,7},{7,6},{8,9},{9,8},{10,11... | collective-permute-start | bytes 6152 | tf_op jit(solution)/shard_map/ppermute | solution.py:60
  31.5 3.7 %collective-permute-start.10 = (f32[4,128]{1,0:T(4,128)S(1)}, f32[4,128]{1,0:T(4,128)S(1)}, u32[]{:S(2)}, u32[]{:S(2)}) collective-permute-start(f32[4,128]{1,0:T(4,128)S(1)} %shard_map.102.refs_4_), channel_id=1, source_target_pairs={{0,2},{1,3},{2,0},{3,1},{4,6},{5,7},{6,4},{7,5},{8,10},{9,11},{10,... | collective-permute-start | bytes 6152 | tf_op jit(solution)/shard_map/ppermute | solution.py:60
  32.5 2.7 %collective-permute-start.8 = (f32[4,128]{1,0:T(4,128)S(1)}, f32[4,128]{1,0:T(4,128)S(1)}, u32[]{:S(2)}, u32[]{:S(2)}) collective-permute-start(f32[4,128]{1,0:T(4,128)S(1)} %collective-permute-done.6.refs_1_), channel_id=1, source_target_pairs={{0,1},{1,0},{2,3},{3,2},{4,5},{5,4},{6,7},{7,6},{8,9},{9,8},{10,11... | collective-permute-start | bytes 6152 | tf_op jit(solution)/shard_map/ppermute | solution.py:60
  35.9 1.3 %collective-permute-start.11 = (bf16[256,128]{1,0:T(8,128)(2,1)S(1)}, bf16[256,128]{1,0:T(8,128)(2,1)S(1)}, u32[]{:S(2)}, u32[]{:S(2)}) collective-permute-start(bf16[256,128]{1,0:T(8,128)(2,1)S(1)} %get-tuple-element.50), channel_id=1, source_target_pairs={{0,1},{1,0},{2,3},{3,2},{4,5},{5,4},{6,7},{7,6},{8,9},{9,8},{10,11... | collective-permute-start | bytes 196616 | tf_op jit(solution)/shard_map/ppermute | solution.py:60
  36.3 4.6 %collective-permute-start.13 = (bf16[256,128]{1,0:T(8,128)(2,1)S(1)}, bf16[256,128]{1,0:T(8,128)(2,1)S(1)}, u32[]{:S(2)}, u32[]{:S(2)}) collective-permute-start(bf16[256,128]{1,0:T(8,128)(2,1)S(1)} %get-tuple-element.58), channel_id=1, source_target_pairs={{0,2},{1,3},{2,0},{3,1},{4,6},{5,7},{6,4},{7,5},{8,10},{9,11},{10,... | collective-permute-start | bytes 196616 | tf_op jit(solution)/shard_map/ppermute | solution.py:60
  37.2 5.5 %collective-permute-start.12 = (bf16[128,128]{1,0:T(8,128)(2,1)S(1)}, bf16[128,128]{1,0:T(8,128)(2,1)S(1)}, u32[]{:S(2)}, u32[]{:S(2)}) collective-permute-start(bf16[128,128]{1,0:T(8,128)(2,1)S(1)} %shard_map.105), channel_id=1, source_target_pairs={{0,8},{1,9},{2,10},{3,11},{4,12},{5,13},{6,14},{7,15},{8,0},{9,1},... | collective-permute-start | bytes 98312 | tf_op jit(solution)/shard_map/ppermute | solution.py:60
  40.8 4.0 %collective-permute-start.14 = (bf16[128,128]{1,0:T(8,128)(2,1)S(1)}, bf16[128,128]{1,0:T(8,128)(2,1)S(1)}, u32[]{:S(2)}, u32[]{:S(2)}) collective-permute-start(bf16[128,128]{1,0:T(8,128)(2,1)S(1)} %shard_map.108), channel_id=1, source_target_pairs={{0,4},{1,5},{2,6},{3,7},{4,0},{5,1},{6,2},{7,3},{8,12},{9,13},{10,... | collective-permute-start | bytes 98312 | tf_op jit(solution)/shard_map/ppermute | solution.py:60

commit v6 on v5

--- a/solution.py
+++ b/solution.py
@@ -60,11 +60,11 @@
     return lax.ppermute(x, "dp", [(i, i ^ offset) for i in range(n)])
 
 
-def gather(block, bits, n, ready=lambda x: x):
-    blocks, sent = [block], [block]
+def gather(block, bits, n, ready=None):
+    blocks = [block]
     for bit in bits:
-        new = [swap(b, bit, n) for b in sent]
-        blocks, sent = blocks + new, sent + [ready(b) for b in new]
+        new = [swap(b, bit, n) for b in blocks]
+        blocks = blocks + (new if ready is None or bit == bits[-1] else [ready(b) for b in new])
     return blocks
 
 
@@ -353,15 +353,17 @@
     img_span, txt_span = span(img_bits), span(txt_bits)
     ni, nt = len(img_span), len(txt_span)
     (img_emb,), img_inv = stream_embed([img_feats], w_img, False)
-    feats = gather(txt_feats, txt_bits, n)
-    texts, txt_inv, w_txt_v = stream_embed(feats[:-1], w_txt, True)
+    far = gather(txt_feats, txt_bits[:-1], n)
+    near = swap(txt_feats, txt_bits[-1], n)
+    (txt_emb,), txt_inv, w_txt_v = stream_embed([txt_feats], w_txt, True)
+    far = [txt_emb] + [embed([x], w_txt_v)[0] for x in far[1:]]
+    texts = far + embed([near], w_txt_v) + [swap(x, txt_bits[-1], n) for x in far[1:]]
     img_keys, txt_keys = call(
         keys_kernel,
         [((rows, a_img.shape[1] * LANES), F32), ((rows, a_txt.shape[1] * LANES), F32)],
         [img_feats, txt_feats, a_img.T, a_txt.T, img_inv, txt_inv],
     )
-    images = gather(img_emb, img_bits, n, lambda x: hold(x, [texts[0], img_keys]))
-    texts = texts + embed(feats[-1:], w_txt_v)
+    images = gather(img_emb, img_bits, n, lambda x: hold(x, [texts[nt // 2], img_keys]))
     raw, rows_lse, tops, totals = call(
         functools.partial(scores_kernel, ni - 1, nt),
         [(((ni - 1) * rows, nt * rows), F32), ((ni - 1, rows), F32), ((nt, rows), F32), ((nt, rows), F32)],

time: 46.1 us -> 45.7 us (level)
  starting transfers between devices: 18.7 us -> 19.2 us
    pallas_call x2, Pallas kernels: 6.38 us -> 5.32 us  [stream_embed(): pl.pallas_call(functools.partial(stream_kernel, blocks, cuts), out_shape=...]
    pallas_call x10 -> x11, Pallas kernels: 7.49 us -> 8.17 us  [call(): pl.pallas_call(kernel, out_shape=[jax.ShapeDtypeStruct(s, d) for s, d in...]
    ppermute x15, starting transfers between devices: 18.7 us -> 19.2 us  [swap(): return lax.ppermute(x, 'dp', [(i, i ^ offset) for i in range(n)])]
    ppermute x15, waiting for transfers between devices: 10.2 us -> 9.77 us  [swap(): return lax.ppermute(x, 'dp', [(i, i ^ offset) for i in range(n)])]
  transfers between devices with their start and end apart: 15 -> 15, of which waited for: 9 -> 10; matrix products, arithmetic and copies ran while one was open for 0% -> 0% of each run, Pallas kernels for 29% -> 29%
where the time goes in v6:
time: 45.7 us; the launch traced here: 45.5 us
  starting transfers between devices  19.2 us (42%)
  Pallas kernels  15.7 us (34%)
  waiting for transfers between devices  9.77 us (21%)
  between operations  0.79 us (2%)
    ppermute x15, starting transfers between devices, swap(): return lax.ppermute(x, 'dp', [(i, i ^ offset) for i in range(n)])  19.2 us
    ppermute x15, waiting for transfers between devices, swap(): return lax.ppermute(x, 'dp', [(i, i ^ offset) for i in range(n)])  9.77 us
    pallas_call x11, Pallas kernels, call(): pl.pallas_call(kernel, out_shape=[jax.ShapeDtypeStruct(s, d) for s, d in...  8.17 us
    pallas_call x2, Pallas kernels, stream_embed(): pl.pallas_call(functools.partial(stream_kernel, blocks, cuts), out_shape=...  5.32 us
    pallas_call x2, Pallas kernels, sketch(): pl.pallas_call(functools.partial(sketch_kernel, len(parts), turned), out_...  2.22 us
  transfers between devices with their start and end apart: 15, of which 10 were waited for; matrix products, arithmetic and copies ran while one was open for 0% of the time, Pallas kernels for 29%

profile of v6, /device:TPU:0, one launch (start us, length us, event | category | flops | bytes accessed | tf_op | source)
XLA Modules:
  0.0 45.5 jit_solution(16038789612385349462)
XLA Ops:
  0.6 3.1 %collective-permute-start.3 = (bf16[128,1280]{1,0:T(8,128)(2,1)}, bf16[128,1280]{1,0:T(8,128)(2,1)S(1)}, u32[]{:S(2)}, u32[]{:S(2)}) collective-permute-start(bf16[128,1280]{1,0:T(8,128)(2,1)} %refs_1_.5), channel_id=1, source_target_pairs={{0,4},{1,5},{2,6},{3,7},{4,0},{5,1},{6,2},{7,3},{8,12},{9,13},{10,... | collective-permute-start | bytes 983048 | tf_op jit(solution)/shard_map/ppermute | solution.py:60
  3.7 1.5 %collective-permute-start.1 = (bf16[128,1280]{1,0:T(8,128)(2,1)}, bf16[128,1280]{1,0:T(8,128)(2,1)S(1)}, u32[]{:S(2)}, u32[]{:S(2)}) collective-permute-start(bf16[128,1280]{1,0:T(8,128)(2,1)} %refs_1_.5), channel_id=1, source_target_pairs={{0,2},{1,3},{2,0},{3,1},{4,6},{5,7},{6,4},{7,5},{8,10},{9,11},{10,... | collective-permute-start | bytes 983048 | tf_op jit(solution)/shard_map/ppermute | solution.py:60
  5.2 2.8 %shard_map.95 = (bf16[128,1280]{1,0:T(8,128)(2,1)S(1)}, f32[128,1]{1,0:T(8,128)S(1)}) custom-call(bf16[128,1664]{1,0:T(8,128)(2,1)} %refs_0_.5, bf16[1664,1280]{1,0:T(8,128)(2,1)} %refs_1_.3), custom_call_target="tpu_custom_call" | custom-call | flops 545259520 | bytes 4259840 | tf_op jit(solution)/shard_map/pallas_call | solution.py:123
  8.1 0.0 copy-start
  8.1 0.0 copy-start.1
  8.1 0.0 copy-start.4
  8.1 0.0 copy-start.5
  8.1 2.7 %collective-permute-start = (bf16[128,1280]{1,0:T(8,128)(2,1)S(1)}, bf16[128,1280]{1,0:T(8,128)(2,1)S(1)}, u32[]{:S(2)}, u32[]{:S(2)}) collective-permute-start(bf16[128,1280]{1,0:T(8,128)(2,1)S(1)} %get-tuple-element.30.refs_0_), channel_id=1, source_target_pairs={{0,8},{1,9},{2,10},{3,11},{4,12},{5,13},{6,14},{7,15},{8,0},{9,1},... | collective-permute-start | bytes 983048 | tf_op jit(solution)/shard_map/ppermute | solution.py:60
  10.8 0.0 collective-permute-start.5
  10.8 2.5 %shard_map.96 = (bf16[128,1280]{1,0:T(8,128)(2,1)S(1)}, f32[128,1]{1,0:T(8,128)S(1)}, bf16[1280,1280]{1,0:T(8,128)(2,1)S(1)}) custom-call(bf16[128,1280]{1,0:T(8,128)(2,1)} %refs_1_.5, bf16[1280,1280]{1,0:T(8,128)(2,1)} %refs_1_.4), custom_call_target="tpu_custom_call" | custom-call | flops 419430400 | bytes 3276800 | tf_op jit(solution)/shard_map/pallas_call | solution.py:123
  13.3 0.7 %collective-permute-done.3.refs_0_ = bf16[128,1280]{1,0:T(8,128)(2,1)S(1)} collective-permute-done((bf16[128,1280]{1,0:T(8,128)(2,1)}, bf16[128,1280]{1,0:T(8,128)(2,1)S(1)}, u32[]{:S(2)}, u32[]{:S(2)}) %collective-permute-start.3) | collective-permute-done | bytes 327712 | tf_op jit(solution)/shard_map/ppermute | solution.py:60
  13.9 0.7 %shard_map.100.refs_4_.refs_2_.refs_5_ = bf16[128,1280]{1,0:T(8,128)(2,1)S(1)} custom-call(bf16[128,1280]{1,0:T(8,128)(2,1)S(1)} %collective-permute-done.3.refs_0_, bf16[1280,1280]{1,0:T(8,128)(2,1)S(1)} %get-tuple-element.31.refs_1_), custom_call_target="tpu_custom_call" | custom-call | flops 419430400 | bytes 3604480 | tf_op jit(solution)/shard_map/pallas_call | solution.py:34
  14.7 3.4 %collective-permute-start.4 = (bf16[128,1280]{1,0:T(8,128)(2,1)S(1)}, bf16[128,1280]{1,0:T(8,128)(2,1)S(1)}, u32[]{:S(2)}, u32[]{:S(2)}) collective-permute-start(bf16[128,1280]{1,0:T(8,128)(2,1)S(1)} %shard_map.100.refs_4_.refs_2_.refs_5_), channel_id=1, source_target_pairs={{0,2},{1,3},{2,0},{3,1},{4,6},{5,7},{6,4},{7,5},{8,10},{9,11},{10,... | collective-permute-start | bytes 983048 | tf_op jit(solution)/shard_map/ppermute | solution.py:60
  18.0 0.0 copy-done
  18.1 0.0 copy-done.1
  18.1 0.0 copy-done.4
  18.1 0.0 copy-done.5
  18.1 2.1 %shard_map.98 = (f32[128,4096]{1,0:T(8,128)S(1)}, f32[128,4096]{1,0:T(8,128)S(1)}) custom-call(bf16[128,1664]{1,0:T(8,128)(2,1)S(1)} %copy-done, bf16[128,1280]{1,0:T(8,128)(2,1)S(1)} %copy-done.1, bf16[32,1664]{1,0:T(8,128)(2,1)S(1)} %bitcast.2, bf16[32,1280]{1,0:T(8,128)(2,1)S(1)} %bitcast.3, f32[128,1]{1,0:T(8,128)S(1)} %get-tuple-element.32.refs_4_, ...), custom_call_target="tpu_custom_call" | custom-call | bytes 943104 | tf_op jit(solution)/shard_map/pallas_call | solution.py:34
  20.2 0.0 collective-permute-done.1.refs_0_
  20.2 0.7 %shard_map.97.refs_1_.refs_5_.refs_3_.refs_6_ = bf16[128,1280]{1,0:T(8,128)(2,1)S(1)} custom-call(bf16[128,1280]{1,0:T(8,128)(2,1)S(1)} %collective-permute-done.1.refs_0_, bf16[1280,1280]{1,0:T(8,128)(2,1)S(1)} %get-tuple-element.31.refs_1_), custom_call_target="tpu_custom_call" | custom-call | flops 419430400 | bytes 3604480 | tf_op jit(solution)/shard_map/pallas_call | solution.py:34
  20.9 4.2 %collective-permute-done.refs_0_ = bf16[128,1280]{1,0:T(8,128)(2,1)S(1)} collective-permute-done((bf16[128,1280]{1,0:T(8,128)(2,1)S(1)}, bf16[128,1280]{1,0:T(8,128)(2,1)S(1)}, u32[]{:S(2)}, u32[]{:S(2)}) %collective-permute-start) | collective-permute-done | bytes 327712 | tf_op jit(solution)/shard_map/ppermute | solution.py:60
  25.1 0.0 copy-start.2
  25.1 0.0 copy-start.3
  25.1 0.0 collective-permute-start.2
  25.1 0.0 collective-permute-done.5.refs_2_
  25.1 0.0 collective-permute-done.4.refs_6_.refs_4_.refs_7_
  25.1 1.1 %shard_map.101 = (f32[384,512]{1,0:T(8,128)S(1)}, f32[3,128]{1,0:T(4,128)S(1)}, f32[4,128]{1,0:T(4,128)S(1)}, f32[4,128]{1,0:T(4,128)S(1)}) custom-call(bf16[128,1280]{1,0:T(8,128)(2,1)S(1)} %get-tuple-element.30.refs_0_, bf16[128,1280]{1,0:T(8,128)(2,1)S(1)} %shard_map.99.refs_1_, bf16[128,1280]{1,0:T(8,128)(2,1)S(1)} %collective-permute-done.5.refs_2_, ...), custom_call_target="tpu_custom_call" | custom-call | flops 503316480 | bytes 2293760 | tf_op jit(solution)/shard_map/pallas_call | solution.py:34
  26.2 0.5 %collective-permute-done.2.refs_0_.refs_3_ = bf16[128,1280]{1,0:T(8,128)(2,1)S(1)} collective-permute-done((bf16[128,1280]{1,0:T(8,128)(2,1)S(1)}, bf16[128,1280]{1,0:T(8,128)(2,1)S(1)}, u32[]{:S(2)}, u32[]{:S(2)}) %collective-permute-start.2) | collective-permute-done | bytes 327712 | tf_op jit(solution)/shard_map/ppermute | solution.py:60
  26.7 0.8 %shard_map.102 = (f32[128,512]{1,0:T(8,128)S(1)}, f32[4,128]{1,0:T(4,128)S(1)}, f32[4,128]{1,0:T(4,128)S(1)}) custom-call(bf16[128,1280]{1,0:T(8,128)(2,1)S(1)} %collective-permute-done.2.refs_0_.refs_3_, bf16[128,1280]{1,0:T(8,128)(2,1)S(1)} %get-tuple-element.35.refs_3_.refs_1_.refs_4_, bf16[128,1280]{1,0:T(8,128)(2,1)S(1)} %shard_map.100.refs_4_.refs_2_.refs_5_, ...), custom_call_target="tpu_custom_call" | custom-call | flops 167772160 | bytes 1644032 | tf_op jit(solution)/shard_map/pallas_call | solution.py:34
  27.5 0.0 collective-permute-start.9
  27.5 3.0 %collective-permute-start.6 = (f32[4,128]{1,0:T(4,128)S(1)}, f32[4,128]{1,0:T(4,128)S(1)}, u32[]{:S(2)}, u32[]{:S(2)}) collective-permute-start(f32[4,128]{1,0:T(4,128)S(1)} %get-tuple-element.39.refs_0_), channel_id=1, source_target_pairs={{0,8},{1,9},{2,10},{3,11},{4,12},{5,13},{6,14},{7,15},{8,0},{9,1},... | collective-permute-start | bytes 6152 | tf_op jit(solution)/shard_map/ppermute | solution.py:60
  30.5 0.0 collective-permute-start.7
  30.5 0.6 %collective-permute-done.9.refs_1_ = f32[4,128]{1,0:T(4,128)S(1)} collective-permute-done((f32[4,128]{1,0:T(4,128)S(1)}, f32[4,128]{1,0:T(4,128)S(1)}, u32[]{:S(2)}, u32[]{:S(2)}) %collective-permute-start.9) | collective-permute-done | bytes 2080 | tf_op jit(solution)/shard_map/ppermute | solution.py:60
  31.1 0.6 %collective-permute-start.10 = (f32[4,128]{1,0:T(4,128)S(1)}, f32[4,128]{1,0:T(4,128)S(1)}, u32[]{:S(2)}, u32[]{:S(2)}) collective-permute-start(f32[4,128]{1,0:T(4,128)S(1)} %shard_map.103.refs_4_), channel_id=1, source_target_pairs={{0,2},{1,3},{2,0},{3,1},{4,6},{5,7},{6,4},{7,5},{8,10},{9,11},{10,... | collective-permute-start | bytes 6152 | tf_op jit(solution)/shard_map/ppermute | solution.py:60
  31.7 0.4 collective-permute-done.6.refs_1_
  32.1 0.0 collective-permute-start.8
  32.1 0.0 copy-done.2
  32.1 0.0 copy-done.3
  32.1 1.7 %shard_map.104 = (f32[512,128]{1,0:T(8,128)S(1)}, bf16[128,512]{1,0:T(8,128)(2,1)S(1)}, bf16[512,128]{1,0:T(8,128)(2,1)S(1)}, f32[128,512]{1,0:T(8,128)S(1)}, f3...) custom-call(bf16[128,1280]{1,0:T(8,128)(2,1)S(1)} %get-tuple-element.30.refs_0_, bf16[128,1280]{1,0:T(8,128)(2,1)S(1)} %shard_map.99.refs_1_, ...), custom_call_target="tpu_custom_call" | custom-call | flops 671088640 | bytes 3276800 | tf_op jit(solution)/shard_map/pallas_call | solution.py:34
  33.8 0.0 collective-permute-done.7.refs_2_
  33.8 0.9 %collective-permute-done.10.refs_5_ = f32[4,128]{1,0:T(4,128)S(1)} collective-permute-done((f32[4,128]{1,0:T(4,128)S(1)}, f32[4,128]{1,0:T(4,128)S(1)}, u32[]{:S(2)}, u32[]{:S(2)}) %collective-permute-start.10) | collective-permute-done | bytes 2080 | tf_op jit(solution)/shard_map/ppermute | solution.py:60
  34.8 0.0 collective-permute-done.8.refs_3_
  34.8 0.7 %shard_map.105 = (f32[128,128]{1,0:T(8,128)S(1)}, f32[128,128]{1,0:T(8,128)S(1)}, bf16[256,128]{1,0:T(8,128)(2,1)S(1)}, bf16[512,512]{1,0:T(8,128)(2,1)S(1)}, f32[4,128]{1,0:T(4,128)S(1)}) custom-call(f32[4,128]{1,0:T(4,128)S(1)} %get-tuple-element.39.refs_0_, f32[4,128]{1,0:T(4,128)S(1)} %collective-permute-done.6.refs_1_, ...), custom_call_target="tpu_custom_call" | custom-call | flops 67108864 | bytes 1454080 | tf_op jit(solution)/shard_map/pallas_call | solution.py:34
  35.5 0.1 collective-permute-start.11
  35.5 0.3 shard_map.108
  35.8 0.7 %collective-permute-start.13 = (bf16[256,128]{1,0:T(8,128)(2,1)S(1)}, bf16[256,128]{1,0:T(8,128)(2,1)S(1)}, u32[]{:S(2)}, u32[]{:S(2)}) collective-permute-start(bf16[256,128]{1,0:T(8,128)(2,1)S(1)} %get-tuple-element.54), channel_id=1, source_target_pairs={{0,2},{1,3},{2,0},{3,1},{4,6},{5,7},{6,4},{7,5},{8,10},{9,11},{10,... | collective-permute-start | bytes 196616 | tf_op jit(solution)/shard_map/ppermute | solution.py:60
  36.6 0.2 collective-permute-done.11.refs_1_
  36.8 2.8 %collective-permute-start.12 = (bf16[128,128]{1,0:T(8,128)(2,1)S(1)}, bf16[128,128]{1,0:T(8,128)(2,1)S(1)}, u32[]{:S(2)}, u32[]{:S(2)}) collective-permute-start(bf16[128,128]{1,0:T(8,128)(2,1)S(1)} %shard_map.106), channel_id=1, source_target_pairs={{0,8},{1,9},{2,10},{3,11},{4,12},{5,13},{6,14},{7,15},{8,0},{9,1},... | collective-permute-start | bytes 98312 | tf_op jit(solution)/shard_map/ppermute | solution.py:60
  39.6 0.8 %collective-permute-done.13.refs_1_ = bf16[256,128]{1,0:T(8,128)(2,1)S(1)} collective-permute-done((bf16[256,128]{1,0:T(8,128)(2,1)S(1)}, bf16[256,128]{1,0:T(8,128)(2,1)S(1)}, u32[]{:S(2)}, u32[]{:S(2)}) %collective-permute-start.13) | collective-permute-done | bytes 65568 | tf_op jit(solution)/shard_map/ppermute | solution.py:60
  40.4 1.3 %collective-permute-start.14 = (bf16[128,128]{1,0:T(8,128)(2,1)S(1)}, bf16[128,128]{1,0:T(8,128)(2,1)S(1)}, u32[]{:S(2)}, u32[]{:S(2)}) collective-permute-start(bf16[128,128]{1,0:T(8,128)(2,1)S(1)} %shard_map.109), channel_id=1, source_target_pairs={{0,4},{1,5},{2,6},{3,7},{4,0},{5,1},{6,2},{7,3},{8,12},{9,13},{10,... | collective-permute-start | bytes 98312 | tf_op jit(solution)/shard_map/ppermute | solution.py:60
  41.7 0.6 %collective-permute-done.12.refs_2_ = bf16[128,128]{1,0:T(8,128)(2,1)S(1)} collective-permute-done((bf16[128,128]{1,0:T(8,128)(2,1)S(1)}, bf16[128,128]{1,0:T(8,128)(2,1)S(1)}, u32[]{:S(2)}, u32[]{:S(2)}) %collective-permute-start.12) | collective-permute-done | bytes 32800 | tf_op jit(solution)/shard_map/ppermute | solution.py:60
  42.3 1.1 %shard_map.107 = bf16[128,4096]{1,0:T(8,128)(2,1)} custom-call(f32[128,128]{1,0:T(8,128)S(1)} %get-tuple-element.45.refs_0_, bf16[256,128]{1,0:T(8,128)(2,1)S(1)} %collective-permute-done.11.refs_1_, bf16[128,128]{1,0:T(8,128)(2,1)S(1)} %collective-permute-done.12.refs_2_, f32[128,128]{1,0:T(8,128)S(1)} %get-tuple-element.48.refs_3_, ...), custom_call_target="tpu_custom_call" | custom-call | flops 524288 | bytes 3145728 | tf_op jit(solution)/shard_map/pallas_call | solution.py:337
  43.4 1.0 %collective-permute-done.14.refs_2_ = bf16[128,128]{1,0:T(8,128)(2,1)S(1)} collective-permute-done((bf16[128,128]{1,0:T(8,128)(2,1)S(1)}, bf16[128,128]{1,0:T(8,128)(2,1)S(1)}, u32[]{:S(2)}, u32[]{:S(2)}) %collective-permute-start.14) | collective-permute-done | bytes 32800 | tf_op jit(solution)/shard_map/ppermute | solution.py:60
  44.4 1.1 %shard_map.110 = bf16[128,4096]{1,0:T(8,128)(2,1)} custom-call(f32[128,128]{1,0:T(8,128)S(1)} %get-tuple-element.53.refs_0_, bf16[256,128]{1,0:T(8,128)(2,1)S(1)} %collective-permute-done.13.refs_1_, bf16[128,128]{1,0:T(8,128)(2,1)S(1)} %collective-permute-done.14.refs_2_, f32[128,128]{1,0:T(8,128)S(1)} %get-tuple-element.56.refs_3_, ...), custom_call_target="tpu_custom_call" | custom-call | flops 524288 | bytes 3145728 | tf_op jit(solution)/shard_map/pallas_call | solution.py:337
  (4 shorter events, 0.0 us)
Async XLA Ops:
  0.6 13.3 %collective-permute-start.3 = (bf16[128,1280]{1,0:T(8,128)(2,1)}, bf16[128,1280]{1,0:T(8,128)(2,1)S(1)}, u32[]{:S(2)}, u32[]{:S(2)}) collective-permute-start(bf16[128,1280]{1,0:T(8,128)(2,1)} %refs_1_.5), channel_id=1, source_target_pairs={{0,4},{1,5},{2,6},{3,7},{4,0},{5,1},{6,2},{7,3},{8,12},{9,13},{10,... | collective-permute-start | bytes 983048 | tf_op jit(solution)/shard_map/ppermute | solution.py:60
  3.7 16.4 %collective-permute-start.1 = (bf16[128,1280]{1,0:T(8,128)(2,1)}, bf16[128,1280]{1,0:T(8,128)(2,1)S(1)}, u32[]{:S(2)}, u32[]{:S(2)}) collective-permute-start(bf16[128,1280]{1,0:T(8,128)(2,1)} %refs_1_.5), channel_id=1, source_target_pairs={{0,2},{1,3},{2,0},{3,1},{4,6},{5,7},{6,4},{7,5},{8,10},{9,11},{10,... | collective-permute-start | bytes 983048 | tf_op jit(solution)/shard_map/ppermute | solution.py:60
  8.1 10.0 %copy-start = (bf16[128,1664]{1,0:T(8,128)(2,1)S(1)}, bf16[128,1664]{1,0:T(8,128)(2,1)}, u32[]{:S(2)}) copy-start(bf16[128,1664]{1,0:T(8,128)(2,1)} %refs_0_.5) | copy-start | bytes 1277956
  8.1 10.0 %copy-start.1 = (bf16[128,1280]{1,0:T(8,128)(2,1)S(1)}, bf16[128,1280]{1,0:T(8,128)(2,1)}, u32[]{:S(2)}) copy-start(bf16[128,1280]{1,0:T(8,128)(2,1)} %refs_1_.5) | copy-start | bytes 983044
  8.1 10.0 %copy-start.4 = (bf16[1664,32]{0,1:T(8,128)(2,1)S(1)}, bf16[1664,32]{0,1:T(8,128)(2,1)}, u32[]{:S(2)}) copy-start(bf16[1664,32]{0,1:T(8,128)(2,1)} %param.12) | copy-start | bytes 319492
  8.1 9.9 %copy-start.5 = (bf16[1280,32]{0,1:T(8,128)(2,1)S(1)}, bf16[1280,32]{0,1:T(8,128)(2,1)}, u32[]{:S(2)}) copy-start(bf16[1280,32]{0,1:T(8,128)(2,1)} %param.14) | copy-start | bytes 245764
  8.1 16.9 %collective-permute-start = (bf16[128,1280]{1,0:T(8,128)(2,1)S(1)}, bf16[128,1280]{1,0:T(8,128)(2,1)S(1)}, u32[]{:S(2)}, u32[]{:S(2)}) collective-permute-start(bf16[128,1280]{1,0:T(8,128)(2,1)S(1)} %get-tuple-element.30.refs_0_), channel_id=1, source_target_pairs={{0,8},{1,9},{2,10},{3,11},{4,12},{5,13},{6,14},{7,15},{8,0},{9,1},... | collective-permute-start | bytes 983048 | tf_op jit(solution)/shard_map/ppermute | solution.py:60
  10.8 14.3 %collective-permute-start.5 = (bf16[128,1280]{1,0:T(8,128)(2,1)S(1)}, bf16[128,1280]{1,0:T(8,128)(2,1)S(1)}, u32[]{:S(2)}, u32[]{:S(2)}) collective-permute-start(bf16[128,1280]{1,0:T(8,128)(2,1)S(1)} %get-tuple-element.30.refs_0_), channel_id=1, source_target_pairs={{0,1},{1,0},{2,3},{3,2},{4,5},{5,4},{6,7},{7,6},{8,9},{9,8},{10,11... | collective-permute-start | bytes 983048 | tf_op jit(solution)/shard_map/ppermute | solution.py:60
  14.7 10.4 %collective-permute-start.4 = (bf16[128,1280]{1,0:T(8,128)(2,1)S(1)}, bf16[128,1280]{1,0:T(8,128)(2,1)S(1)}, u32[]{:S(2)}, u32[]{:S(2)}) collective-permute-start(bf16[128,1280]{1,0:T(8,128)(2,1)S(1)} %shard_map.100.refs_4_.refs_2_.refs_5_), channel_id=1, source_target_pairs={{0,2},{1,3},{2,0},{3,1},{4,6},{5,7},{6,4},{7,5},{8,10},{9,11},{10,... | collective-permute-start | bytes 983048 | tf_op jit(solution)/shard_map/ppermute | solution.py:60
  25.1 7.1 %copy-start.2 = (bf16[1280,128]{1,0:T(8,128)(2,1)S(1)}, bf16[1280,128]{1,0:T(8,128)(2,1)}, u32[]{:S(2)}) copy-start(bf16[1280,128]{1,0:T(8,128)(2,1)} %refs_8_.1) | copy-start | bytes 983044
  25.1 7.1 %copy-start.3 = (bf16[1280,128]{1,0:T(8,128)(2,1)S(1)}, bf16[1280,128]{1,0:T(8,128)(2,1)}, u32[]{:S(2)}) copy-start(bf16[1280,128]{1,0:T(8,128)(2,1)} %refs_9_.1) | copy-start | bytes 983044
  25.1 1.6 %collective-permute-start.2 = (bf16[128,1280]{1,0:T(8,128)(2,1)S(1)}, bf16[128,1280]{1,0:T(8,128)(2,1)S(1)}, u32[]{:S(2)}, u32[]{:S(2)}) collective-permute-start(bf16[128,1280]{1,0:T(8,128)(2,1)S(1)} %shard_map.99.refs_1_), channel_id=1, source_target_pairs={{0,1},{1,0},{2,3},{3,2},{4,5},{5,4},{6,7},{7,6},{8,9},{9,8},{10,11... | collective-permute-start | bytes 983048 | tf_op jit(solution)/shard_map/ppermute | solution.py:60
  27.5 3.6 %collective-permute-start.9 = (f32[4,128]{1,0:T(4,128)S(1)}, f32[4,128]{1,0:T(4,128)S(1)}, u32[]{:S(2)}, u32[]{:S(2)}) collective-permute-start(f32[4,128]{1,0:T(4,128)S(1)} %get-tuple-element.40.refs_0_), channel_id=1, source_target_pairs={{0,4},{1,5},{2,6},{3,7},{4,0},{5,1},{6,2},{7,3},{8,12},{9,13},{10,... | collective-permute-start | bytes 6152 | tf_op jit(solution)/shard_map/ppermute | solution.py:60
  27.5 4.6 %collective-permute-start.6 = (f32[4,128]{1,0:T(4,128)S(1)}, f32[4,128]{1,0:T(4,128)S(1)}, u32[]{:S(2)}, u32[]{:S(2)}) collective-permute-start(f32[4,128]{1,0:T(4,128)S(1)} %get-tuple-element.39.refs_0_), channel_id=1, source_target_pairs={{0,8},{1,9},{2,10},{3,11},{4,12},{5,13},{6,14},{7,15},{8,0},{9,1},... | collective-permute-start | bytes 6152 | tf_op jit(solution)/shard_map/ppermute | solution.py:60
  30.5 3.3 %collective-permute-start.7 = (f32[4,128]{1,0:T(4,128)S(1)}, f32[4,128]{1,0:T(4,128)S(1)}, u32[]{:S(2)}, u32[]{:S(2)}) collective-permute-start(f32[4,128]{1,0:T(4,128)S(1)} %get-tuple-element.39.refs_0_), channel_id=1, source_target_pairs={{0,1},{1,0},{2,3},{3,2},{4,5},{5,4},{6,7},{7,6},{8,9},{9,8},{10,11... | collective-permute-start | bytes 6152 | tf_op jit(solution)/shard_map/ppermute | solution.py:60
  31.1 3.7 %collective-permute-start.10 = (f32[4,128]{1,0:T(4,128)S(1)}, f32[4,128]{1,0:T(4,128)S(1)}, u32[]{:S(2)}, u32[]{:S(2)}) collective-permute-start(f32[4,128]{1,0:T(4,128)S(1)} %shard_map.103.refs_4_), channel_id=1, source_target_pairs={{0,2},{1,3},{2,0},{3,1},{4,6},{5,7},{6,4},{7,5},{8,10},{9,11},{10,... | collective-permute-start | bytes 6152 | tf_op jit(solution)/shard_map/ppermute | solution.py:60
  32.1 2.7 %collective-permute-start.8 = (f32[4,128]{1,0:T(4,128)S(1)}, f32[4,128]{1,0:T(4,128)S(1)}, u32[]{:S(2)}, u32[]{:S(2)}) collective-permute-start(f32[4,128]{1,0:T(4,128)S(1)} %collective-permute-done.6.refs_1_), channel_id=1, source_target_pairs={{0,1},{1,0},{2,3},{3,2},{4,5},{5,4},{6,7},{7,6},{8,9},{9,8},{10,11... | collective-permute-start | bytes 6152 | tf_op jit(solution)/shard_map/ppermute | solution.py:60
  35.5 1.3 %collective-permute-start.11 = (bf16[256,128]{1,0:T(8,128)(2,1)S(1)}, bf16[256,128]{1,0:T(8,128)(2,1)S(1)}, u32[]{:S(2)}, u32[]{:S(2)}) collective-permute-start(bf16[256,128]{1,0:T(8,128)(2,1)S(1)} %get-tuple-element.46), channel_id=1, source_target_pairs={{0,1},{1,0},{2,3},{3,2},{4,5},{5,4},{6,7},{7,6},{8,9},{9,8},{10,11... | collective-permute-start | bytes 196616 | tf_op jit(solution)/shard_map/ppermute | solution.py:60
  35.8 4.6 %collective-permute-start.13 = (bf16[256,128]{1,0:T(8,128)(2,1)S(1)}, bf16[256,128]{1,0:T(8,128)(2,1)S(1)}, u32[]{:S(2)}, u32[]{:S(2)}) collective-permute-start(bf16[256,128]{1,0:T(8,128)(2,1)S(1)} %get-tuple-element.54), channel_id=1, source_target_pairs={{0,2},{1,3},{2,0},{3,1},{4,6},{5,7},{6,4},{7,5},{8,10},{9,11},{10,... | collective-permute-start | bytes 196616 | tf_op jit(solution)/shard_map/ppermute | solution.py:60
  36.8 5.5 %collective-permute-start.12 = (bf16[128,128]{1,0:T(8,128)(2,1)S(1)}, bf16[128,128]{1,0:T(8,128)(2,1)S(1)}, u32[]{:S(2)}, u32[]{:S(2)}) collective-permute-start(bf16[128,128]{1,0:T(8,128)(2,1)S(1)} %shard_map.106), channel_id=1, source_target_pairs={{0,8},{1,9},{2,10},{3,11},{4,12},{5,13},{6,14},{7,15},{8,0},{9,1},... | collective-permute-start | bytes 98312 | tf_op jit(solution)/shard_map/ppermute | solution.py:60
  40.4 4.0 %collective-permute-start.14 = (bf16[128,128]{1,0:T(8,128)(2,1)S(1)}, bf16[128,128]{1,0:T(8,128)(2,1)S(1)}, u32[]{:S(2)}, u32[]{:S(2)}) collective-permute-start(bf16[128,128]{1,0:T(8,128)(2,1)S(1)} %shard_map.109), channel_id=1, source_target_pairs={{0,4},{1,5},{2,6},{3,7},{4,0},{5,1},{6,2},{7,3},{8,12},{9,13},{10,... | collective-permute-start | bytes 98312 | tf_op jit(solution)/shard_map/ppermute | solution.py:60

commit v7 on v6

--- a/solution.py
+++ b/solution.py
@@ -357,13 +357,14 @@
     near = swap(txt_feats, txt_bits[-1], n)
     (txt_emb,), txt_inv, w_txt_v = stream_embed([txt_feats], w_txt, True)
     far = [txt_emb] + [embed([x], w_txt_v)[0] for x in far[1:]]
-    texts = far + embed([near], w_txt_v) + [swap(x, txt_bits[-1], n) for x in far[1:]]
+    onward = [swap(x, txt_bits[-1], n) for x in far[1:]]
+    texts = far + embed([near], w_txt_v) + onward
     img_keys, txt_keys = call(
         keys_kernel,
         [((rows, a_img.shape[1] * LANES), F32), ((rows, a_txt.shape[1] * LANES), F32)],
         [img_feats, txt_feats, a_img.T, a_txt.T, img_inv, txt_inv],
     )
-    images = gather(img_emb, img_bits, n, lambda x: hold(x, [texts[nt // 2], img_keys]))
+    images = gather(img_emb, img_bits, n, lambda x: hold(x, [texts[0], img_keys]))
     raw, rows_lse, tops, totals = call(
         functools.partial(scores_kernel, ni - 1, nt),
         [(((ni - 1) * rows, nt * rows), F32), ((ni - 1, rows), F32), ((nt, rows), F32), ((nt, rows), F32)],

time: 45.7 us -> 45.4 us (level)
  transfers between devices with their start and end apart: 15 -> 15, of which waited for: 10 -> 8; matrix products, arithmetic and copies ran while one was open for 0% -> 0% of each run, Pallas kernels for 29% -> 29%
where the time goes in v7:
time: 45.4 us; the launch traced here: 45.3 us
  starting transfers between devices  19.2 us (42%)
  Pallas kernels  15.7 us (35%)
  waiting for transfers between devices  9.52 us (21%)
  between operations  0.78 us (2%)
    ppermute x15, starting transfers between devices, swap(): return lax.ppermute(x, 'dp', [(i, i ^ offset) for i in range(n)])  19.2 us
    ppermute x15, waiting for transfers between devices, swap(): return lax.ppermute(x, 'dp', [(i, i ^ offset) for i in range(n)])  9.52 us
    pallas_call x11, Pallas kernels, call(): pl.pallas_call(kernel, out_shape=[jax.ShapeDtypeStruct(s, d) for s, d in...  8.15 us
    pallas_call x2, Pallas kernels, stream_embed(): pl.pallas_call(functools.partial(stream_kernel, blocks, cuts), out_shape=...  5.32 us
    pallas_call x2, Pallas kernels, sketch(): pl.pallas_call(functools.partial(sketch_kernel, len(parts), turned), out_...  2.23 us
  transfers between devices with their start and end apart: 15, of which 8 were waited for; matrix products, arithmetic and copies ran while one was open for 0% of the time, Pallas kernels for 29%

profile of v7, /device:TPU:0, one launch (start us, length us, event | category | flops | bytes accessed | tf_op | source)
XLA Modules:
  0.0 45.3 jit_solution(13461772343351190359)
XLA Ops:
  0.6 0.0 copy-start.1
  0.6 3.1 %collective-permute-start.2 = (bf16[128,1280]{1,0:T(8,128)(2,1)}, bf16[128,1280]{1,0:T(8,128)(2,1)S(1)}, u32[]{:S(2)}, u32[]{:S(2)}) collective-permute-start(bf16[128,1280]{1,0:T(8,128)(2,1)} %refs_1_.5), channel_id=1, source_target_pairs={{0,4},{1,5},{2,6},{3,7},{4,0},{5,1},{6,2},{7,3},{8,12},{9,13},{10,... | collective-permute-start | bytes 983048 | tf_op jit(solution)/shard_map/ppermute | solution.py:60
  3.7 2.8 %shard_map.95 = (bf16[128,1280]{1,0:T(8,128)(2,1)S(1)}, f32[128,1]{1,0:T(8,128)S(1)}) custom-call(bf16[128,1664]{1,0:T(8,128)(2,1)} %refs_0_.5, bf16[1664,1280]{1,0:T(8,128)(2,1)} %refs_1_.3), custom_call_target="tpu_custom_call" | custom-call | flops 545259520 | bytes 4259840 | tf_op jit(solution)/shard_map/pallas_call | solution.py:123
  6.6 0.0 copy-start
  6.6 0.0 copy-start.2
  6.6 0.0 copy-start.5
  6.6 0.0 copy-start.6
  6.6 2.7 %collective-permute-start = (bf16[128,1280]{1,0:T(8,128)(2,1)S(1)}, bf16[128,1280]{1,0:T(8,128)(2,1)S(1)}, u32[]{:S(2)}, u32[]{:S(2)}) collective-permute-start(bf16[128,1280]{1,0:T(8,128)(2,1)S(1)} %get-tuple-element.30.refs_0_), channel_id=1, source_target_pairs={{0,8},{1,9},{2,10},{3,11},{4,12},{5,13},{6,14},{7,15},{8,0},{9,1},... | collective-permute-start | bytes 983048 | tf_op jit(solution)/shard_map/ppermute | solution.py:60
  9.3 0.0 copy-done.1
  9.3 1.5 %collective-permute-start.3 = (bf16[128,1280]{1,0:T(8,128)(2,1)S(1)}, bf16[128,1280]{1,0:T(8,128)(2,1)S(1)}, u32[]{:S(2)}, u32[]{:S(2)}) collective-permute-start(bf16[128,1280]{1,0:T(8,128)(2,1)S(1)} %copy-done.1), channel_id=1, source_target_pairs={{0,2},{1,3},{2,0},{3,1},{4,6},{5,7},{6,4},{7,5},{8,10},{9,11},{10,... | collective-permute-start | bytes 983048 | tf_op jit(solution)/shard_map/ppermute | solution.py:60
  10.8 0.0 collective-permute-start.5
  10.8 2.5 %shard_map.96 = (bf16[128,1280]{1,0:T(8,128)(2,1)S(1)}, f32[128,1]{1,0:T(8,128)S(1)}, bf16[1280,1280]{1,0:T(8,128)(2,1)S(1)}) custom-call(bf16[128,1280]{1,0:T(8,128)(2,1)} %refs_1_.5, bf16[1280,1280]{1,0:T(8,128)(2,1)} %refs_1_.4), custom_call_target="tpu_custom_call" | custom-call | flops 419430400 | bytes 3276800 | tf_op jit(solution)/shard_map/pallas_call | solution.py:123
  13.3 2.5 %collective-permute-done.2.refs_0_ = bf16[128,1280]{1,0:T(8,128)(2,1)S(1)} collective-permute-done((bf16[128,1280]{1,0:T(8,128)(2,1)}, bf16[128,1280]{1,0:T(8,128)(2,1)S(1)}, u32[]{:S(2)}, u32[]{:S(2)}) %collective-permute-start.2) | collective-permute-done | bytes 327712 | tf_op jit(solution)/shard_map/ppermute | solution.py:60
  15.8 0.7 %shard_map.99.refs_4_.refs_2_.refs_5_ = bf16[128,1280]{1,0:T(8,128)(2,1)S(1)} custom-call(bf16[128,1280]{1,0:T(8,128)(2,1)S(1)} %collective-permute-done.2.refs_0_, bf16[1280,1280]{1,0:T(8,128)(2,1)S(1)} %get-tuple-element.35.refs_1_), custom_call_target="tpu_custom_call" | custom-call | flops 419430400 | bytes 3604480 | tf_op jit(solution)/shard_map/pallas_call | solution.py:34
  16.5 1.8 %collective-permute-start.4 = (bf16[128,1280]{1,0:T(8,128)(2,1)S(1)}, bf16[128,1280]{1,0:T(8,128)(2,1)S(1)}, u32[]{:S(2)}, u32[]{:S(2)}) collective-permute-start(bf16[128,1280]{1,0:T(8,128)(2,1)S(1)} %shard_map.99.refs_4_.refs_2_.refs_5_), channel_id=1, source_target_pairs={{0,2},{1,3},{2,0},{3,1},{4,6},{5,7},{6,4},{7,5},{8,10},{9,11},{10,... | collective-permute-start | bytes 983048 | tf_op jit(solution)/shard_map/ppermute | solution.py:60
  18.3 0.0 copy-done
  18.3 0.0 copy-done.2
  18.3 0.0 copy-done.5
  18.3 0.0 copy-done.6
  18.3 2.1 %shard_map.97 = (f32[128,4096]{1,0:T(8,128)S(1)}, f32[128,4096]{1,0:T(8,128)S(1)}) custom-call(bf16[128,1664]{1,0:T(8,128)(2,1)S(1)} %copy-done, bf16[128,1280]{1,0:T(8,128)(2,1)S(1)} %copy-done.2, bf16[32,1664]{1,0:T(8,128)(2,1)S(1)} %bitcast.2, bf16[32,1280]{1,0:T(8,128)(2,1)S(1)} %bitcast.3, f32[128,1]{1,0:T(8,128)S(1)} %get-tuple-element.32.refs_4_, ...), custom_call_target="tpu_custom_call" | custom-call | bytes 943104 | tf_op jit(solution)/shard_map/pallas_call | solution.py:34
  20.4 3.4 %collective-permute-done.refs_0_ = bf16[128,1280]{1,0:T(8,128)(2,1)S(1)} collective-permute-done((bf16[128,1280]{1,0:T(8,128)(2,1)S(1)}, bf16[128,1280]{1,0:T(8,128)(2,1)S(1)}, u32[]{:S(2)}, u32[]{:S(2)}) %collective-permute-start) | collective-permute-done | bytes 327712 | tf_op jit(solution)/shard_map/ppermute | solution.py:60
  23.8 0.0 copy-start.3
  23.8 0.0 copy-start.4
  23.8 0.0 collective-permute-start.1
  23.8 0.0 collective-permute-done.3.refs_0_
  23.8 0.7 %shard_map.100.refs_5_.refs_3_.refs_6_ = bf16[128,1280]{1,0:T(8,128)(2,1)S(1)} custom-call(bf16[128,1280]{1,0:T(8,128)(2,1)S(1)} %collective-permute-done.3.refs_0_, bf16[1280,1280]{1,0:T(8,128)(2,1)S(1)} %get-tuple-element.35.refs_1_), custom_call_target="tpu_custom_call" | custom-call | flops 419430400 | bytes 3604480 | tf_op jit(solution)/shard_map/pallas_call | solution.py:34
  24.6 0.0 collective-permute-done.5.refs_2_
  24.6 0.7 %collective-permute-done.4.refs_6_.refs_4_.refs_7_ = bf16[128,1280]{1,0:T(8,128)(2,1)S(1)} collective-permute-done((bf16[128,1280]{1,0:T(8,128)(2,1)S(1)}, bf16[128,1280]{1,0:T(8,128)(2,1)S(1)}, u32[]{:S(2)}, u32[]{:S(2)}) %collective-permute-start.4) | collective-permute-done | bytes 327712 | tf_op jit(solution)/shard_map/ppermute | solution.py:60
  25.3 1.1 %shard_map.101 = (f32[384,512]{1,0:T(8,128)S(1)}, f32[3,128]{1,0:T(4,128)S(1)}, f32[4,128]{1,0:T(4,128)S(1)}, f32[4,128]{1,0:T(4,128)S(1)}) custom-call(bf16[128,1280]{1,0:T(8,128)(2,1)S(1)} %get-tuple-element.30.refs_0_, bf16[128,1280]{1,0:T(8,128)(2,1)S(1)} %shard_map.98.refs_1_, bf16[128,1280]{1,0:T(8,128)(2,1)S(1)} %collective-permute-done.5.refs_2_, ...), custom_call_target="tpu_custom_call" | custom-call | flops 503316480 | bytes 2293760 | tf_op jit(solution)/shard_map/pallas_call | solution.py:34
  26.4 0.0 collective-permute-done.1.refs_0_.refs_3_
  26.4 0.8 %shard_map.102 = (f32[128,512]{1,0:T(8,128)S(1)}, f32[4,128]{1,0:T(4,128)S(1)}, f32[4,128]{1,0:T(4,128)S(1)}) custom-call(bf16[128,1280]{1,0:T(8,128)(2,1)S(1)} %collective-permute-done.1.refs_0_.refs_3_, bf16[128,1280]{1,0:T(8,128)(2,1)S(1)} %get-tuple-element.31.refs_1_.refs_3_.refs_4_, bf16[128,1280]{1,0:T(8,128)(2,1)S(1)} %shard_map.99.refs_4_.refs_2_.refs_5_, ...), custom_call_target="tpu_custom_call" | custom-call | flops 167772160 | bytes 1644032 | tf_op jit(solution)/shard_map/pallas_call | solution.py:34
  27.2 0.4 collective-permute-start.9
  27.6 2.7 %collective-permute-start.6 = (f32[4,128]{1,0:T(4,128)S(1)}, f32[4,128]{1,0:T(4,128)S(1)}, u32[]{:S(2)}, u32[]{:S(2)}) collective-permute-start(f32[4,128]{1,0:T(4,128)S(1)} %get-tuple-element.39.refs_0_), channel_id=1, source_target_pairs={{0,8},{1,9},{2,10},{3,11},{4,12},{5,13},{6,14},{7,15},{8,0},{9,1},... | collective-permute-start | bytes 6152 | tf_op jit(solution)/shard_map/ppermute | solution.py:60
  30.3 0.0 collective-permute-start.7
  30.3 0.5 %collective-permute-done.9.refs_1_ = f32[4,128]{1,0:T(4,128)S(1)} collective-permute-done((f32[4,128]{1,0:T(4,128)S(1)}, f32[4,128]{1,0:T(4,128)S(1)}, u32[]{:S(2)}, u32[]{:S(2)}) %collective-permute-start.9) | collective-permute-done | bytes 2080 | tf_op jit(solution)/shard_map/ppermute | solution.py:60
  30.8 1.5 %collective-permute-start.10 = (f32[4,128]{1,0:T(4,128)S(1)}, f32[4,128]{1,0:T(4,128)S(1)}, u32[]{:S(2)}, u32[]{:S(2)}) collective-permute-start(f32[4,128]{1,0:T(4,128)S(1)} %shard_map.103.refs_4_), channel_id=1, source_target_pairs={{0,2},{1,3},{2,0},{3,1},{4,6},{5,7},{6,4},{7,5},{8,10},{9,11},{10,... | collective-permute-start | bytes 6152 | tf_op jit(solution)/shard_map/ppermute | solution.py:60
  32.3 0.0 collective-permute-done.6.refs_1_
  32.3 0.0 collective-permute-start.8
  32.3 0.0 copy-done.3
  32.4 0.0 copy-done.4
  32.4 1.7 %shard_map.104 = (f32[512,128]{1,0:T(8,128)S(1)}, bf16[128,512]{1,0:T(8,128)(2,1)S(1)}, bf16[512,128]{1,0:T(8,128)(2,1)S(1)}, f32[128,512]{1,0:T(8,128)S(1)}, f3...) custom-call(bf16[128,1280]{1,0:T(8,128)(2,1)S(1)} %get-tuple-element.30.refs_0_, bf16[128,1280]{1,0:T(8,128)(2,1)S(1)} %shard_map.98.refs_1_, ...), custom_call_target="tpu_custom_call" | custom-call | flops 671088640 | bytes 3276800 | tf_op jit(solution)/shard_map/pallas_call | solution.py:34
  34.1 0.0 collective-permute-done.7.refs_2_
  34.1 0.4 collective-permute-done.10.refs_5_
  34.5 0.0 collective-permute-done.8.refs_3_
  34.5 0.7 %shard_map.105 = (f32[128,128]{1,0:T(8,128)S(1)}, f32[128,128]{1,0:T(8,128)S(1)}, bf16[256,128]{1,0:T(8,128)(2,1)S(1)}, bf16[512,512]{1,0:T(8,128)(2,1)S(1)}, f32[4,128]{1,0:T(4,128)S(1)}) custom-call(f32[4,128]{1,0:T(4,128)S(1)} %get-tuple-element.39.refs_0_, f32[4,128]{1,0:T(4,128)S(1)} %collective-permute-done.6.refs_1_, ...), custom_call_target="tpu_custom_call" | custom-call | flops 67108864 | bytes 1454080 | tf_op jit(solution)/shard_map/pallas_call | solution.py:34
  35.2 0.1 collective-permute-start.11
  35.3 0.3 shard_map.108
  35.6 1.4 %collective-permute-start.13 = (bf16[256,128]{1,0:T(8,128)(2,1)S(1)}, bf16[256,128]{1,0:T(8,128)(2,1)S(1)}, u32[]{:S(2)}, u32[]{:S(2)}) collective-permute-start(bf16[256,128]{1,0:T(8,128)(2,1)S(1)} %get-tuple-element.54), channel_id=1, source_target_pairs={{0,2},{1,3},{2,0},{3,1},{4,6},{5,7},{6,4},{7,5},{8,10},{9,11},{10,... | collective-permute-start | bytes 196616 | tf_op jit(solution)/shard_map/ppermute | solution.py:60
  37.1 0.0 collective-permute-done.11.refs_1_
  37.1 2.7 %collective-permute-start.12 = (bf16[128,128]{1,0:T(8,128)(2,1)S(1)}, bf16[128,128]{1,0:T(8,128)(2,1)S(1)}, u32[]{:S(2)}, u32[]{:S(2)}) collective-permute-start(bf16[128,128]{1,0:T(8,128)(2,1)S(1)} %shard_map.106), channel_id=1, source_target_pairs={{0,8},{1,9},{2,10},{3,11},{4,12},{5,13},{6,14},{7,15},{8,0},{9,1},... | collective-permute-start | bytes 98312 | tf_op jit(solution)/shard_map/ppermute | solution.py:60
  39.8 0.3 collective-permute-done.13.refs_1_
  40.1 1.3 %collective-permute-start.14 = (bf16[128,128]{1,0:T(8,128)(2,1)S(1)}, bf16[128,128]{1,0:T(8,128)(2,1)S(1)}, u32[]{:S(2)}, u32[]{:S(2)}) collective-permute-start(bf16[128,128]{1,0:T(8,128)(2,1)S(1)} %shard_map.109), channel_id=1, source_target_pairs={{0,4},{1,5},{2,6},{3,7},{4,0},{5,1},{6,2},{7,3},{8,12},{9,13},{10,... | collective-permute-start | bytes 98312 | tf_op jit(solution)/shard_map/ppermute | solution.py:60
  41.5 0.5 %collective-permute-done.12.refs_2_ = bf16[128,128]{1,0:T(8,128)(2,1)S(1)} collective-permute-done((bf16[128,128]{1,0:T(8,128)(2,1)S(1)}, bf16[128,128]{1,0:T(8,128)(2,1)S(1)}, u32[]{:S(2)}, u32[]{:S(2)}) %collective-permute-start.12) | collective-permute-done | bytes 32800 | tf_op jit(solution)/shard_map/ppermute | solution.py:60
  42.0 1.1 %shard_map.107 = bf16[128,4096]{1,0:T(8,128)(2,1)} custom-call(f32[128,128]{1,0:T(8,128)S(1)} %get-tuple-element.45.refs_0_, bf16[256,128]{1,0:T(8,128)(2,1)S(1)} %collective-permute-done.11.refs_1_, bf16[128,128]{1,0:T(8,128)(2,1)S(1)} %collective-permute-done.12.refs_2_, f32[128,128]{1,0:T(8,128)S(1)} %get-tuple-element.48.refs_3_, ...), custom_call_target="tpu_custom_call" | custom-call | flops 524288 | bytes 3145728 | tf_op jit(solution)/shard_map/pallas_call | solution.py:337
  43.1 1.1 %collective-permute-done.14.refs_2_ = bf16[128,128]{1,0:T(8,128)(2,1)S(1)} collective-permute-done((bf16[128,128]{1,0:T(8,128)(2,1)S(1)}, bf16[128,128]{1,0:T(8,128)(2,1)S(1)}, u32[]{:S(2)}, u32[]{:S(2)}) %collective-permute-start.14) | collective-permute-done | bytes 32800 | tf_op jit(solution)/shard_map/ppermute | solution.py:60
  44.1 1.1 %shard_map.110 = bf16[128,4096]{1,0:T(8,128)(2,1)} custom-call(f32[128,128]{1,0:T(8,128)S(1)} %get-tuple-element.53.refs_0_, bf16[256,128]{1,0:T(8,128)(2,1)S(1)} %collective-permute-done.13.refs_1_, bf16[128,128]{1,0:T(8,128)(2,1)S(1)} %collective-permute-done.14.refs_2_, f32[128,128]{1,0:T(8,128)S(1)} %get-tuple-element.56.refs_3_, ...), custom_call_target="tpu_custom_call" | custom-call | flops 524288 | bytes 3145728 | tf_op jit(solution)/shard_map/pallas_call | solution.py:337
  (4 shorter events, 0.0 us)
Async XLA Ops:
  0.6 8.6 %copy-start.1 = (bf16[128,1280]{1,0:T(8,128)(2,1)S(1)}, bf16[128,1280]{1,0:T(8,128)(2,1)}, u32[]{:S(2)}) copy-start(bf16[128,1280]{1,0:T(8,128)(2,1)} %refs_1_.5) | copy-start | bytes 983044
  0.6 15.2 %collective-permute-start.2 = (bf16[128,1280]{1,0:T(8,128)(2,1)}, bf16[128,1280]{1,0:T(8,128)(2,1)S(1)}, u32[]{:S(2)}, u32[]{:S(2)}) collective-permute-start(bf16[128,1280]{1,0:T(8,128)(2,1)} %refs_1_.5), channel_id=1, source_target_pairs={{0,4},{1,5},{2,6},{3,7},{4,0},{5,1},{6,2},{7,3},{8,12},{9,13},{10,... | collective-permute-start | bytes 983048 | tf_op jit(solution)/shard_map/ppermute | solution.py:60
  6.6 11.7 %copy-start = (bf16[128,1664]{1,0:T(8,128)(2,1)S(1)}, bf16[128,1664]{1,0:T(8,128)(2,1)}, u32[]{:S(2)}) copy-start(bf16[128,1664]{1,0:T(8,128)(2,1)} %refs_0_.5) | copy-start | bytes 1277956
  6.6 11.7 %copy-start.2 = (bf16[128,1280]{1,0:T(8,128)(2,1)S(1)}, bf16[128,1280]{1,0:T(8,128)(2,1)}, u32[]{:S(2)}) copy-start(bf16[128,1280]{1,0:T(8,128)(2,1)} %refs_1_.5) | copy-start | bytes 983044
  6.6 11.7 %copy-start.5 = (bf16[1664,32]{0,1:T(8,128)(2,1)S(1)}, bf16[1664,32]{0,1:T(8,128)(2,1)}, u32[]{:S(2)}) copy-start(bf16[1664,32]{0,1:T(8,128)(2,1)} %param.12) | copy-start | bytes 319492
  6.6 11.7 %copy-start.6 = (bf16[1280,32]{0,1:T(8,128)(2,1)S(1)}, bf16[1280,32]{0,1:T(8,128)(2,1)}, u32[]{:S(2)}) copy-start(bf16[1280,32]{0,1:T(8,128)(2,1)} %param.14) | copy-start | bytes 245764
  6.6 17.2 %collective-permute-start = (bf16[128,1280]{1,0:T(8,128)(2,1)S(1)}, bf16[128,1280]{1,0:T(8,128)(2,1)S(1)}, u32[]{:S(2)}, u32[]{:S(2)}) collective-permute-start(bf16[128,1280]{1,0:T(8,128)(2,1)S(1)} %get-tuple-element.30.refs_0_), channel_id=1, source_target_pairs={{0,8},{1,9},{2,10},{3,11},{4,12},{5,13},{6,14},{7,15},{8,0},{9,1},... | collective-permute-start | bytes 983048 | tf_op jit(solution)/shard_map/ppermute | solution.py:60
  9.3 14.6 %collective-permute-start.3 = (bf16[128,1280]{1,0:T(8,128)(2,1)S(1)}, bf16[128,1280]{1,0:T(8,128)(2,1)S(1)}, u32[]{:S(2)}, u32[]{:S(2)}) collective-permute-start(bf16[128,1280]{1,0:T(8,128)(2,1)S(1)} %copy-done.1), channel_id=1, source_target_pairs={{0,2},{1,3},{2,0},{3,1},{4,6},{5,7},{6,4},{7,5},{8,10},{9,11},{10,... | collective-permute-start | bytes 983048 | tf_op jit(solution)/shard_map/ppermute | solution.py:60
  10.8 13.8 %collective-permute-start.5 = (bf16[128,1280]{1,0:T(8,128)(2,1)S(1)}, bf16[128,1280]{1,0:T(8,128)(2,1)S(1)}, u32[]{:S(2)}, u32[]{:S(2)}) collective-permute-start(bf16[128,1280]{1,0:T(8,128)(2,1)S(1)} %get-tuple-element.30.refs_0_), channel_id=1, source_target_pairs={{0,1},{1,0},{2,3},{3,2},{4,5},{5,4},{6,7},{7,6},{8,9},{9,8},{10,11... | collective-permute-start | bytes 983048 | tf_op jit(solution)/shard_map/ppermute | solution.py:60
  16.5 8.7 %collective-permute-start.4 = (bf16[128,1280]{1,0:T(8,128)(2,1)S(1)}, bf16[128,1280]{1,0:T(8,128)(2,1)S(1)}, u32[]{:S(2)}, u32[]{:S(2)}) collective-permute-start(bf16[128,1280]{1,0:T(8,128)(2,1)S(1)} %shard_map.99.refs_4_.refs_2_.refs_5_), channel_id=1, source_target_pairs={{0,2},{1,3},{2,0},{3,1},{4,6},{5,7},{6,4},{7,5},{8,10},{9,11},{10,... | collective-permute-start | bytes 983048 | tf_op jit(solution)/shard_map/ppermute | solution.py:60
  23.8 8.5 %copy-start.3 = (bf16[1280,128]{1,0:T(8,128)(2,1)S(1)}, bf16[1280,128]{1,0:T(8,128)(2,1)}, u32[]{:S(2)}) copy-start(bf16[1280,128]{1,0:T(8,128)(2,1)} %refs_8_.1) | copy-start | bytes 983044
  23.8 8.5 %copy-start.4 = (bf16[1280,128]{1,0:T(8,128)(2,1)S(1)}, bf16[1280,128]{1,0:T(8,128)(2,1)}, u32[]{:S(2)}) copy-start(bf16[1280,128]{1,0:T(8,128)(2,1)} %refs_9_.1) | copy-start | bytes 983044
  23.8 2.6 %collective-permute-start.1 = (bf16[128,1280]{1,0:T(8,128)(2,1)S(1)}, bf16[128,1280]{1,0:T(8,128)(2,1)S(1)}, u32[]{:S(2)}, u32[]{:S(2)}) collective-permute-start(bf16[128,1280]{1,0:T(8,128)(2,1)S(1)} %shard_map.98.refs_1_), channel_id=1, source_target_pairs={{0,1},{1,0},{2,3},{3,2},{4,5},{5,4},{6,7},{7,6},{8,9},{9,8},{10,11... | collective-permute-start | bytes 983048 | tf_op jit(solution)/shard_map/ppermute | solution.py:60
  27.2 3.6 %collective-permute-start.9 = (f32[4,128]{1,0:T(4,128)S(1)}, f32[4,128]{1,0:T(4,128)S(1)}, u32[]{:S(2)}, u32[]{:S(2)}) collective-permute-start(f32[4,128]{1,0:T(4,128)S(1)} %get-tuple-element.40.refs_0_), channel_id=1, source_target_pairs={{0,4},{1,5},{2,6},{3,7},{4,0},{5,1},{6,2},{7,3},{8,12},{9,13},{10,... | collective-permute-start | bytes 6152 | tf_op jit(solution)/shard_map/ppermute | solution.py:60
  27.6 4.7 %collective-permute-start.6 = (f32[4,128]{1,0:T(4,128)S(1)}, f32[4,128]{1,0:T(4,128)S(1)}, u32[]{:S(2)}, u32[]{:S(2)}) collective-permute-start(f32[4,128]{1,0:T(4,128)S(1)} %get-tuple-element.39.refs_0_), channel_id=1, source_target_pairs={{0,8},{1,9},{2,10},{3,11},{4,12},{5,13},{6,14},{7,15},{8,0},{9,1},... | collective-permute-start | bytes 6152 | tf_op jit(solution)/shard_map/ppermute | solution.py:60
  30.3 3.7 %collective-permute-start.7 = (f32[4,128]{1,0:T(4,128)S(1)}, f32[4,128]{1,0:T(4,128)S(1)}, u32[]{:S(2)}, u32[]{:S(2)}) collective-permute-start(f32[4,128]{1,0:T(4,128)S(1)} %get-tuple-element.39.refs_0_), channel_id=1, source_target_pairs={{0,1},{1,0},{2,3},{3,2},{4,5},{5,4},{6,7},{7,6},{8,9},{9,8},{10,11... | collective-permute-start | bytes 6152 | tf_op jit(solution)/shard_map/ppermute | solution.py:60
  30.8 3.7 %collective-permute-start.10 = (f32[4,128]{1,0:T(4,128)S(1)}, f32[4,128]{1,0:T(4,128)S(1)}, u32[]{:S(2)}, u32[]{:S(2)}) collective-permute-start(f32[4,128]{1,0:T(4,128)S(1)} %shard_map.103.refs_4_), channel_id=1, source_target_pairs={{0,2},{1,3},{2,0},{3,1},{4,6},{5,7},{6,4},{7,5},{8,10},{9,11},{10,... | collective-permute-start | bytes 6152 | tf_op jit(solution)/shard_map/ppermute | solution.py:60
  32.3 2.2 %collective-permute-start.8 = (f32[4,128]{1,0:T(4,128)S(1)}, f32[4,128]{1,0:T(4,128)S(1)}, u32[]{:S(2)}, u32[]{:S(2)}) collective-permute-start(f32[4,128]{1,0:T(4,128)S(1)} %collective-permute-done.6.refs_1_), channel_id=1, source_target_pairs={{0,1},{1,0},{2,3},{3,2},{4,5},{5,4},{6,7},{7,6},{8,9},{9,8},{10,11... | collective-permute-start | bytes 6152 | tf_op jit(solution)/shard_map/ppermute | solution.py:60
  35.2 1.9 %collective-permute-start.11 = (bf16[256,128]{1,0:T(8,128)(2,1)S(1)}, bf16[256,128]{1,0:T(8,128)(2,1)S(1)}, u32[]{:S(2)}, u32[]{:S(2)}) collective-permute-start(bf16[256,128]{1,0:T(8,128)(2,1)S(1)} %get-tuple-element.46), channel_id=1, source_target_pairs={{0,1},{1,0},{2,3},{3,2},{4,5},{5,4},{6,7},{7,6},{8,9},{9,8},{10,11... | collective-permute-start | bytes 196616 | tf_op jit(solution)/shard_map/ppermute | solution.py:60
  35.6 4.5 %collective-permute-start.13 = (bf16[256,128]{1,0:T(8,128)(2,1)S(1)}, bf16[256,128]{1,0:T(8,128)(2,1)S(1)}, u32[]{:S(2)}, u32[]{:S(2)}) collective-permute-start(bf16[256,128]{1,0:T(8,128)(2,1)S(1)} %get-tuple-element.54), channel_id=1, source_target_pairs={{0,2},{1,3},{2,0},{3,1},{4,6},{5,7},{6,4},{7,5},{8,10},{9,11},{10,... | collective-permute-start | bytes 196616 | tf_op jit(solution)/shard_map/ppermute | solution.py:60
  37.1 4.9 %collective-permute-start.12 = (bf16[128,128]{1,0:T(8,128)(2,1)S(1)}, bf16[128,128]{1,0:T(8,128)(2,1)S(1)}, u32[]{:S(2)}, u32[]{:S(2)}) collective-permute-start(bf16[128,128]{1,0:T(8,128)(2,1)S(1)} %shard_map.106), channel_id=1, source_target_pairs={{0,8},{1,9},{2,10},{3,11},{4,12},{5,13},{6,14},{7,15},{8,0},{9,1},... | collective-permute-start | bytes 98312 | tf_op jit(solution)/shard_map/ppermute | solution.py:60
  40.1 4.0 %collective-permute-start.14 = (bf16[128,128]{1,0:T(8,128)(2,1)S(1)}, bf16[128,128]{1,0:T(8,128)(2,1)S(1)}, u32[]{:S(2)}, u32[]{:S(2)}) collective-permute-start(bf16[128,128]{1,0:T(8,128)(2,1)S(1)} %shard_map.109), channel_id=1, source_target_pairs={{0,4},{1,5},{2,6},{3,7},{4,0},{5,1},{6,2},{7,3},{8,12},{9,13},{10,... | collective-permute-start | bytes 98312 | tf_op jit(solution)/shard_map/ppermute | solution.py:60

commit v8 on v7

--- a/solution.py
+++ b/solution.py
@@ -30,7 +30,8 @@
     specs = [pl.BlockSpec(memory_space=pltpu.VMEM)] * len(args)
     if after:
         kernel = functools.partial(skip, kernel, len(args), len(after))
-        args, specs = args + list(after), specs + [pl.BlockSpec(memory_space=pl.ANY)] * len(after)
+        args += [pltpu.with_memory_space_constraint(a, pltpu.VMEM) for a in after]
+        specs += [pl.BlockSpec(memory_space=pltpu.VMEM)] * len(after)
     return pl.pallas_call(
         kernel,
         out_shape=[jax.ShapeDtypeStruct(s, d) for s, d in outs],
@@ -163,37 +164,50 @@
     return top, jnp.sum(jnp.exp(scores - top), axis=axis, keepdims=True)
 
 
+def lay(blocks, whole):
+    rows = blocks[0].shape[0]
+    for k, block in enumerate(blocks):
+        whole[k * rows : (k + 1) * rows] = block[...]
+
+
 def scores_kernel(ni, nt, *refs):
-    images, texts = refs[:ni], refs[ni : ni + nt]
-    raw, row_lse, col_top, col_total, all_images, all_texts = refs[ni + nt :]
+    images, texts, refs = refs[:ni], refs[ni : ni + nt], refs[ni + nt :]
+    raw, row_top, row_total, col_top, col_total, all_images, all_texts = refs
     rows = images[0].shape[0]
-    for a in range(ni):
-        all_images[a * rows : (a + 1) * rows] = images[a][...]
-    for t in range(nt):
-        all_texts[t * rows : (t + 1) * rows] = texts[t][...]
+    lay(images, all_images)
+    lay(texts, all_texts)
     raw[...] = dot(all_images[...], all_texts[...], 1, 1)
-    for a in range(ni):
-        top, total = lse_parts(LOGIT_SCALE * raw[a * rows : (a + 1) * rows], 1)
-        row_lse[a : a + 1] = jnp.broadcast_to(top + jnp.log(total), (rows, LANES)).T[:1]
+    row_top[...], row_total[...] = lse_parts(LOGIT_SCALE * raw[...], 1)
     for t in range(nt):
         col_top[t : t + 1], col_total[t : t + 1] = lse_parts(LOGIT_SCALE * raw[:, t * rows : (t + 1) * rows], 0)
 
 
+def joined(top, total, other_top, other_total):
+    high = jnp.maximum(top, other_top)
+    return high + jnp.log(total * jnp.exp(top - high) + other_total * jnp.exp(other_top - high))
+
+
 def last_scores_kernel(ni, nt, *refs):
-    image, texts, (rows_lse, tops, totals) = refs[0], refs[1 : 1 + nt], refs[1 + nt : 4 + nt]
-    raw, row_lse, col_lse, all_texts = refs[4 + nt :]
-    rows = image.shape[0]
+    images, texts, refs = refs[:ni], refs[ni : ni + nt], refs[ni + nt :]
+    row_top, row_total, col_top, col_total, last_col, last_row, row_lse, col_lse, all_images, all_texts = refs
+    rows = images[0].shape[0]
+    lay(images[:-1], all_images)
+    lay(texts, all_texts)
+    last_col[...] = dot(all_images[...], texts[-1][...], 1, 1)
+    last_row[...] = dot(images[-1][...], all_texts[...], 1, 1)
+    col_scores, row_scores = LOGIT_SCALE * last_col[...], LOGIT_SCALE * last_row[...]
+    lse = joined(row_top[...], row_total[...], *lse_parts(col_scores, 1))
+    top, total = lse_parts(row_scores, 1)
+    lses = [lse[a * rows : (a + 1) * rows] for a in range(ni - 1)] + [top + jnp.log(total)]
+    for a in range(ni):
+        row_lse[a : a + 1] = jnp.broadcast_to(lses[a], (rows, LANES)).T[:1]
     for t in range(nt):
-        all_texts[t * rows : (t + 1) * rows] = texts[t][...]
-    raw[...] = dot(image[...], all_texts[...], 1, 1)
-    top, total = lse_parts(LOGIT_SCALE * raw[...], 1)
-    row_lse[: ni - 1] = rows_lse[...]
-    row_lse[ni - 1 :] = jnp.broadcast_to(top + jnp.log(total), (rows, LANES)).T[:1]
-    for t in range(nt):
-        top, total = lse_parts(LOGIT_SCALE * raw[:, t * rows : (t + 1) * rows], 0)
-        high = jnp.maximum(top, tops[t : t + 1])
-        total = total * jnp.exp(top - high) + totals[t : t + 1] * jnp.exp(tops[t : t + 1] - high)
-        col_lse[t : t + 1] = high + jnp.log(total)
+        top, total = lse_parts(row_scores[:, t * rows : (t + 1) * rows], 0)
+        if t < nt - 1:
+            others = col_top[t : t + 1], col_total[t : t + 1]
+        else:
+            others = lse_parts(col_scores, 0)
+        col_lse[t : t + 1] = joined(top, total, *others)
 
 
 def factors_kernel(ni, nt, *refs):
@@ -273,9 +287,9 @@
 def weights_kernel(ni, nt, row_flips, col_flips, *refs):
     row_parts, refs = refs[: len(row_flips)], refs[len(row_flips) :]
     col_parts, refs = refs[: len(col_flips)], refs[len(col_flips) :]
-    raw, last_raw, img_low, txt_low = refs[:4]
+    raw, last_col, last_row, img_low, txt_low = refs[:5]
     half = ni // 2
-    *img_kept, img_sent, weights_bf, inners = refs[4:]
+    *img_kept, img_sent, weights_bf, inners = refs[5:]
     rows = LANES
     row_lse = merge(row_parts, row_flips)
     col_lse = merge(col_parts, col_flips)
@@ -285,7 +299,10 @@
         inner_row = jnp.zeros((rows, rows), F32)
         for t in range(nt):
             cols = slice(t * rows, (t + 1) * rows)
-            here = raw[a * rows : (a + 1) * rows, cols] if a < ni - 1 else last_raw[:, cols]
+            if a == ni - 1:
+                here = last_row[:, cols]
+            else:
+                here = (raw[a * rows : (a + 1) * rows, cols] if t < nt - 1 else last_col[a * rows : (a + 1) * rows])
             scores = LOGIT_SCALE * here
             weights = jnp.exp(scores - row) + jnp.exp(scores - col_lse[t : t + 1])
             weights_bf[a * rows : (a + 1) * rows, t * rows : (t + 1) * rows] = weights.astype(BF16)
@@ -363,21 +380,24 @@
         keys_kernel,
         [((rows, a_img.shape[1] * LANES), F32), ((rows, a_txt.shape[1] * LANES), F32)],
         [img_feats, txt_feats, a_img.T, a_txt.T, img_inv, txt_inv],
+        after=far[1:2],
     )
     images = gather(img_emb, img_bits, n, lambda x: hold(x, [texts[0], img_keys]))
-    raw, rows_lse, tops, totals = call(
-        functools.partial(scores_kernel, ni - 1, nt),
-        [(((ni - 1) * rows, nt * rows), F32), ((ni - 1, rows), F32), ((nt, rows), F32), ((nt, rows), F32)],
-        images[:-1] + texts,
+    raw, *halfway = call(
+        functools.partial(scores_kernel, ni - 1, nt - 1),
+        [(((ni - 1) * rows, (nt - 1) * rows), F32)]
+        + [(((ni - 1) * rows, 1), F32)] * 2
+        + [((nt - 1, rows), F32)] * 2,
+        images[:-1] + texts[:-1],
+        scratch=[pltpu.VMEM(((ni - 1) * rows, wide), BF16), pltpu.VMEM(((nt - 1) * rows, wide), BF16)],
+        flops=2 * (ni - 1) * (nt - 1) * rows * rows * wide,
+    )
+    last_col, last_row, row_lse, col_lse = call(
+        functools.partial(last_scores_kernel, ni, nt),
+        [(((ni - 1) * rows, rows), F32), ((rows, nt * rows), F32), ((ni, rows), F32), ((nt, rows), F32)],
+        images + texts + halfway,
         scratch=[pltpu.VMEM(((ni - 1) * rows, wide), BF16), pltpu.VMEM((nt * rows, wide), BF16)],
-        flops=2 * (ni - 1) * nt * rows * rows * wide,
-    )
-    last_raw, row_lse, col_lse = call(
-        functools.partial(last_scores_kernel, ni, nt),
-        [((rows, nt * rows), F32), ((ni, rows), F32), ((nt, rows), F32)],
-        images[-1:] + texts + [rows_lse, tops, totals],
-        scratch=[pltpu.VMEM((nt * rows, wide), BF16)],
-        flops=2 * nt * rows * rows * wide,
+        flops=2 * (ni + nt) * rows * rows * wide,
     )
     row_parts = gather(row_lse, img_bits, n)
     col_parts, col_flips = gather_lse(col_lse, txt_bits, n)
@@ -399,7 +419,7 @@
         functools.partial(weights_kernel, ni, nt, tuple(range(ni)), col_flips),
         [((rows, low), F32)] * half
         + [((half * rows, low), BF16), ((ni * rows, nt * rows), BF16), ((nt, rows), F32)],
-        row_parts + col_parts + [raw, last_raw, img_low, txt_low],
+        row_parts + col_parts + [raw, last_col, last_row, img_low, txt_low],
         flops=2 * ni * nt * rows * rows * low,
     )
     *txt_kept, txt_sent = call(

time: 45.4 us -> 45.1 us (level)
  waiting for transfers between devices: 9.52 us -> 8.85 us
    ppermute x15, waiting for transfers between devices: 9.52 us -> 8.85 us  [swap(): return lax.ppermute(x, 'dp', [(i, i ^ offset) for i in range(n)])]
  transfers between devices with their start and end apart: 15 -> 15, of which waited for: 8 -> 7; matrix products, arithmetic and copies ran while one was open for 0% -> 0% of each run, Pallas kernels for 29% -> 29%
where the time goes in v8:
time: 45.1 us; the launch traced here: 45 us
  starting transfers between devices  19.2 us (43%)
  Pallas kernels  16.1 us (36%)
  waiting for transfers between devices  8.85 us (20%)
  between operations  0.8 us (2%)
    ppermute x15, starting transfers between devices, swap(): return lax.ppermute(x, 'dp', [(i, i ^ offset) for i in range(n)])  19.2 us
    ppermute x15, waiting for transfers between devices, swap(): return lax.ppermute(x, 'dp', [(i, i ^ offset) for i in range(n)])  8.85 us
    pallas_call x11, Pallas kernels, call(): pl.pallas_call(kernel, out_shape=[jax.ShapeDtypeStruct(s, d) for s, d in...  8.52 us
    pallas_call x2, Pallas kernels, stream_embed(): pl.pallas_call(functools.partial(stream_kernel, blocks, cuts), out_shape=...  5.32 us
    pallas_call x2, Pallas kernels, sketch(): pl.pallas_call(functools.partial(sketch_kernel, len(parts), turned), out_...  2.23 us
  transfers between devices with their start and end apart: 15, of which 7 were waited for; matrix products, arithmetic and copies ran while one was open for 0% of the time, Pallas kernels for 29%

profile of v8, /device:TPU:0, one launch (start us, length us, event | category | flops | bytes accessed | tf_op | source)
XLA Modules:
  0.0 45.0 jit_solution(12949721895525650449)
XLA Ops:
  0.6 0.0 copy-start.1
  0.6 3.1 %collective-permute-start.1 = (bf16[128,1280]{1,0:T(8,128)(2,1)}, bf16[128,1280]{1,0:T(8,128)(2,1)S(1)}, u32[]{:S(2)}, u32[]{:S(2)}) collective-permute-start(bf16[128,1280]{1,0:T(8,128)(2,1)} %refs_1_.5), channel_id=1, source_target_pairs={{0,4},{1,5},{2,6},{3,7},{4,0},{5,1},{6,2},{7,3},{8,12},{9,13},{10,... | collective-permute-start | bytes 983048 | tf_op jit(solution)/shard_map/ppermute | solution.py:61
  3.7 2.8 %shard_map.95 = (bf16[128,1280]{1,0:T(8,128)(2,1)S(1)}, f32[128,1]{1,0:T(8,128)S(1)}) custom-call(bf16[128,1664]{1,0:T(8,128)(2,1)} %refs_0_.5, bf16[1664,1280]{1,0:T(8,128)(2,1)} %refs_1_.3), custom_call_target="tpu_custom_call" | custom-call | flops 545259520 | bytes 4259840 | tf_op jit(solution)/shard_map/pallas_call | solution.py:124
  6.6 0.0 copy-start
  6.6 0.0 copy-start.2
  6.6 0.0 copy-start.5
  6.6 0.0 copy-start.6
  6.6 2.7 %collective-permute-start = (bf16[128,1280]{1,0:T(8,128)(2,1)S(1)}, bf16[128,1280]{1,0:T(8,128)(2,1)S(1)}, u32[]{:S(2)}, u32[]{:S(2)}) collective-permute-start(bf16[128,1280]{1,0:T(8,128)(2,1)S(1)} %get-tuple-element.32.refs_0_), channel_id=1, source_target_pairs={{0,8},{1,9},{2,10},{3,11},{4,12},{5,13},{6,14},{7,15},{8,0},{9,1},... | collective-permute-start | bytes 983048 | tf_op jit(solution)/shard_map/ppermute | solution.py:61
  9.3 0.0 copy-done.1
  9.3 1.5 %collective-permute-start.4 = (bf16[128,1280]{1,0:T(8,128)(2,1)S(1)}, bf16[128,1280]{1,0:T(8,128)(2,1)S(1)}, u32[]{:S(2)}, u32[]{:S(2)}) collective-permute-start(bf16[128,1280]{1,0:T(8,128)(2,1)S(1)} %copy-done.1), channel_id=1, source_target_pairs={{0,2},{1,3},{2,0},{3,1},{4,6},{5,7},{6,4},{7,5},{8,10},{9,11},{10,... | collective-permute-start | bytes 983048 | tf_op jit(solution)/shard_map/ppermute | solution.py:61
  10.8 0.0 collective-permute-start.2
  10.8 2.5 %shard_map.96 = (bf16[128,1280]{1,0:T(8,128)(2,1)S(1)}, f32[128,1]{1,0:T(8,128)S(1)}, bf16[1280,1280]{1,0:T(8,128)(2,1)S(1)}) custom-call(bf16[128,1280]{1,0:T(8,128)(2,1)} %refs_1_.5, bf16[1280,1280]{1,0:T(8,128)(2,1)} %refs_1_.4), custom_call_target="tpu_custom_call" | custom-call | flops 419430400 | bytes 3276800 | tf_op jit(solution)/shard_map/pallas_call | solution.py:124
  13.3 2.5 %collective-permute-done.1.refs_0_ = bf16[128,1280]{1,0:T(8,128)(2,1)S(1)} collective-permute-done((bf16[128,1280]{1,0:T(8,128)(2,1)}, bf16[128,1280]{1,0:T(8,128)(2,1)S(1)}, u32[]{:S(2)}, u32[]{:S(2)}) %collective-permute-start.1) | collective-permute-done | bytes 327712 | tf_op jit(solution)/shard_map/ppermute | solution.py:61
  15.8 0.7 %shard_map.97.refs_6_.refs_4_.refs_5_ = bf16[128,1280]{1,0:T(8,128)(2,1)S(1)} custom-call(bf16[128,1280]{1,0:T(8,128)(2,1)S(1)} %collective-permute-done.1.refs_0_, bf16[1280,1280]{1,0:T(8,128)(2,1)S(1)} %get-tuple-element.36.refs_1_), custom_call_target="tpu_custom_call" | custom-call | flops 419430400 | bytes 3604480 | tf_op jit(solution)/shard_map/pallas_call | solution.py:35
  16.5 1.8 %collective-permute-start.5 = (bf16[128,1280]{1,0:T(8,128)(2,1)S(1)}, bf16[128,1280]{1,0:T(8,128)(2,1)S(1)}, u32[]{:S(2)}, u32[]{:S(2)}) collective-permute-start(bf16[128,1280]{1,0:T(8,128)(2,1)S(1)} %shard_map.97.refs_6_.refs_4_.refs_5_), channel_id=1, source_target_pairs={{0,2},{1,3},{2,0},{3,1},{4,6},{5,7},{6,4},{7,5},{8,10},{9,11},{10,... | collective-permute-start | bytes 983048 | tf_op jit(solution)/shard_map/ppermute | solution.py:61
  18.3 0.0 copy-done
  18.3 0.0 copy-done.2
  18.3 0.0 copy-done.5
  18.3 0.0 copy-done.6
  18.3 2.1 %shard_map.98 = (f32[128,4096]{1,0:T(8,128)S(1)}, f32[128,4096]{1,0:T(8,128)S(1)}) custom-call(bf16[128,1664]{1,0:T(8,128)(2,1)S(1)} %copy-done, bf16[128,1280]{1,0:T(8,128)(2,1)S(1)} %copy-done.2, bf16[32,1664]{1,0:T(8,128)(2,1)S(1)} %bitcast.2, bf16[32,1280]{1,0:T(8,128)(2,1)S(1)} %bitcast.3, f32[128,1]{1,0:T(8,128)S(1)} %get-tuple-element.34.refs_4_, ...), custom_call_target="tpu_custom_call" | custom-call | bytes 943104 | tf_op jit(solution)/shard_map/pallas_call | solution.py:35
  20.4 3.4 %collective-permute-done.refs_0_ = bf16[128,1280]{1,0:T(8,128)(2,1)S(1)} collective-permute-done((bf16[128,1280]{1,0:T(8,128)(2,1)S(1)}, bf16[128,1280]{1,0:T(8,128)(2,1)S(1)}, u32[]{:S(2)}, u32[]{:S(2)}) %collective-permute-start) | collective-permute-done | bytes 327712 | tf_op jit(solution)/shard_map/ppermute | solution.py:61
  23.8 0.0 collective-permute-start.3
  23.8 0.0 collective-permute-done.4.refs_0_
  23.8 0.7 %shard_map.100.refs_5_.refs_6_ = bf16[128,1280]{1,0:T(8,128)(2,1)S(1)} custom-call(bf16[128,1280]{1,0:T(8,128)(2,1)S(1)} %collective-permute-done.4.refs_0_, bf16[1280,1280]{1,0:T(8,128)(2,1)S(1)} %get-tuple-element.36.refs_1_), custom_call_target="tpu_custom_call" | custom-call | flops 419430400 | bytes 3604480 | tf_op jit(solution)/shard_map/pallas_call | solution.py:35
  24.6 0.0 copy-start.3
  24.6 0.0 copy-start.4
  24.6 0.0 collective-permute-done.2.refs_2_
  24.6 1.0 %shard_map.101 = (f32[384,384]{1,0:T(8,128)S(1)}, f32[384,1]{1,0:T(8,128)S(1)}, f32[384,1]{1,0:T(8,128)S(1)}, f32[3,128]{1,0:T(4,128)S(1)}, f32[3,128]{1,0:T(4,128)S(1)}) custom-call(bf16[128,1280]{1,0:T(8,128)(2,1)S(1)} %get-tuple-element.32.refs_0_, bf16[128,1280]{1,0:T(8,128)(2,1)S(1)} %shard_map.99.refs_1_, ...), custom_call_target="tpu_custom_call" | custom-call | flops 377487360 | bytes 1966080 | tf_op jit(solution)/shard_map/pallas_call | solution.py:35
  25.6 0.0 collective-permute-done.5.refs_7_
  25.6 0.0 collective-permute-done.3.refs_3_
  25.6 1.3 %shard_map.102 = (f32[384,128]{1,0:T(8,128)S(1)}, f32[128,512]{1,0:T(8,128)S(1)}, f32[4,128]{1,0:T(4,128)S(1)}, f32[4,128]{1,0:T(4,128)S(1)}) custom-call(bf16[128,1280]{1,0:T(8,128)(2,1)S(1)} %get-tuple-element.32.refs_0_, bf16[128,1280]{1,0:T(8,128)(2,1)S(1)} %shard_map.99.refs_1_, bf16[128,1280]{1,0:T(8,128)(2,1)S(1)} %collective-permute-done.2.refs_2_, ...), custom_call_target="tpu_custom_call" | custom-call | flops 335544320 | bytes 2627584 | tf_op jit(solution)/shard_map/pallas_call | solution.py:35
  26.9 0.1 collective-permute-start.9
  27.0 3.0 %collective-permute-start.6 = (f32[4,128]{1,0:T(4,128)S(1)}, f32[4,128]{1,0:T(4,128)S(1)}, u32[]{:S(2)}, u32[]{:S(2)}) collective-permute-start(f32[4,128]{1,0:T(4,128)S(1)} %get-tuple-element.42.refs_0_), channel_id=1, source_target_pairs={{0,8},{1,9},{2,10},{3,11},{4,12},{5,13},{6,14},{7,15},{8,0},{9,1},... | collective-permute-start | bytes 6152 | tf_op jit(solution)/shard_map/ppermute | solution.py:61
  30.0 0.0 collective-permute-start.7
  30.0 0.5 %collective-permute-done.9.refs_1_ = f32[4,128]{1,0:T(4,128)S(1)} collective-permute-done((f32[4,128]{1,0:T(4,128)S(1)}, f32[4,128]{1,0:T(4,128)S(1)}, u32[]{:S(2)}, u32[]{:S(2)}) %collective-permute-start.9) | collective-permute-done | bytes 2080 | tf_op jit(solution)/shard_map/ppermute | solution.py:61
  30.5 1.6 %collective-permute-start.10 = (f32[4,128]{1,0:T(4,128)S(1)}, f32[4,128]{1,0:T(4,128)S(1)}, u32[]{:S(2)}, u32[]{:S(2)}) collective-permute-start(f32[4,128]{1,0:T(4,128)S(1)} %shard_map.103.refs_4_), channel_id=1, source_target_pairs={{0,2},{1,3},{2,0},{3,1},{4,6},{5,7},{6,4},{7,5},{8,10},{9,11},{10,... | collective-permute-start | bytes 6152 | tf_op jit(solution)/shard_map/ppermute | solution.py:61
  32.1 0.0 collective-permute-done.6.refs_1_
  32.1 0.0 collective-permute-start.8
  32.1 0.0 copy-done.3
  32.1 0.0 copy-done.4
  32.1 1.7 %shard_map.104 = (f32[512,128]{1,0:T(8,128)S(1)}, bf16[128,512]{1,0:T(8,128)(2,1)S(1)}, bf16[512,128]{1,0:T(8,128)(2,1)S(1)}, f32[128,512]{1,0:T(8,128)S(1)}, f3...) custom-call(bf16[128,1280]{1,0:T(8,128)(2,1)S(1)} %get-tuple-element.32.refs_0_, bf16[128,1280]{1,0:T(8,128)(2,1)S(1)} %shard_map.99.refs_1_, ...), custom_call_target="tpu_custom_call" | custom-call | flops 671088640 | bytes 3276800 | tf_op jit(solution)/shard_map/pallas_call | solution.py:35
  33.8 0.0 collective-permute-done.7.refs_2_
  33.8 0.4 collective-permute-done.10.refs_5_
  34.2 0.0 collective-permute-done.8.refs_3_
  34.2 0.7 %shard_map.105 = (f32[128,128]{1,0:T(8,128)S(1)}, f32[128,128]{1,0:T(8,128)S(1)}, bf16[256,128]{1,0:T(8,128)(2,1)S(1)}, bf16[512,512]{1,0:T(8,128)(2,1)S(1)}, f32[4,128]{1,0:T(4,128)S(1)}) custom-call(f32[4,128]{1,0:T(4,128)S(1)} %get-tuple-element.42.refs_0_, f32[4,128]{1,0:T(4,128)S(1)} %collective-permute-done.6.refs_1_, ...), custom_call_target="tpu_custom_call" | custom-call | flops 67108864 | bytes 1454080 | tf_op jit(solution)/shard_map/pallas_call | solution.py:35
  34.9 0.2 collective-permute-start.11
  35.1 0.3 shard_map.108
  35.4 1.4 %collective-permute-start.13 = (bf16[256,128]{1,0:T(8,128)(2,1)S(1)}, bf16[256,128]{1,0:T(8,128)(2,1)S(1)}, u32[]{:S(2)}, u32[]{:S(2)}) collective-permute-start(bf16[256,128]{1,0:T(8,128)(2,1)S(1)} %get-tuple-element.58), channel_id=1, source_target_pairs={{0,2},{1,3},{2,0},{3,1},{4,6},{5,7},{6,4},{7,5},{8,10},{9,11},{10,... | collective-permute-start | bytes 196616 | tf_op jit(solution)/shard_map/ppermute | solution.py:61
  36.9 0.0 collective-permute-done.11.refs_1_
  36.9 2.5 %collective-permute-start.12 = (bf16[128,128]{1,0:T(8,128)(2,1)S(1)}, bf16[128,128]{1,0:T(8,128)(2,1)S(1)}, u32[]{:S(2)}, u32[]{:S(2)}) collective-permute-start(bf16[128,128]{1,0:T(8,128)(2,1)S(1)} %shard_map.106), channel_id=1, source_target_pairs={{0,8},{1,9},{2,10},{3,11},{4,12},{5,13},{6,14},{7,15},{8,0},{9,1},... | collective-permute-start | bytes 98312 | tf_op jit(solution)/shard_map/ppermute | solution.py:61
  39.4 0.4 collective-permute-done.13.refs_1_
  39.8 1.3 %collective-permute-start.14 = (bf16[128,128]{1,0:T(8,128)(2,1)S(1)}, bf16[128,128]{1,0:T(8,128)(2,1)S(1)}, u32[]{:S(2)}, u32[]{:S(2)}) collective-permute-start(bf16[128,128]{1,0:T(8,128)(2,1)S(1)} %shard_map.109), channel_id=1, source_target_pairs={{0,4},{1,5},{2,6},{3,7},{4,0},{5,1},{6,2},{7,3},{8,12},{9,13},{10,... | collective-permute-start | bytes 98312 | tf_op jit(solution)/shard_map/ppermute | solution.py:61
  41.2 0.6 %collective-permute-done.12.refs_2_ = bf16[128,128]{1,0:T(8,128)(2,1)S(1)} collective-permute-done((bf16[128,128]{1,0:T(8,128)(2,1)S(1)}, bf16[128,128]{1,0:T(8,128)(2,1)S(1)}, u32[]{:S(2)}, u32[]{:S(2)}) %collective-permute-start.12) | collective-permute-done | bytes 32800 | tf_op jit(solution)/shard_map/ppermute | solution.py:61
  41.8 1.1 %shard_map.107 = bf16[128,4096]{1,0:T(8,128)(2,1)} custom-call(f32[128,128]{1,0:T(8,128)S(1)} %get-tuple-element.49.refs_0_, bf16[256,128]{1,0:T(8,128)(2,1)S(1)} %collective-permute-done.11.refs_1_, bf16[128,128]{1,0:T(8,128)(2,1)S(1)} %collective-permute-done.12.refs_2_, f32[128,128]{1,0:T(8,128)S(1)} %get-tuple-element.52.refs_3_, ...), custom_call_target="tpu_custom_call" | custom-call | flops 524288 | bytes 3145728 | tf_op jit(solution)/shard_map/pallas_call | solution.py:354
  42.9 1.0 %collective-permute-done.14.refs_2_ = bf16[128,128]{1,0:T(8,128)(2,1)S(1)} collective-permute-done((bf16[128,128]{1,0:T(8,128)(2,1)S(1)}, bf16[128,128]{1,0:T(8,128)(2,1)S(1)}, u32[]{:S(2)}, u32[]{:S(2)}) %collective-permute-start.14) | collective-permute-done | bytes 32800 | tf_op jit(solution)/shard_map/ppermute | solution.py:61
  43.8 1.1 %shard_map.110 = bf16[128,4096]{1,0:T(8,128)(2,1)} custom-call(f32[128,128]{1,0:T(8,128)S(1)} %get-tuple-element.57.refs_0_, bf16[256,128]{1,0:T(8,128)(2,1)S(1)} %collective-permute-done.13.refs_1_, bf16[128,128]{1,0:T(8,128)(2,1)S(1)} %collective-permute-done.14.refs_2_, f32[128,128]{1,0:T(8,128)S(1)} %get-tuple-element.60.refs_3_, ...), custom_call_target="tpu_custom_call" | custom-call | flops 524288 | bytes 3145728 | tf_op jit(solution)/shard_map/pallas_call | solution.py:354
  (4 shorter events, 0.0 us)
Async XLA Ops:
  0.6 8.6 %copy-start.1 = (bf16[128,1280]{1,0:T(8,128)(2,1)S(1)}, bf16[128,1280]{1,0:T(8,128)(2,1)}, u32[]{:S(2)}) copy-start(bf16[128,1280]{1,0:T(8,128)(2,1)} %refs_1_.5) | copy-start | bytes 983044
  0.6 15.2 %collective-permute-start.1 = (bf16[128,1280]{1,0:T(8,128)(2,1)}, bf16[128,1280]{1,0:T(8,128)(2,1)S(1)}, u32[]{:S(2)}, u32[]{:S(2)}) collective-permute-start(bf16[128,1280]{1,0:T(8,128)(2,1)} %refs_1_.5), channel_id=1, source_target_pairs={{0,4},{1,5},{2,6},{3,7},{4,0},{5,1},{6,2},{7,3},{8,12},{9,13},{10,... | collective-permute-start | bytes 983048 | tf_op jit(solution)/shard_map/ppermute | solution.py:61
  6.6 11.7 %copy-start = (bf16[128,1664]{1,0:T(8,128)(2,1)S(1)}, bf16[128,1664]{1,0:T(8,128)(2,1)}, u32[]{:S(2)}) copy-start(bf16[128,1664]{1,0:T(8,128)(2,1)} %refs_0_.5) | copy-start | bytes 1277956
  6.6 11.7 %copy-start.2 = (bf16[128,1280]{1,0:T(8,128)(2,1)S(1)}, bf16[128,1280]{1,0:T(8,128)(2,1)}, u32[]{:S(2)}) copy-start(bf16[128,1280]{1,0:T(8,128)(2,1)} %refs_1_.5) | copy-start | bytes 983044
  6.6 11.7 %copy-start.5 = (bf16[1664,32]{0,1:T(8,128)(2,1)S(1)}, bf16[1664,32]{0,1:T(8,128)(2,1)}, u32[]{:S(2)}) copy-start(bf16[1664,32]{0,1:T(8,128)(2,1)} %param.12) | copy-start | bytes 319492
  6.6 11.7 %copy-start.6 = (bf16[1280,32]{0,1:T(8,128)(2,1)S(1)}, bf16[1280,32]{0,1:T(8,128)(2,1)}, u32[]{:S(2)}) copy-start(bf16[1280,32]{0,1:T(8,128)(2,1)} %param.14) | copy-start | bytes 245764
  6.6 17.2 %collective-permute-start = (bf16[128,1280]{1,0:T(8,128)(2,1)S(1)}, bf16[128,1280]{1,0:T(8,128)(2,1)S(1)}, u32[]{:S(2)}, u32[]{:S(2)}) collective-permute-start(bf16[128,1280]{1,0:T(8,128)(2,1)S(1)} %get-tuple-element.32.refs_0_), channel_id=1, source_target_pairs={{0,8},{1,9},{2,10},{3,11},{4,12},{5,13},{6,14},{7,15},{8,0},{9,1},... | collective-permute-start | bytes 983048 | tf_op jit(solution)/shard_map/ppermute | solution.py:61
  9.3 14.6 %collective-permute-start.4 = (bf16[128,1280]{1,0:T(8,128)(2,1)S(1)}, bf16[128,1280]{1,0:T(8,128)(2,1)S(1)}, u32[]{:S(2)}, u32[]{:S(2)}) collective-permute-start(bf16[128,1280]{1,0:T(8,128)(2,1)S(1)} %copy-done.1), channel_id=1, source_target_pairs={{0,2},{1,3},{2,0},{3,1},{4,6},{5,7},{6,4},{7,5},{8,10},{9,11},{10,... | collective-permute-start | bytes 983048 | tf_op jit(solution)/shard_map/ppermute | solution.py:61
  10.8 13.8 %collective-permute-start.2 = (bf16[128,1280]{1,0:T(8,128)(2,1)S(1)}, bf16[128,1280]{1,0:T(8,128)(2,1)S(1)}, u32[]{:S(2)}, u32[]{:S(2)}) collective-permute-start(bf16[128,1280]{1,0:T(8,128)(2,1)S(1)} %get-tuple-element.32.refs_0_), channel_id=1, source_target_pairs={{0,1},{1,0},{2,3},{3,2},{4,5},{5,4},{6,7},{7,6},{8,9},{9,8},{10,11... | collective-permute-start | bytes 983048 | tf_op jit(solution)/shard_map/ppermute | solution.py:61
  16.5 9.1 %collective-permute-start.5 = (bf16[128,1280]{1,0:T(8,128)(2,1)S(1)}, bf16[128,1280]{1,0:T(8,128)(2,1)S(1)}, u32[]{:S(2)}, u32[]{:S(2)}) collective-permute-start(bf16[128,1280]{1,0:T(8,128)(2,1)S(1)} %shard_map.97.refs_6_.refs_4_.refs_5_), channel_id=1, source_target_pairs={{0,2},{1,3},{2,0},{3,1},{4,6},{5,7},{6,4},{7,5},{8,10},{9,11},{10,... | collective-permute-start | bytes 983048 | tf_op jit(solution)/shard_map/ppermute | solution.py:61
  23.8 1.8 %collective-permute-start.3 = (bf16[128,1280]{1,0:T(8,128)(2,1)S(1)}, bf16[128,1280]{1,0:T(8,128)(2,1)S(1)}, u32[]{:S(2)}, u32[]{:S(2)}) collective-permute-start(bf16[128,1280]{1,0:T(8,128)(2,1)S(1)} %shard_map.99.refs_1_), channel_id=1, source_target_pairs={{0,1},{1,0},{2,3},{3,2},{4,5},{5,4},{6,7},{7,6},{8,9},{9,8},{10,11... | collective-permute-start | bytes 983048 | tf_op jit(solution)/shard_map/ppermute | solution.py:61
  24.6 7.6 %copy-start.3 = (bf16[1280,128]{1,0:T(8,128)(2,1)S(1)}, bf16[1280,128]{1,0:T(8,128)(2,1)}, u32[]{:S(2)}) copy-start(bf16[1280,128]{1,0:T(8,128)(2,1)} %refs_8_.1) | copy-start | bytes 983044
  24.6 7.6 %copy-start.4 = (bf16[1280,128]{1,0:T(8,128)(2,1)S(1)}, bf16[1280,128]{1,0:T(8,128)(2,1)}, u32[]{:S(2)}) copy-start(bf16[1280,128]{1,0:T(8,128)(2,1)} %refs_9_.1) | copy-start | bytes 983044
  26.9 3.6 %collective-permute-start.9 = (f32[4,128]{1,0:T(4,128)S(1)}, f32[4,128]{1,0:T(4,128)S(1)}, u32[]{:S(2)}, u32[]{:S(2)}) collective-permute-start(f32[4,128]{1,0:T(4,128)S(1)} %get-tuple-element.43.refs_0_), channel_id=1, source_target_pairs={{0,4},{1,5},{2,6},{3,7},{4,0},{5,1},{6,2},{7,3},{8,12},{9,13},{10,... | collective-permute-start | bytes 6152 | tf_op jit(solution)/shard_map/ppermute | solution.py:61
  27.0 5.1 %collective-permute-start.6 = (f32[4,128]{1,0:T(4,128)S(1)}, f32[4,128]{1,0:T(4,128)S(1)}, u32[]{:S(2)}, u32[]{:S(2)}) collective-permute-start(f32[4,128]{1,0:T(4,128)S(1)} %get-tuple-element.42.refs_0_), channel_id=1, source_target_pairs={{0,8},{1,9},{2,10},{3,11},{4,12},{5,13},{6,14},{7,15},{8,0},{9,1},... | collective-permute-start | bytes 6152 | tf_op jit(solution)/shard_map/ppermute | solution.py:61
  30.0 3.9 %collective-permute-start.7 = (f32[4,128]{1,0:T(4,128)S(1)}, f32[4,128]{1,0:T(4,128)S(1)}, u32[]{:S(2)}, u32[]{:S(2)}) collective-permute-start(f32[4,128]{1,0:T(4,128)S(1)} %get-tuple-element.42.refs_0_), channel_id=1, source_target_pairs={{0,1},{1,0},{2,3},{3,2},{4,5},{5,4},{6,7},{7,6},{8,9},{9,8},{10,11... | collective-permute-start | bytes 6152 | tf_op jit(solution)/shard_map/ppermute | solution.py:61
  30.5 3.7 %collective-permute-start.10 = (f32[4,128]{1,0:T(4,128)S(1)}, f32[4,128]{1,0:T(4,128)S(1)}, u32[]{:S(2)}, u32[]{:S(2)}) collective-permute-start(f32[4,128]{1,0:T(4,128)S(1)} %shard_map.103.refs_4_), channel_id=1, source_target_pairs={{0,2},{1,3},{2,0},{3,1},{4,6},{5,7},{6,4},{7,5},{8,10},{9,11},{10,... | collective-permute-start | bytes 6152 | tf_op jit(solution)/shard_map/ppermute | solution.py:61
  32.1 2.1 %collective-permute-start.8 = (f32[4,128]{1,0:T(4,128)S(1)}, f32[4,128]{1,0:T(4,128)S(1)}, u32[]{:S(2)}, u32[]{:S(2)}) collective-permute-start(f32[4,128]{1,0:T(4,128)S(1)} %collective-permute-done.6.refs_1_), channel_id=1, source_target_pairs={{0,1},{1,0},{2,3},{3,2},{4,5},{5,4},{6,7},{7,6},{8,9},{9,8},{10,11... | collective-permute-start | bytes 6152 | tf_op jit(solution)/shard_map/ppermute | solution.py:61
  34.9 2.0 %collective-permute-start.11 = (bf16[256,128]{1,0:T(8,128)(2,1)S(1)}, bf16[256,128]{1,0:T(8,128)(2,1)S(1)}, u32[]{:S(2)}, u32[]{:S(2)}) collective-permute-start(bf16[256,128]{1,0:T(8,128)(2,1)S(1)} %get-tuple-element.50), channel_id=1, source_target_pairs={{0,1},{1,0},{2,3},{3,2},{4,5},{5,4},{6,7},{7,6},{8,9},{9,8},{10,11... | collective-permute-start | bytes 196616 | tf_op jit(solution)/shard_map/ppermute | solution.py:61
  35.4 4.4 %collective-permute-start.13 = (bf16[256,128]{1,0:T(8,128)(2,1)S(1)}, bf16[256,128]{1,0:T(8,128)(2,1)S(1)}, u32[]{:S(2)}, u32[]{:S(2)}) collective-permute-start(bf16[256,128]{1,0:T(8,128)(2,1)S(1)} %get-tuple-element.58), channel_id=1, source_target_pairs={{0,2},{1,3},{2,0},{3,1},{4,6},{5,7},{6,4},{7,5},{8,10},{9,11},{10,... | collective-permute-start | bytes 196616 | tf_op jit(solution)/shard_map/ppermute | solution.py:61
  36.9 4.9 %collective-permute-start.12 = (bf16[128,128]{1,0:T(8,128)(2,1)S(1)}, bf16[128,128]{1,0:T(8,128)(2,1)S(1)}, u32[]{:S(2)}, u32[]{:S(2)}) collective-permute-start(bf16[128,128]{1,0:T(8,128)(2,1)S(1)} %shard_map.106), channel_id=1, source_target_pairs={{0,8},{1,9},{2,10},{3,11},{4,12},{5,13},{6,14},{7,15},{8,0},{9,1},... | collective-permute-start | bytes 98312 | tf_op jit(solution)/shard_map/ppermute | solution.py:61
  39.8 4.0 %collective-permute-start.14 = (bf16[128,128]{1,0:T(8,128)(2,1)S(1)}, bf16[128,128]{1,0:T(8,128)(2,1)S(1)}, u32[]{:S(2)}, u32[]{:S(2)}) collective-permute-start(bf16[128,128]{1,0:T(8,128)(2,1)S(1)} %shard_map.109), channel_id=1, source_target_pairs={{0,4},{1,5},{2,6},{3,7},{4,0},{5,1},{6,2},{7,3},{8,12},{9,13},{10,... | collective-permute-start | bytes 98312 | tf_op jit(solution)/shard_map/ppermute | solution.py:61

commit v9 on v8

--- a/solution.py
+++ b/solution.py
@@ -188,13 +188,12 @@
 
 
 def last_scores_kernel(ni, nt, *refs):
-    images, texts, refs = refs[:ni], refs[ni : ni + nt], refs[ni + nt :]
-    row_top, row_total, col_top, col_total, last_col, last_row, row_lse, col_lse, all_images, all_texts = refs
-    rows = images[0].shape[0]
-    lay(images[:-1], all_images)
-    lay(texts, all_texts)
-    last_col[...] = dot(all_images[...], texts[-1][...], 1, 1)
-    last_row[...] = dot(images[-1][...], all_texts[...], 1, 1)
+    image, text, row_top, row_total, col_top, col_total, all_images, all_texts, *refs = refs
+    last_col, last_row, row_lse, col_lse = refs
+    rows = image.shape[0]
+    last_col[...] = dot(all_images[...], text[...], 1, 1)
+    last_row[:, : (nt - 1) * rows] = dot(image[...], all_texts[...], 1, 1)
+    last_row[:, (nt - 1) * rows :] = dot(image[...], text[...], 1, 1)
     col_scores, row_scores = LOGIT_SCALE * last_col[...], LOGIT_SCALE * last_row[...]
     lse = joined(row_top[...], row_total[...], *lse_parts(col_scores, 1))
     top, total = lse_parts(row_scores, 1)
@@ -387,16 +386,15 @@
         functools.partial(scores_kernel, ni - 1, nt - 1),
         [(((ni - 1) * rows, (nt - 1) * rows), F32)]
         + [(((ni - 1) * rows, 1), F32)] * 2
-        + [((nt - 1, rows), F32)] * 2,
+        + [((nt - 1, rows), F32)] * 2
+        + [(((ni - 1) * rows, wide), BF16), (((nt - 1) * rows, wide), BF16)],
         images[:-1] + texts[:-1],
-        scratch=[pltpu.VMEM(((ni - 1) * rows, wide), BF16), pltpu.VMEM(((nt - 1) * rows, wide), BF16)],
         flops=2 * (ni - 1) * (nt - 1) * rows * rows * wide,
     )
     last_col, last_row, row_lse, col_lse = call(
         functools.partial(last_scores_kernel, ni, nt),
         [(((ni - 1) * rows, rows), F32), ((rows, nt * rows), F32), ((ni, rows), F32), ((nt, rows), F32)],
-        images + texts + halfway,
-        scratch=[pltpu.VMEM(((ni - 1) * rows, wide), BF16), pltpu.VMEM((nt * rows, wide), BF16)],
+        [images[-1], texts[-1], *halfway],
         flops=2 * (ni + nt) * rows * rows * wide,
     )
     row_parts = gather(row_lse, img_bits, n)

time: 45.1 us -> 53.5 us (1.19)
  waiting for transfers between devices: 8.85 us -> 17.5 us
    ppermute x15, waiting for transfers between devices: 8.85 us -> 17.5 us  [swap(): return lax.ppermute(x, 'dp', [(i, i ^ offset) for i in range(n)])]
  transfers between devices with their start and end apart: 15 -> 15, of which waited for: 7 -> 8; matrix products, arithmetic and copies ran while one was open for 0% -> 0% of each run, Pallas kernels for 29% -> 24%
where the time goes in v9:
time: 53.5 us; the launch traced here: 53.3 us
  starting transfers between devices  18.9 us (35%)
  waiting for transfers between devices  17.5 us (33%)
  Pallas kernels  16 us (30%)
  between operations  0.83 us (2%)
    ppermute x15, starting transfers between devices, swap(): return lax.ppermute(x, 'dp', [(i, i ^ offset) for i in range(n)])  18.9 us
    ppermute x15, waiting for transfers between devices, swap(): return lax.ppermute(x, 'dp', [(i, i ^ offset) for i in range(n)])  17.5 us
    pallas_call x11, Pallas kernels, call(): pl.pallas_call(kernel, out_shape=[jax.ShapeDtypeStruct(s, d) for s, d in...  8.51 us
    pallas_call x2, Pallas kernels, stream_embed(): pl.pallas_call(functools.partial(stream_kernel, blocks, cuts), out_shape=...  5.32 us
    pallas_call x2, Pallas kernels, sketch(): pl.pallas_call(functools.partial(sketch_kernel, len(parts), turned), out_...  2.22 us
  transfers between devices with their start and end apart: 15, of which 8 were waited for; matrix products, arithmetic and copies ran while one was open for 0% of the time, Pallas kernels for 24%

profile of v9, /device:TPU:0, one launch (start us, length us, event | category | flops | bytes accessed | tf_op | source)
XLA Modules:
  0.0 53.3 jit_solution(13770307904944418948)
XLA Ops:
  0.6 0.0 copy-start.1
  0.6 3.1 %collective-permute-start.1 = (bf16[128,1280]{1,0:T(8,128)(2,1)}, bf16[128,1280]{1,0:T(8,128)(2,1)S(1)}, u32[]{:S(2)}, u32[]{:S(2)}) collective-permute-start(bf16[128,1280]{1,0:T(8,128)(2,1)} %refs_1_.5), channel_id=1, source_target_pairs={{0,4},{1,5},{2,6},{3,7},{4,0},{5,1},{6,2},{7,3},{8,12},{9,13},{10,... | collective-permute-start | bytes 983048 | tf_op jit(solution)/shard_map/ppermute | solution.py:61
  3.7 2.8 %shard_map.95 = (bf16[128,1280]{1,0:T(8,128)(2,1)S(1)}, f32[128,1]{1,0:T(8,128)S(1)}) custom-call(bf16[128,1664]{1,0:T(8,128)(2,1)} %refs_0_.5, bf16[1664,1280]{1,0:T(8,128)(2,1)} %refs_1_.3), custom_call_target="tpu_custom_call" | custom-call | flops 545259520 | bytes 4259840 | tf_op jit(solution)/shard_map/pallas_call | solution.py:124
  6.6 0.0 copy-start
  6.6 0.0 copy-start.2
  6.6 0.0 copy-start.5
  6.6 0.0 copy-start.6
  6.6 2.7 %collective-permute-start = (bf16[128,1280]{1,0:T(8,128)(2,1)S(1)}, bf16[128,1280]{1,0:T(8,128)(2,1)S(1)}, u32[]{:S(2)}, u32[]{:S(2)}) collective-permute-start(bf16[128,1280]{1,0:T(8,128)(2,1)S(1)} %get-tuple-element.34.refs_0_), channel_id=1, source_target_pairs={{0,8},{1,9},{2,10},{3,11},{4,12},{5,13},{6,14},{7,15},{8,0},{9,1},... | collective-permute-start | bytes 983048 | tf_op jit(solution)/shard_map/ppermute | solution.py:61
  9.3 0.0 collective-permute-start.4
  9.3 0.0 copy-done.1
  9.3 1.5 %collective-permute-start.5 = (bf16[128,1280]{1,0:T(8,128)(2,1)S(1)}, bf16[128,1280]{1,0:T(8,128)(2,1)S(1)}, u32[]{:S(2)}, u32[]{:S(2)}) collective-permute-start(bf16[128,1280]{1,0:T(8,128)(2,1)S(1)} %copy-done.1), channel_id=1, source_target_pairs={{0,2},{1,3},{2,0},{3,1},{4,6},{5,7},{6,4},{7,5},{8,10},{9,11},{10,... | collective-permute-start | bytes 983048 | tf_op jit(solution)/shard_map/ppermute | solution.py:61
  10.8 2.5 %shard_map.96 = (bf16[128,1280]{1,0:T(8,128)(2,1)S(1)}, f32[128,1]{1,0:T(8,128)S(1)}, bf16[1280,1280]{1,0:T(8,128)(2,1)S(1)}) custom-call(bf16[128,1280]{1,0:T(8,128)(2,1)} %refs_1_.5, bf16[1280,1280]{1,0:T(8,128)(2,1)} %refs_1_.4), custom_call_target="tpu_custom_call" | custom-call | flops 419430400 | bytes 3276800 | tf_op jit(solution)/shard_map/pallas_call | solution.py:124
  13.3 2.5 %collective-permute-done.1.refs_0_ = bf16[128,1280]{1,0:T(8,128)(2,1)S(1)} collective-permute-done((bf16[128,1280]{1,0:T(8,128)(2,1)}, bf16[128,1280]{1,0:T(8,128)(2,1)S(1)}, u32[]{:S(2)}, u32[]{:S(2)}) %collective-permute-start.1) | collective-permute-done | bytes 327712 | tf_op jit(solution)/shard_map/ppermute | solution.py:61
  15.8 0.7 %shard_map.97.refs_6_.refs_4_.refs_5_ = bf16[128,1280]{1,0:T(8,128)(2,1)S(1)} custom-call(bf16[128,1280]{1,0:T(8,128)(2,1)S(1)} %collective-permute-done.1.refs_0_, bf16[1280,1280]{1,0:T(8,128)(2,1)S(1)} %get-tuple-element.38.refs_1_), custom_call_target="tpu_custom_call" | custom-call | flops 419430400 | bytes 3604480 | tf_op jit(solution)/shard_map/pallas_call | solution.py:35
  16.5 0.0 copy-done
  16.5 0.0 copy-done.2
  16.5 0.0 copy-done.5
  16.6 0.0 copy-done.6
  16.6 2.1 %shard_map.98 = (f32[128,4096]{1,0:T(8,128)S(1)}, f32[128,4096]{1,0:T(8,128)S(1)}) custom-call(bf16[128,1664]{1,0:T(8,128)(2,1)S(1)} %copy-done, bf16[128,1280]{1,0:T(8,128)(2,1)S(1)} %copy-done.2, bf16[32,1664]{1,0:T(8,128)(2,1)S(1)} %bitcast.2, bf16[32,1280]{1,0:T(8,128)(2,1)S(1)} %bitcast.3, f32[128,1]{1,0:T(8,128)S(1)} %get-tuple-element.36.refs_4_, ...), custom_call_target="tpu_custom_call" | custom-call | bytes 943104 | tf_op jit(solution)/shard_map/pallas_call | solution.py:35
  18.7 5.2 %collective-permute-done.refs_0_ = bf16[128,1280]{1,0:T(8,128)(2,1)S(1)} collective-permute-done((bf16[128,1280]{1,0:T(8,128)(2,1)S(1)}, bf16[128,1280]{1,0:T(8,128)(2,1)S(1)}, u32[]{:S(2)}, u32[]{:S(2)}) %collective-permute-start) | collective-permute-done | bytes 327712 | tf_op jit(solution)/shard_map/ppermute | solution.py:61
  23.8 0.0 collective-permute-start.2
  23.8 1.5 %collective-permute-start.3 = (bf16[128,1280]{1,0:T(8,128)(2,1)S(1)}, bf16[128,1280]{1,0:T(8,128)(2,1)S(1)}, u32[]{:S(2)}, u32[]{:S(2)}) collective-permute-start(bf16[128,1280]{1,0:T(8,128)(2,1)S(1)} %shard_map.97.refs_6_.refs_4_.refs_5_), channel_id=1, source_target_pairs={{0,2},{1,3},{2,0},{3,1},{4,6},{5,7},{6,4},{7,5},{8,10},{9,11},{10,... | collective-permute-start | bytes 983048 | tf_op jit(solution)/shard_map/ppermute | solution.py:61
  25.3 0.0 collective-permute-done.5.refs_0_
  25.4 0.7 %shard_map.100.refs_5_.refs_6_ = bf16[128,1280]{1,0:T(8,128)(2,1)S(1)} custom-call(bf16[128,1280]{1,0:T(8,128)(2,1)S(1)} %collective-permute-done.5.refs_0_, bf16[1280,1280]{1,0:T(8,128)(2,1)S(1)} %get-tuple-element.38.refs_1_), custom_call_target="tpu_custom_call" | custom-call | flops 419430400 | bytes 3604480 | tf_op jit(solution)/shard_map/pallas_call | solution.py:35
  26.1 0.0 copy-start.3
  26.1 0.0 copy-start.4
  26.1 0.0 collective-permute-done.4.refs_2_
  26.1 1.0 %shard_map.101 = (f32[384,384]{1,0:T(8,128)S(1)}, f32[384,1]{1,0:T(8,128)S(1)}, f32[384,1]{1,0:T(8,128)S(1)}, f32[3,128]{1,0:T(4,128)S(1)}, f32[3,128]{1,0:T(4,1...) custom-call(bf16[128,1280]{1,0:T(8,128)(2,1)S(1)} %get-tuple-element.34.refs_0_, ...), custom_call_target="tpu_custom_call" | custom-call | flops 377487360 | bytes 1966080 | tf_op jit(solution)/shard_map/pallas_call | solution.py:35
  27.1 0.0 collective-permute-done.2.refs_0_.refs_3_
  27.1 6.9 %collective-permute-done.3.refs_1_.refs_7_ = bf16[128,1280]{1,0:T(8,128)(2,1)S(1)} collective-permute-done((bf16[128,1280]{1,0:T(8,128)(2,1)S(1)}, bf16[128,1280]{1,0:T(8,128)(2,1)S(1)}, u32[]{:S(2)}, u32[]{:S(2)}) %collective-permute-start.3) | collective-permute-done | bytes 327712 | tf_op jit(solution)/shard_map/ppermute | solution.py:61
  34.0 1.3 %shard_map.102 = (f32[384,128]{1,0:T(8,128)S(1)}, f32[128,512]{1,0:T(8,128)S(1)}, f32[4,128]{1,0:T(4,128)S(1)}, f32[4,128]{1,0:T(4,128)S(1)}) custom-call(bf16[128,1280]{1,0:T(8,128)(2,1)S(1)} %collective-permute-done.2.refs_0_.refs_3_, bf16[128,1280]{1,0:T(8,128)(2,1)S(1)} %collective-permute-done.3.refs_1_.refs_7_, ...), custom_call_target="tpu_custom_call" | custom-call | flops 335544320 | bytes 2627584 | tf_op jit(solution)/shard_map/pallas_call | solution.py:35
  35.3 0.0 collective-permute-start.9
  35.3 3.0 %collective-permute-start.6 = (f32[4,128]{1,0:T(4,128)S(1)}, f32[4,128]{1,0:T(4,128)S(1)}, u32[]{:S(2)}, u32[]{:S(2)}) collective-permute-start(f32[4,128]{1,0:T(4,128)S(1)} %get-tuple-element.46.refs_0_), channel_id=1, source_target_pairs={{0,8},{1,9},{2,10},{3,11},{4,12},{5,13},{6,14},{7,15},{8,0},{9,1},... | collective-permute-start | bytes 6152 | tf_op jit(solution)/shard_map/ppermute | solution.py:61
  38.3 0.0 collective-permute-start.7
  38.3 0.5 %collective-permute-done.9.refs_1_ = f32[4,128]{1,0:T(4,128)S(1)} collective-permute-done((f32[4,128]{1,0:T(4,128)S(1)}, f32[4,128]{1,0:T(4,128)S(1)}, u32[]{:S(2)}, u32[]{:S(2)}) %collective-permute-start.9) | collective-permute-done | bytes 2080 | tf_op jit(solution)/shard_map/ppermute | solution.py:61
  38.9 1.6 %collective-permute-start.10 = (f32[4,128]{1,0:T(4,128)S(1)}, f32[4,128]{1,0:T(4,128)S(1)}, u32[]{:S(2)}, u32[]{:S(2)}) collective-permute-start(f32[4,128]{1,0:T(4,128)S(1)} %shard_map.103.refs_4_), channel_id=1, source_target_pairs={{0,2},{1,3},{2,0},{3,1},{4,6},{5,7},{6,4},{7,5},{8,10},{9,11},{10,... | collective-permute-start | bytes 6152 | tf_op jit(solution)/shard_map/ppermute | solution.py:61
  40.5 0.0 collective-permute-done.6.refs_1_
  40.5 0.0 collective-permute-start.8
  40.5 0.0 copy-done.3
  40.5 0.0 copy-done.4
  40.5 1.7 %shard_map.104 = (f32[512,128]{1,0:T(8,128)S(1)}, bf16[128,512]{1,0:T(8,128)(2,1)S(1)}, bf16[512,128]{1,0:T(8,128)(2,1)S(1)}, f32[128,512]{1,0:T(8,128)S(1)}, f3...) custom-call(bf16[128,1280]{1,0:T(8,128)(2,1)S(1)} %get-tuple-element.34.refs_0_, bf16[128,1280]{1,0:T(8,128)(2,1)S(1)} %shard_map.99.refs_1_, ...), custom_call_target="tpu_custom_call" | custom-call | flops 671088640 | bytes 3276800 | tf_op jit(solution)/shard_map/pallas_call | solution.py:35
  42.1 0.0 collective-permute-done.7.refs_2_
  42.2 0.4 collective-permute-done.10.refs_5_
  42.5 0.0 collective-permute-done.8.refs_3_
  42.5 0.7 %shard_map.105 = (f32[128,128]{1,0:T(8,128)S(1)}, f32[128,128]{1,0:T(8,128)S(1)}, bf16[256,128]{1,0:T(8,128)(2,1)S(1)}, bf16[512,512]{1,0:T(8,128)(2,1)S(1)}, f32[4,128]{1,0:T(4,128)S(1)}) custom-call(f32[4,128]{1,0:T(4,128)S(1)} %get-tuple-element.46.refs_0_, f32[4,128]{1,0:T(4,128)S(1)} %collective-permute-done.6.refs_1_, ...), custom_call_target="tpu_custom_call" | custom-call | flops 67108864 | bytes 1454080 | tf_op jit(solution)/shard_map/pallas_call | solution.py:35
  43.3 0.2 collective-permute-start.11
  43.5 0.3 shard_map.108
  43.8 1.5 %collective-permute-start.13 = (bf16[256,128]{1,0:T(8,128)(2,1)S(1)}, bf16[256,128]{1,0:T(8,128)(2,1)S(1)}, u32[]{:S(2)}, u32[]{:S(2)}) collective-permute-start(bf16[256,128]{1,0:T(8,128)(2,1)S(1)} %get-tuple-element.62), channel_id=1, source_target_pairs={{0,2},{1,3},{2,0},{3,1},{4,6},{5,7},{6,4},{7,5},{8,10},{9,11},{10,... | collective-permute-start | bytes 196616 | tf_op jit(solution)/shard_map/ppermute | solution.py:61
  45.2 0.0 collective-permute-done.11.refs_1_
  45.2 2.5 %collective-permute-start.12 = (bf16[128,128]{1,0:T(8,128)(2,1)S(1)}, bf16[128,128]{1,0:T(8,128)(2,1)S(1)}, u32[]{:S(2)}, u32[]{:S(2)}) collective-permute-start(bf16[128,128]{1,0:T(8,128)(2,1)S(1)} %shard_map.106), channel_id=1, source_target_pairs={{0,8},{1,9},{2,10},{3,11},{4,12},{5,13},{6,14},{7,15},{8,0},{9,1},... | collective-permute-start | bytes 98312 | tf_op jit(solution)/shard_map/ppermute | solution.py:61
  47.8 0.4 collective-permute-done.13.refs_1_
  48.2 1.3 %collective-permute-start.14 = (bf16[128,128]{1,0:T(8,128)(2,1)S(1)}, bf16[128,128]{1,0:T(8,128)(2,1)S(1)}, u32[]{:S(2)}, u32[]{:S(2)}) collective-permute-start(bf16[128,128]{1,0:T(8,128)(2,1)S(1)} %shard_map.109), channel_id=1, source_target_pairs={{0,4},{1,5},{2,6},{3,7},{4,0},{5,1},{6,2},{7,3},{8,12},{9,13},{10,... | collective-permute-start | bytes 98312 | tf_op jit(solution)/shard_map/ppermute | solution.py:61
  49.5 0.6 %collective-permute-done.12.refs_2_ = bf16[128,128]{1,0:T(8,128)(2,1)S(1)} collective-permute-done((bf16[128,128]{1,0:T(8,128)(2,1)S(1)}, bf16[128,128]{1,0:T(8,128)(2,1)S(1)}, u32[]{:S(2)}, u32[]{:S(2)}) %collective-permute-start.12) | collective-permute-done | bytes 32800 | tf_op jit(solution)/shard_map/ppermute | solution.py:61
  50.1 1.1 %shard_map.107 = bf16[128,4096]{1,0:T(8,128)(2,1)} custom-call(f32[128,128]{1,0:T(8,128)S(1)} %get-tuple-element.53.refs_0_, bf16[256,128]{1,0:T(8,128)(2,1)S(1)} %collective-permute-done.11.refs_1_, bf16[128,128]{1,0:T(8,128)(2,1)S(1)} %collective-permute-done.12.refs_2_, f32[128,128]{1,0:T(8,128)S(1)} %get-tuple-element.56.refs_3_, ...), custom_call_target="tpu_custom_call" | custom-call | flops 524288 | bytes 3145728 | tf_op jit(solution)/shard_map/pallas_call | solution.py:353
  51.2 1.0 %collective-permute-done.14.refs_2_ = bf16[128,128]{1,0:T(8,128)(2,1)S(1)} collective-permute-done((bf16[128,128]{1,0:T(8,128)(2,1)S(1)}, bf16[128,128]{1,0:T(8,128)(2,1)S(1)}, u32[]{:S(2)}, u32[]{:S(2)}) %collective-permute-start.14) | collective-permute-done | bytes 32800 | tf_op jit(solution)/shard_map/ppermute | solution.py:61
  52.2 1.1 %shard_map.110 = bf16[128,4096]{1,0:T(8,128)(2,1)} custom-call(f32[128,128]{1,0:T(8,128)S(1)} %get-tuple-element.61.refs_0_, bf16[256,128]{1,0:T(8,128)(2,1)S(1)} %collective-permute-done.13.refs_1_, bf16[128,128]{1,0:T(8,128)(2,1)S(1)} %collective-permute-done.14.refs_2_, f32[128,128]{1,0:T(8,128)S(1)} %get-tuple-element.64.refs_3_, ...), custom_call_target="tpu_custom_call" | custom-call | flops 524288 | bytes 3145728 | tf_op jit(solution)/shard_map/pallas_call | solution.py:353
  (4 shorter events, 0.0 us)
Async XLA Ops:
  0.6 8.7 %copy-start.1 = (bf16[128,1280]{1,0:T(8,128)(2,1)S(1)}, bf16[128,1280]{1,0:T(8,128)(2,1)}, u32[]{:S(2)}) copy-start(bf16[128,1280]{1,0:T(8,128)(2,1)} %refs_1_.5) | copy-start | bytes 983044
  0.6 15.2 %collective-permute-start.1 = (bf16[128,1280]{1,0:T(8,128)(2,1)}, bf16[128,1280]{1,0:T(8,128)(2,1)S(1)}, u32[]{:S(2)}, u32[]{:S(2)}) collective-permute-start(bf16[128,1280]{1,0:T(8,128)(2,1)} %refs_1_.5), channel_id=1, source_target_pairs={{0,4},{1,5},{2,6},{3,7},{4,0},{5,1},{6,2},{7,3},{8,12},{9,13},{10,... | collective-permute-start | bytes 983048 | tf_op jit(solution)/shard_map/ppermute | solution.py:61
  6.6 10.0 %copy-start = (bf16[128,1664]{1,0:T(8,128)(2,1)S(1)}, bf16[128,1664]{1,0:T(8,128)(2,1)}, u32[]{:S(2)}) copy-start(bf16[128,1664]{1,0:T(8,128)(2,1)} %refs_0_.5) | copy-start | bytes 1277956
  6.6 10.0 %copy-start.2 = (bf16[128,1280]{1,0:T(8,128)(2,1)S(1)}, bf16[128,1280]{1,0:T(8,128)(2,1)}, u32[]{:S(2)}) copy-start(bf16[128,1280]{1,0:T(8,128)(2,1)} %refs_1_.5) | copy-start | bytes 983044
  6.6 10.0 %copy-start.5 = (bf16[1664,32]{0,1:T(8,128)(2,1)S(1)}, bf16[1664,32]{0,1:T(8,128)(2,1)}, u32[]{:S(2)}) copy-start(bf16[1664,32]{0,1:T(8,128)(2,1)} %param.12) | copy-start | bytes 319492
  6.6 9.9 %copy-start.6 = (bf16[1280,32]{0,1:T(8,128)(2,1)S(1)}, bf16[1280,32]{0,1:T(8,128)(2,1)}, u32[]{:S(2)}) copy-start(bf16[1280,32]{0,1:T(8,128)(2,1)} %param.14) | copy-start | bytes 245764
  6.6 17.2 %collective-permute-start = (bf16[128,1280]{1,0:T(8,128)(2,1)S(1)}, bf16[128,1280]{1,0:T(8,128)(2,1)S(1)}, u32[]{:S(2)}, u32[]{:S(2)}) collective-permute-start(bf16[128,1280]{1,0:T(8,128)(2,1)S(1)} %get-tuple-element.34.refs_0_), channel_id=1, source_target_pairs={{0,8},{1,9},{2,10},{3,11},{4,12},{5,13},{6,14},{7,15},{8,0},{9,1},... | collective-permute-start | bytes 983048 | tf_op jit(solution)/shard_map/ppermute | solution.py:61
  9.3 16.8 %collective-permute-start.4 = (bf16[128,1280]{1,0:T(8,128)(2,1)S(1)}, bf16[128,1280]{1,0:T(8,128)(2,1)S(1)}, u32[]{:S(2)}, u32[]{:S(2)}) collective-permute-start(bf16[128,1280]{1,0:T(8,128)(2,1)S(1)} %get-tuple-element.34.refs_0_), channel_id=1, source_target_pairs={{0,1},{1,0},{2,3},{3,2},{4,5},{5,4},{6,7},{7,6},{8,9},{9,8},{10,11... | collective-permute-start | bytes 983048 | tf_op jit(solution)/shard_map/ppermute | solution.py:61
  9.3 16.1 %collective-permute-start.5 = (bf16[128,1280]{1,0:T(8,128)(2,1)S(1)}, bf16[128,1280]{1,0:T(8,128)(2,1)S(1)}, u32[]{:S(2)}, u32[]{:S(2)}) collective-permute-start(bf16[128,1280]{1,0:T(8,128)(2,1)S(1)} %copy-done.1), channel_id=1, source_target_pairs={{0,2},{1,3},{2,0},{3,1},{4,6},{5,7},{6,4},{7,5},{8,10},{9,11},{10,... | collective-permute-start | bytes 983048 | tf_op jit(solution)/shard_map/ppermute | solution.py:61
  23.8 3.3 %collective-permute-start.2 = (bf16[128,1280]{1,0:T(8,128)(2,1)S(1)}, bf16[128,1280]{1,0:T(8,128)(2,1)S(1)}, u32[]{:S(2)}, u32[]{:S(2)}) collective-permute-start(bf16[128,1280]{1,0:T(8,128)(2,1)S(1)} %shard_map.99.refs_1_), channel_id=1, source_target_pairs={{0,1},{1,0},{2,3},{3,2},{4,5},{5,4},{6,7},{7,6},{8,9},{9,8},{10,11... | collective-permute-start | bytes 983048 | tf_op jit(solution)/shard_map/ppermute | solution.py:61
  23.8 10.1 %collective-permute-start.3 = (bf16[128,1280]{1,0:T(8,128)(2,1)S(1)}, bf16[128,1280]{1,0:T(8,128)(2,1)S(1)}, u32[]{:S(2)}, u32[]{:S(2)}) collective-permute-start(bf16[128,1280]{1,0:T(8,128)(2,1)S(1)} %shard_map.97.refs_6_.refs_4_.refs_5_), channel_id=1, source_target_pairs={{0,2},{1,3},{2,0},{3,1},{4,6},{5,7},{6,4},{7,5},{8,10},{9,11},{10,... | collective-permute-start | bytes 983048 | tf_op jit(solution)/shard_map/ppermute | solution.py:61
  26.1 14.4 %copy-start.3 = (bf16[1280,128]{1,0:T(8,128)(2,1)S(1)}, bf16[1280,128]{1,0:T(8,128)(2,1)}, u32[]{:S(2)}) copy-start(bf16[1280,128]{1,0:T(8,128)(2,1)} %refs_8_.1) | copy-start | bytes 983044
  26.1 14.4 %copy-start.4 = (bf16[1280,128]{1,0:T(8,128)(2,1)S(1)}, bf16[1280,128]{1,0:T(8,128)(2,1)}, u32[]{:S(2)}) copy-start(bf16[1280,128]{1,0:T(8,128)(2,1)} %refs_9_.1) | copy-start | bytes 983044
  35.3 3.6 %collective-permute-start.9 = (f32[4,128]{1,0:T(4,128)S(1)}, f32[4,128]{1,0:T(4,128)S(1)}, u32[]{:S(2)}, u32[]{:S(2)}) collective-permute-start(f32[4,128]{1,0:T(4,128)S(1)} %get-tuple-element.47.refs_0_), channel_id=1, source_target_pairs={{0,4},{1,5},{2,6},{3,7},{4,0},{5,1},{6,2},{7,3},{8,12},{9,13},{10,... | collective-permute-start | bytes 6152 | tf_op jit(solution)/shard_map/ppermute | solution.py:61
  35.3 5.2 %collective-permute-start.6 = (f32[4,128]{1,0:T(4,128)S(1)}, f32[4,128]{1,0:T(4,128)S(1)}, u32[]{:S(2)}, u32[]{:S(2)}) collective-permute-start(f32[4,128]{1,0:T(4,128)S(1)} %get-tuple-element.46.refs_0_), channel_id=1, source_target_pairs={{0,8},{1,9},{2,10},{3,11},{4,12},{5,13},{6,14},{7,15},{8,0},{9,1},... | collective-permute-start | bytes 6152 | tf_op jit(solution)/shard_map/ppermute | solution.py:61
  38.3 3.8 %collective-permute-start.7 = (f32[4,128]{1,0:T(4,128)S(1)}, f32[4,128]{1,0:T(4,128)S(1)}, u32[]{:S(2)}, u32[]{:S(2)}) collective-permute-start(f32[4,128]{1,0:T(4,128)S(1)} %get-tuple-element.46.refs_0_), channel_id=1, source_target_pairs={{0,1},{1,0},{2,3},{3,2},{4,5},{5,4},{6,7},{7,6},{8,9},{9,8},{10,11... | collective-permute-start | bytes 6152 | tf_op jit(solution)/shard_map/ppermute | solution.py:61
  38.9 3.7 %collective-permute-start.10 = (f32[4,128]{1,0:T(4,128)S(1)}, f32[4,128]{1,0:T(4,128)S(1)}, u32[]{:S(2)}, u32[]{:S(2)}) collective-permute-start(f32[4,128]{1,0:T(4,128)S(1)} %shard_map.103.refs_4_), channel_id=1, source_target_pairs={{0,2},{1,3},{2,0},{3,1},{4,6},{5,7},{6,4},{7,5},{8,10},{9,11},{10,... | collective-permute-start | bytes 6152 | tf_op jit(solution)/shard_map/ppermute | solution.py:61
  40.5 2.1 %collective-permute-start.8 = (f32[4,128]{1,0:T(4,128)S(1)}, f32[4,128]{1,0:T(4,128)S(1)}, u32[]{:S(2)}, u32[]{:S(2)}) collective-permute-start(f32[4,128]{1,0:T(4,128)S(1)} %collective-permute-done.6.refs_1_), channel_id=1, source_target_pairs={{0,1},{1,0},{2,3},{3,2},{4,5},{5,4},{6,7},{7,6},{8,9},{9,8},{10,11... | collective-permute-start | bytes 6152 | tf_op jit(solution)/shard_map/ppermute | solution.py:61
  43.3 2.0 %collective-permute-start.11 = (bf16[256,128]{1,0:T(8,128)(2,1)S(1)}, bf16[256,128]{1,0:T(8,128)(2,1)S(1)}, u32[]{:S(2)}, u32[]{:S(2)}) collective-permute-start(bf16[256,128]{1,0:T(8,128)(2,1)S(1)} %get-tuple-element.54), channel_id=1, source_target_pairs={{0,1},{1,0},{2,3},{3,2},{4,5},{5,4},{6,7},{7,6},{8,9},{9,8},{10,11... | collective-permute-start | bytes 196616 | tf_op jit(solution)/shard_map/ppermute | solution.py:61
  43.8 4.4 %collective-permute-start.13 = (bf16[256,128]{1,0:T(8,128)(2,1)S(1)}, bf16[256,128]{1,0:T(8,128)(2,1)S(1)}, u32[]{:S(2)}, u32[]{:S(2)}) collective-permute-start(bf16[256,128]{1,0:T(8,128)(2,1)S(1)} %get-tuple-element.62), channel_id=1, source_target_pairs={{0,2},{1,3},{2,0},{3,1},{4,6},{5,7},{6,4},{7,5},{8,10},{9,11},{10,... | collective-permute-start | bytes 196616 | tf_op jit(solution)/shard_map/ppermute | solution.py:61
  45.2 4.9 %collective-permute-start.12 = (bf16[128,128]{1,0:T(8,128)(2,1)S(1)}, bf16[128,128]{1,0:T(8,128)(2,1)S(1)}, u32[]{:S(2)}, u32[]{:S(2)}) collective-permute-start(bf16[128,128]{1,0:T(8,128)(2,1)S(1)} %shard_map.106), channel_id=1, source_target_pairs={{0,8},{1,9},{2,10},{3,11},{4,12},{5,13},{6,14},{7,15},{8,0},{9,1},... | collective-permute-start | bytes 98312 | tf_op jit(solution)/shard_map/ppermute | solution.py:61
  48.2 4.0 %collective-permute-start.14 = (bf16[128,128]{1,0:T(8,128)(2,1)S(1)}, bf16[128,128]{1,0:T(8,128)(2,1)S(1)}, u32[]{:S(2)}, u32[]{:S(2)}) collective-permute-start(bf16[128,128]{1,0:T(8,128)(2,1)S(1)} %shard_map.109), channel_id=1, source_target_pairs={{0,4},{1,5},{2,6},{3,7},{4,0},{5,1},{6,2},{7,3},{8,12},{9,13},{10,... | collective-permute-start | bytes 98312 | tf_op jit(solution)/shard_map/ppermute | solution.py:61

commit v10 on v8

--- a/solution.py
+++ b/solution.py
@@ -338,8 +338,8 @@
     rows = base.shape[0]
     grad = sum((part[:rows].astype(F32) for part in parts[1:]), parts[0][...])
     grad = (grad.T if turned else grad) + base[...]
-    copies, step = [], rows // 2
-    for k in range(2):
+    copies, step = [], rows // 4
+    for k in range(4):
         here = slice(k * step, (k + 1) * step)
         for a in range(0, made.shape[1], LANES):
             made[here, a : a + LANES] = (keys[here, a : a + LANES] * grad[here]).astype(BF16)
@@ -356,7 +356,7 @@
         out_shape=jax.ShapeDtypeStruct(keys.shape, BF16),
         in_specs=[pl.BlockSpec(memory_space=pltpu.VMEM)] * len(args),
         out_specs=pl.BlockSpec(memory_space=pltpu.HBM),
-        scratch_shapes=[pltpu.VMEM(keys.shape, BF16), pltpu.SemaphoreType.DMA((2,))],
+        scratch_shapes=[pltpu.VMEM(keys.shape, BF16), pltpu.SemaphoreType.DMA((4,))],
         compiler_params=pltpu.CompilerParams(vmem_limit_bytes=16 << 20),
         cost_estimate=pl.CostEstimate(flops=keys.size, bytes_accessed=6 * keys.size, transcendentals=0),
     )(*args)

time: 45.1 us -> 45.1 us (level)
  no operation moved by 1% of the time
where the time goes in v10:
time: 45.1 us; the launch traced here: 44.9 us
  starting transfers between devices  19.2 us (43%)
  Pallas kernels  16 us (35%)
  waiting for transfers between devices  8.89 us (20%)
  between operations  0.8 us (2%)
    ppermute x15, starting transfers between devices, swap(): return lax.ppermute(x, 'dp', [(i, i ^ offset) for i in range(n)])  19.2 us
    ppermute x15, waiting for transfers between devices, swap(): return lax.ppermute(x, 'dp', [(i, i ^ offset) for i in range(n)])  8.89 us
    pallas_call x11, Pallas kernels, call(): pl.pallas_call(kernel, out_shape=[jax.ShapeDtypeStruct(s, d) for s, d in...  8.52 us
    pallas_call x2, Pallas kernels, stream_embed(): pl.pallas_call(functools.partial(stream_kernel, blocks, cuts), out_shape=...  5.32 us
    pallas_call x2, Pallas kernels, sketch(): pl.pallas_call(functools.partial(sketch_kernel, len(parts), turned), out_...  2.16 us
  transfers between devices with their start and end apart: 15, of which 7 were waited for; matrix products, arithmetic and copies ran while one was open for 0% of the time, Pallas kernels for 29%

profile of v10, /device:TPU:0, one launch (start us, length us, event | category | flops | bytes accessed | tf_op | source)
XLA Modules:
  0.0 44.9 jit_solution(16756196850236982001)
XLA Ops:
  0.6 0.0 copy-start.1
  0.6 3.1 %collective-permute-start.1 = (bf16[128,1280]{1,0:T(8,128)(2,1)}, bf16[128,1280]{1,0:T(8,128)(2,1)S(1)}, u32[]{:S(2)}, u32[]{:S(2)}) collective-permute-start(bf16[128,1280]{1,0:T(8,128)(2,1)} %refs_1_.5), channel_id=1, source_target_pairs={{0,4},{1,5},{2,6},{3,7},{4,0},{5,1},{6,2},{7,3},{8,12},{9,13},{10,... | collective-permute-start | bytes 983048 | tf_op jit(solution)/shard_map/ppermute | solution.py:61
  3.7 2.8 %shard_map.95 = (bf16[128,1280]{1,0:T(8,128)(2,1)S(1)}, f32[128,1]{1,0:T(8,128)S(1)}) custom-call(bf16[128,1664]{1,0:T(8,128)(2,1)} %refs_0_.5, bf16[1664,1280]{1,0:T(8,128)(2,1)} %refs_1_.3), custom_call_target="tpu_custom_call" | custom-call | flops 545259520 | bytes 4259840 | tf_op jit(solution)/shard_map/pallas_call | solution.py:124
  6.6 0.0 copy-start
  6.6 0.0 copy-start.2
  6.6 0.0 copy-start.5
  6.6 0.0 copy-start.6
  6.6 2.7 %collective-permute-start = (bf16[128,1280]{1,0:T(8,128)(2,1)S(1)}, bf16[128,1280]{1,0:T(8,128)(2,1)S(1)}, u32[]{:S(2)}, u32[]{:S(2)}) collective-permute-start(bf16[128,1280]{1,0:T(8,128)(2,1)S(1)} %get-tuple-element.32.refs_0_), channel_id=1, source_target_pairs={{0,8},{1,9},{2,10},{3,11},{4,12},{5,13},{6,14},{7,15},{8,0},{9,1},... | collective-permute-start | bytes 983048 | tf_op jit(solution)/shard_map/ppermute | solution.py:61
  9.3 0.0 copy-done.1
  9.3 1.5 %collective-permute-start.4 = (bf16[128,1280]{1,0:T(8,128)(2,1)S(1)}, bf16[128,1280]{1,0:T(8,128)(2,1)S(1)}, u32[]{:S(2)}, u32[]{:S(2)}) collective-permute-start(bf16[128,1280]{1,0:T(8,128)(2,1)S(1)} %copy-done.1), channel_id=1, source_target_pairs={{0,2},{1,3},{2,0},{3,1},{4,6},{5,7},{6,4},{7,5},{8,10},{9,11},{10,... | collective-permute-start | bytes 983048 | tf_op jit(solution)/shard_map/ppermute | solution.py:61
  10.8 0.0 collective-permute-start.2
  10.8 2.5 %shard_map.96 = (bf16[128,1280]{1,0:T(8,128)(2,1)S(1)}, f32[128,1]{1,0:T(8,128)S(1)}, bf16[1280,1280]{1,0:T(8,128)(2,1)S(1)}) custom-call(bf16[128,1280]{1,0:T(8,128)(2,1)} %refs_1_.5, bf16[1280,1280]{1,0:T(8,128)(2,1)} %refs_1_.4), custom_call_target="tpu_custom_call" | custom-call | flops 419430400 | bytes 3276800 | tf_op jit(solution)/shard_map/pallas_call | solution.py:124
  13.3 2.5 %collective-permute-done.1.refs_0_ = bf16[128,1280]{1,0:T(8,128)(2,1)S(1)} collective-permute-done((bf16[128,1280]{1,0:T(8,128)(2,1)}, bf16[128,1280]{1,0:T(8,128)(2,1)S(1)}, u32[]{:S(2)}, u32[]{:S(2)}) %collective-permute-start.1) | collective-permute-done | bytes 327712 | tf_op jit(solution)/shard_map/ppermute | solution.py:61
  15.8 0.7 %shard_map.97.refs_6_.refs_4_.refs_5_ = bf16[128,1280]{1,0:T(8,128)(2,1)S(1)} custom-call(bf16[128,1280]{1,0:T(8,128)(2,1)S(1)} %collective-permute-done.1.refs_0_, bf16[1280,1280]{1,0:T(8,128)(2,1)S(1)} %get-tuple-element.36.refs_1_), custom_call_target="tpu_custom_call" | custom-call | flops 419430400 | bytes 3604480 | tf_op jit(solution)/shard_map/pallas_call | solution.py:35
  16.5 1.8 %collective-permute-start.5 = (bf16[128,1280]{1,0:T(8,128)(2,1)S(1)}, bf16[128,1280]{1,0:T(8,128)(2,1)S(1)}, u32[]{:S(2)}, u32[]{:S(2)}) collective-permute-start(bf16[128,1280]{1,0:T(8,128)(2,1)S(1)} %shard_map.97.refs_6_.refs_4_.refs_5_), channel_id=1, source_target_pairs={{0,2},{1,3},{2,0},{3,1},{4,6},{5,7},{6,4},{7,5},{8,10},{9,11},{10,... | collective-permute-start | bytes 983048 | tf_op jit(solution)/shard_map/ppermute | solution.py:61
  18.3 0.0 copy-done
  18.3 0.0 copy-done.2
  18.3 0.0 copy-done.5
  18.3 0.0 copy-done.6
  18.3 2.1 %shard_map.98 = (f32[128,4096]{1,0:T(8,128)S(1)}, f32[128,4096]{1,0:T(8,128)S(1)}) custom-call(bf16[128,1664]{1,0:T(8,128)(2,1)S(1)} %copy-done, bf16[128,1280]{1,0:T(8,128)(2,1)S(1)} %copy-done.2, bf16[32,1664]{1,0:T(8,128)(2,1)S(1)} %bitcast.2, bf16[32,1280]{1,0:T(8,128)(2,1)S(1)} %bitcast.3, f32[128,1]{1,0:T(8,128)S(1)} %get-tuple-element.34.refs_4_, ...), custom_call_target="tpu_custom_call" | custom-call | bytes 943104 | tf_op jit(solution)/shard_map/pallas_call | solution.py:35
  20.4 3.4 %collective-permute-done.refs_0_ = bf16[128,1280]{1,0:T(8,128)(2,1)S(1)} collective-permute-done((bf16[128,1280]{1,0:T(8,128)(2,1)S(1)}, bf16[128,1280]{1,0:T(8,128)(2,1)S(1)}, u32[]{:S(2)}, u32[]{:S(2)}) %collective-permute-start) | collective-permute-done | bytes 327712 | tf_op jit(solution)/shard_map/ppermute | solution.py:61
  23.8 0.0 collective-permute-start.3
  23.8 0.0 collective-permute-done.4.refs_0_
  23.8 0.7 %shard_map.100.refs_5_.refs_6_ = bf16[128,1280]{1,0:T(8,128)(2,1)S(1)} custom-call(bf16[128,1280]{1,0:T(8,128)(2,1)S(1)} %collective-permute-done.4.refs_0_, bf16[1280,1280]{1,0:T(8,128)(2,1)S(1)} %get-tuple-element.36.refs_1_), custom_call_target="tpu_custom_call" | custom-call | flops 419430400 | bytes 3604480 | tf_op jit(solution)/shard_map/pallas_call | solution.py:35
  24.6 0.0 copy-start.3
  24.6 0.0 copy-start.4
  24.6 0.0 collective-permute-done.2.refs_2_
  24.6 1.0 %shard_map.101 = (f32[384,384]{1,0:T(8,128)S(1)}, f32[384,1]{1,0:T(8,128)S(1)}, f32[384,1]{1,0:T(8,128)S(1)}, f32[3,128]{1,0:T(4,128)S(1)}, f32[3,128]{1,0:T(4,128)S(1)}) custom-call(bf16[128,1280]{1,0:T(8,128)(2,1)S(1)} %get-tuple-element.32.refs_0_, bf16[128,1280]{1,0:T(8,128)(2,1)S(1)} %shard_map.99.refs_1_, ...), custom_call_target="tpu_custom_call" | custom-call | flops 377487360 | bytes 1966080 | tf_op jit(solution)/shard_map/pallas_call | solution.py:35
  25.6 0.0 collective-permute-done.5.refs_7_
  25.6 0.0 collective-permute-done.3.refs_3_
  25.6 1.3 %shard_map.102 = (f32[384,128]{1,0:T(8,128)S(1)}, f32[128,512]{1,0:T(8,128)S(1)}, f32[4,128]{1,0:T(4,128)S(1)}, f32[4,128]{1,0:T(4,128)S(1)}) custom-call(bf16[128,1280]{1,0:T(8,128)(2,1)S(1)} %get-tuple-element.32.refs_0_, bf16[128,1280]{1,0:T(8,128)(2,1)S(1)} %shard_map.99.refs_1_, bf16[128,1280]{1,0:T(8,128)(2,1)S(1)} %collective-permute-done.2.refs_2_, ...), custom_call_target="tpu_custom_call" | custom-call | flops 335544320 | bytes 2627584 | tf_op jit(solution)/shard_map/pallas_call | solution.py:35
  26.9 0.1 collective-permute-start.9
  27.0 3.0 %collective-permute-start.6 = (f32[4,128]{1,0:T(4,128)S(1)}, f32[4,128]{1,0:T(4,128)S(1)}, u32[]{:S(2)}, u32[]{:S(2)}) collective-permute-start(f32[4,128]{1,0:T(4,128)S(1)} %get-tuple-element.42.refs_0_), channel_id=1, source_target_pairs={{0,8},{1,9},{2,10},{3,11},{4,12},{5,13},{6,14},{7,15},{8,0},{9,1},... | collective-permute-start | bytes 6152 | tf_op jit(solution)/shard_map/ppermute | solution.py:61
  30.0 0.0 collective-permute-start.7
  30.0 0.5 %collective-permute-done.9.refs_1_ = f32[4,128]{1,0:T(4,128)S(1)} collective-permute-done((f32[4,128]{1,0:T(4,128)S(1)}, f32[4,128]{1,0:T(4,128)S(1)}, u32[]{:S(2)}, u32[]{:S(2)}) %collective-permute-start.9) | collective-permute-done | bytes 2080 | tf_op jit(solution)/shard_map/ppermute | solution.py:61
  30.5 1.6 %collective-permute-start.10 = (f32[4,128]{1,0:T(4,128)S(1)}, f32[4,128]{1,0:T(4,128)S(1)}, u32[]{:S(2)}, u32[]{:S(2)}) collective-permute-start(f32[4,128]{1,0:T(4,128)S(1)} %shard_map.103.refs_4_), channel_id=1, source_target_pairs={{0,2},{1,3},{2,0},{3,1},{4,6},{5,7},{6,4},{7,5},{8,10},{9,11},{10,... | collective-permute-start | bytes 6152 | tf_op jit(solution)/shard_map/ppermute | solution.py:61
  32.1 0.0 collective-permute-done.6.refs_1_
  32.1 0.0 collective-permute-start.8
  32.1 0.0 copy-done.3
  32.1 0.0 copy-done.4
  32.1 1.7 %shard_map.104 = (f32[512,128]{1,0:T(8,128)S(1)}, bf16[128,512]{1,0:T(8,128)(2,1)S(1)}, bf16[512,128]{1,0:T(8,128)(2,1)S(1)}, f32[128,512]{1,0:T(8,128)S(1)}, f3...) custom-call(bf16[128,1280]{1,0:T(8,128)(2,1)S(1)} %get-tuple-element.32.refs_0_, bf16[128,1280]{1,0:T(8,128)(2,1)S(1)} %shard_map.99.refs_1_, ...), custom_call_target="tpu_custom_call" | custom-call | flops 671088640 | bytes 3276800 | tf_op jit(solution)/shard_map/pallas_call | solution.py:35
  33.8 0.0 collective-permute-done.7.refs_2_
  33.8 0.4 collective-permute-done.10.refs_5_
  34.2 0.0 collective-permute-done.8.refs_3_
  34.2 0.7 %shard_map.105 = (f32[128,128]{1,0:T(8,128)S(1)}, f32[128,128]{1,0:T(8,128)S(1)}, bf16[256,128]{1,0:T(8,128)(2,1)S(1)}, bf16[512,512]{1,0:T(8,128)(2,1)S(1)}, f32[4,128]{1,0:T(4,128)S(1)}) custom-call(f32[4,128]{1,0:T(4,128)S(1)} %get-tuple-element.42.refs_0_, f32[4,128]{1,0:T(4,128)S(1)} %collective-permute-done.6.refs_1_, ...), custom_call_target="tpu_custom_call" | custom-call | flops 67108864 | bytes 1454080 | tf_op jit(solution)/shard_map/pallas_call | solution.py:35
  34.9 0.2 collective-permute-start.11
  35.1 0.3 shard_map.108
  35.4 1.4 %collective-permute-start.13 = (bf16[256,128]{1,0:T(8,128)(2,1)S(1)}, bf16[256,128]{1,0:T(8,128)(2,1)S(1)}, u32[]{:S(2)}, u32[]{:S(2)}) collective-permute-start(bf16[256,128]{1,0:T(8,128)(2,1)S(1)} %get-tuple-element.58), channel_id=1, source_target_pairs={{0,2},{1,3},{2,0},{3,1},{4,6},{5,7},{6,4},{7,5},{8,10},{9,11},{10,... | collective-permute-start | bytes 196616 | tf_op jit(solution)/shard_map/ppermute | solution.py:61
  36.9 0.0 collective-permute-done.11.refs_1_
  36.9 2.5 %collective-permute-start.12 = (bf16[128,128]{1,0:T(8,128)(2,1)S(1)}, bf16[128,128]{1,0:T(8,128)(2,1)S(1)}, u32[]{:S(2)}, u32[]{:S(2)}) collective-permute-start(bf16[128,128]{1,0:T(8,128)(2,1)S(1)} %shard_map.106), channel_id=1, source_target_pairs={{0,8},{1,9},{2,10},{3,11},{4,12},{5,13},{6,14},{7,15},{8,0},{9,1},... | collective-permute-start | bytes 98312 | tf_op jit(solution)/shard_map/ppermute | solution.py:61
  39.4 0.4 collective-permute-done.13.refs_1_
  39.8 1.3 %collective-permute-start.14 = (bf16[128,128]{1,0:T(8,128)(2,1)S(1)}, bf16[128,128]{1,0:T(8,128)(2,1)S(1)}, u32[]{:S(2)}, u32[]{:S(2)}) collective-permute-start(bf16[128,128]{1,0:T(8,128)(2,1)S(1)} %shard_map.109), channel_id=1, source_target_pairs={{0,4},{1,5},{2,6},{3,7},{4,0},{5,1},{6,2},{7,3},{8,12},{9,13},{10,... | collective-permute-start | bytes 98312 | tf_op jit(solution)/shard_map/ppermute | solution.py:61
  41.2 0.6 %collective-permute-done.12.refs_2_ = bf16[128,128]{1,0:T(8,128)(2,1)S(1)} collective-permute-done((bf16[128,128]{1,0:T(8,128)(2,1)S(1)}, bf16[128,128]{1,0:T(8,128)(2,1)S(1)}, u32[]{:S(2)}, u32[]{:S(2)}) %collective-permute-start.12) | collective-permute-done | bytes 32800 | tf_op jit(solution)/shard_map/ppermute | solution.py:61
  41.8 1.0 %shard_map.107 = bf16[128,4096]{1,0:T(8,128)(2,1)} custom-call(f32[128,128]{1,0:T(8,128)S(1)} %get-tuple-element.49.refs_0_, bf16[256,128]{1,0:T(8,128)(2,1)S(1)} %collective-permute-done.11.refs_1_, bf16[128,128]{1,0:T(8,128)(2,1)S(1)} %collective-permute-done.12.refs_2_, f32[128,128]{1,0:T(8,128)S(1)} %get-tuple-element.52.refs_3_, ...), custom_call_target="tpu_custom_call" | custom-call | flops 524288 | bytes 3145728 | tf_op jit(solution)/shard_map/pallas_call | solution.py:354
  42.8 1.0 %collective-permute-done.14.refs_2_ = bf16[128,128]{1,0:T(8,128)(2,1)S(1)} collective-permute-done((bf16[128,128]{1,0:T(8,128)(2,1)S(1)}, bf16[128,128]{1,0:T(8,128)(2,1)S(1)}, u32[]{:S(2)}, u32[]{:S(2)}) %collective-permute-start.14) | collective-permute-done | bytes 32800 | tf_op jit(solution)/shard_map/ppermute | solution.py:61
  43.8 1.1 %shard_map.110 = bf16[128,4096]{1,0:T(8,128)(2,1)} custom-call(f32[128,128]{1,0:T(8,128)S(1)} %get-tuple-element.57.refs_0_, bf16[256,128]{1,0:T(8,128)(2,1)S(1)} %collective-permute-done.13.refs_1_, bf16[128,128]{1,0:T(8,128)(2,1)S(1)} %collective-permute-done.14.refs_2_, f32[128,128]{1,0:T(8,128)S(1)} %get-tuple-element.60.refs_3_, ...), custom_call_target="tpu_custom_call" | custom-call | flops 524288 | bytes 3145728 | tf_op jit(solution)/shard_map/pallas_call | solution.py:354
  (4 shorter events, 0.0 us)
Async XLA Ops:
  0.6 8.6 %copy-start.1 = (bf16[128,1280]{1,0:T(8,128)(2,1)S(1)}, bf16[128,1280]{1,0:T(8,128)(2,1)}, u32[]{:S(2)}) copy-start(bf16[128,1280]{1,0:T(8,128)(2,1)} %refs_1_.5) | copy-start | bytes 983044
  0.6 15.2 %collective-permute-start.1 = (bf16[128,1280]{1,0:T(8,128)(2,1)}, bf16[128,1280]{1,0:T(8,128)(2,1)S(1)}, u32[]{:S(2)}, u32[]{:S(2)}) collective-permute-start(bf16[128,1280]{1,0:T(8,128)(2,1)} %refs_1_.5), channel_id=1, source_target_pairs={{0,4},{1,5},{2,6},{3,7},{4,0},{5,1},{6,2},{7,3},{8,12},{9,13},{10,... | collective-permute-start | bytes 983048 | tf_op jit(solution)/shard_map/ppermute | solution.py:61
  6.6 11.7 %copy-start = (bf16[128,1664]{1,0:T(8,128)(2,1)S(1)}, bf16[128,1664]{1,0:T(8,128)(2,1)}, u32[]{:S(2)}) copy-start(bf16[128,1664]{1,0:T(8,128)(2,1)} %refs_0_.5) | copy-start | bytes 1277956
  6.6 11.7 %copy-start.2 = (bf16[128,1280]{1,0:T(8,128)(2,1)S(1)}, bf16[128,1280]{1,0:T(8,128)(2,1)}, u32[]{:S(2)}) copy-start(bf16[128,1280]{1,0:T(8,128)(2,1)} %refs_1_.5) | copy-start | bytes 983044
  6.6 11.7 %copy-start.5 = (bf16[1664,32]{0,1:T(8,128)(2,1)S(1)}, bf16[1664,32]{0,1:T(8,128)(2,1)}, u32[]{:S(2)}) copy-start(bf16[1664,32]{0,1:T(8,128)(2,1)} %param.12) | copy-start | bytes 319492
  6.6 11.7 %copy-start.6 = (bf16[1280,32]{0,1:T(8,128)(2,1)S(1)}, bf16[1280,32]{0,1:T(8,128)(2,1)}, u32[]{:S(2)}) copy-start(bf16[1280,32]{0,1:T(8,128)(2,1)} %param.14) | copy-start | bytes 245764
  6.6 17.2 %collective-permute-start = (bf16[128,1280]{1,0:T(8,128)(2,1)S(1)}, bf16[128,1280]{1,0:T(8,128)(2,1)S(1)}, u32[]{:S(2)}, u32[]{:S(2)}) collective-permute-start(bf16[128,1280]{1,0:T(8,128)(2,1)S(1)} %get-tuple-element.32.refs_0_), channel_id=1, source_target_pairs={{0,8},{1,9},{2,10},{3,11},{4,12},{5,13},{6,14},{7,15},{8,0},{9,1},... | collective-permute-start | bytes 983048 | tf_op jit(solution)/shard_map/ppermute | solution.py:61
  9.3 14.6 %collective-permute-start.4 = (bf16[128,1280]{1,0:T(8,128)(2,1)S(1)}, bf16[128,1280]{1,0:T(8,128)(2,1)S(1)}, u32[]{:S(2)}, u32[]{:S(2)}) collective-permute-start(bf16[128,1280]{1,0:T(8,128)(2,1)S(1)} %copy-done.1), channel_id=1, source_target_pairs={{0,2},{1,3},{2,0},{3,1},{4,6},{5,7},{6,4},{7,5},{8,10},{9,11},{10,... | collective-permute-start | bytes 983048 | tf_op jit(solution)/shard_map/ppermute | solution.py:61
  10.8 13.8 %collective-permute-start.2 = (bf16[128,1280]{1,0:T(8,128)(2,1)S(1)}, bf16[128,1280]{1,0:T(8,128)(2,1)S(1)}, u32[]{:S(2)}, u32[]{:S(2)}) collective-permute-start(bf16[128,1280]{1,0:T(8,128)(2,1)S(1)} %get-tuple-element.32.refs_0_), channel_id=1, source_target_pairs={{0,1},{1,0},{2,3},{3,2},{4,5},{5,4},{6,7},{7,6},{8,9},{9,8},{10,11... | collective-permute-start | bytes 983048 | tf_op jit(solution)/shard_map/ppermute | solution.py:61
  16.5 9.1 %collective-permute-start.5 = (bf16[128,1280]{1,0:T(8,128)(2,1)S(1)}, bf16[128,1280]{1,0:T(8,128)(2,1)S(1)}, u32[]{:S(2)}, u32[]{:S(2)}) collective-permute-start(bf16[128,1280]{1,0:T(8,128)(2,1)S(1)} %shard_map.97.refs_6_.refs_4_.refs_5_), channel_id=1, source_target_pairs={{0,2},{1,3},{2,0},{3,1},{4,6},{5,7},{6,4},{7,5},{8,10},{9,11},{10,... | collective-permute-start | bytes 983048 | tf_op jit(solution)/shard_map/ppermute | solution.py:61
  23.8 1.8 %collective-permute-start.3 = (bf16[128,1280]{1,0:T(8,128)(2,1)S(1)}, bf16[128,1280]{1,0:T(8,128)(2,1)S(1)}, u32[]{:S(2)}, u32[]{:S(2)}) collective-permute-start(bf16[128,1280]{1,0:T(8,128)(2,1)S(1)} %shard_map.99.refs_1_), channel_id=1, source_target_pairs={{0,1},{1,0},{2,3},{3,2},{4,5},{5,4},{6,7},{7,6},{8,9},{9,8},{10,11... | collective-permute-start | bytes 983048 | tf_op jit(solution)/shard_map/ppermute | solution.py:61
  24.6 7.6 %copy-start.3 = (bf16[1280,128]{1,0:T(8,128)(2,1)S(1)}, bf16[1280,128]{1,0:T(8,128)(2,1)}, u32[]{:S(2)}) copy-start(bf16[1280,128]{1,0:T(8,128)(2,1)} %refs_8_.1) | copy-start | bytes 983044
  24.6 7.6 %copy-start.4 = (bf16[1280,128]{1,0:T(8,128)(2,1)S(1)}, bf16[1280,128]{1,0:T(8,128)(2,1)}, u32[]{:S(2)}) copy-start(bf16[1280,128]{1,0:T(8,128)(2,1)} %refs_9_.1) | copy-start | bytes 983044
  26.9 3.6 %collective-permute-start.9 = (f32[4,128]{1,0:T(4,128)S(1)}, f32[4,128]{1,0:T(4,128)S(1)}, u32[]{:S(2)}, u32[]{:S(2)}) collective-permute-start(f32[4,128]{1,0:T(4,128)S(1)} %get-tuple-element.43.refs_0_), channel_id=1, source_target_pairs={{0,4},{1,5},{2,6},{3,7},{4,0},{5,1},{6,2},{7,3},{8,12},{9,13},{10,... | collective-permute-start | bytes 6152 | tf_op jit(solution)/shard_map/ppermute | solution.py:61
  27.0 5.1 %collective-permute-start.6 = (f32[4,128]{1,0:T(4,128)S(1)}, f32[4,128]{1,0:T(4,128)S(1)}, u32[]{:S(2)}, u32[]{:S(2)}) collective-permute-start(f32[4,128]{1,0:T(4,128)S(1)} %get-tuple-element.42.refs_0_), channel_id=1, source_target_pairs={{0,8},{1,9},{2,10},{3,11},{4,12},{5,13},{6,14},{7,15},{8,0},{9,1},... | collective-permute-start | bytes 6152 | tf_op jit(solution)/shard_map/ppermute | solution.py:61
  30.0 3.9 %collective-permute-start.7 = (f32[4,128]{1,0:T(4,128)S(1)}, f32[4,128]{1,0:T(4,128)S(1)}, u32[]{:S(2)}, u32[]{:S(2)}) collective-permute-start(f32[4,128]{1,0:T(4,128)S(1)} %get-tuple-element.42.refs_0_), channel_id=1, source_target_pairs={{0,1},{1,0},{2,3},{3,2},{4,5},{5,4},{6,7},{7,6},{8,9},{9,8},{10,11... | collective-permute-start | bytes 6152 | tf_op jit(solution)/shard_map/ppermute | solution.py:61
  30.5 3.7 %collective-permute-start.10 = (f32[4,128]{1,0:T(4,128)S(1)}, f32[4,128]{1,0:T(4,128)S(1)}, u32[]{:S(2)}, u32[]{:S(2)}) collective-permute-start(f32[4,128]{1,0:T(4,128)S(1)} %shard_map.103.refs_4_), channel_id=1, source_target_pairs={{0,2},{1,3},{2,0},{3,1},{4,6},{5,7},{6,4},{7,5},{8,10},{9,11},{10,... | collective-permute-start | bytes 6152 | tf_op jit(solution)/shard_map/ppermute | solution.py:61
  32.1 2.1 %collective-permute-start.8 = (f32[4,128]{1,0:T(4,128)S(1)}, f32[4,128]{1,0:T(4,128)S(1)}, u32[]{:S(2)}, u32[]{:S(2)}) collective-permute-start(f32[4,128]{1,0:T(4,128)S(1)} %collective-permute-done.6.refs_1_), channel_id=1, source_target_pairs={{0,1},{1,0},{2,3},{3,2},{4,5},{5,4},{6,7},{7,6},{8,9},{9,8},{10,11... | collective-permute-start | bytes 6152 | tf_op jit(solution)/shard_map/ppermute | solution.py:61
  34.9 2.0 %collective-permute-start.11 = (bf16[256,128]{1,0:T(8,128)(2,1)S(1)}, bf16[256,128]{1,0:T(8,128)(2,1)S(1)}, u32[]{:S(2)}, u32[]{:S(2)}) collective-permute-start(bf16[256,128]{1,0:T(8,128)(2,1)S(1)} %get-tuple-element.50), channel_id=1, source_target_pairs={{0,1},{1,0},{2,3},{3,2},{4,5},{5,4},{6,7},{7,6},{8,9},{9,8},{10,11... | collective-permute-start | bytes 196616 | tf_op jit(solution)/shard_map/ppermute | solution.py:61
  35.4 4.4 %collective-permute-start.13 = (bf16[256,128]{1,0:T(8,128)(2,1)S(1)}, bf16[256,128]{1,0:T(8,128)(2,1)S(1)}, u32[]{:S(2)}, u32[]{:S(2)}) collective-permute-start(bf16[256,128]{1,0:T(8,128)(2,1)S(1)} %get-tuple-element.58), channel_id=1, source_target_pairs={{0,2},{1,3},{2,0},{3,1},{4,6},{5,7},{6,4},{7,5},{8,10},{9,11},{10,... | collective-permute-start | bytes 196616 | tf_op jit(solution)/shard_map/ppermute | solution.py:61
  36.9 4.9 %collective-permute-start.12 = (bf16[128,128]{1,0:T(8,128)(2,1)S(1)}, bf16[128,128]{1,0:T(8,128)(2,1)S(1)}, u32[]{:S(2)}, u32[]{:S(2)}) collective-permute-start(bf16[128,128]{1,0:T(8,128)(2,1)S(1)} %shard_map.106), channel_id=1, source_target_pairs={{0,8},{1,9},{2,10},{3,11},{4,12},{5,13},{6,14},{7,15},{8,0},{9,1},... | collective-permute-start | bytes 98312 | tf_op jit(solution)/shard_map/ppermute | solution.py:61
  39.8 4.0 %collective-permute-start.14 = (bf16[128,128]{1,0:T(8,128)(2,1)S(1)}, bf16[128,128]{1,0:T(8,128)(2,1)S(1)}, u32[]{:S(2)}, u32[]{:S(2)}) collective-permute-start(bf16[128,128]{1,0:T(8,128)(2,1)S(1)} %shard_map.109), channel_id=1, source_target_pairs={{0,4},{1,5},{2,6},{3,7},{4,0},{5,1},{6,2},{7,3},{8,12},{9,13},{10,... | collective-permute-start | bytes 98312 | tf_op jit(solution)/shard_map/ppermute | solution.py:61
